TPU v7x, 32 devices: a whole 2x2x4 slice. The times are simulated.
32 devices in a mesh: fsdp: 16 (over z, y, core), tp: 2 (over x).
Axes of the slice: x: 2, y: 2, z: 4, core: 2. Of those that a mesh axis runs over, the one named last changes fastest.
Arguments:
- tokens: bfloat16 [8192, 1280], P(('fsdp', 'tp')), may hold values from -6 to 6
- seg_starts: int32 [16, 8], P('fsdp'), may hold values from 0 to 511, as said below
- gain_attn: float32 [1280], replicated, may hold values from 0.5 to 1.5
- gain_mlp: float32 [1280], replicated, may hold values from 0.5 to 1.5
- query_scale: float32 [80], replicated, may hold values from -0.5 to 1
- w_query: bfloat16 [1280, 1280], P('fsdp', 'tp'), may hold values from -0.15625 to 0.15625
- w_key: bfloat16 [1280, 1280], P('fsdp', 'tp'), may hold values from -0.15625 to 0.15625
- w_value: bfloat16 [1280, 1280], P('fsdp', 'tp'), may hold values from -0.15625 to 0.15625
- w_out: bfloat16 [1280, 1280], P('tp', 'fsdp'), may hold values from -1.25 to 1.25
- w_up: bfloat16 [1280, 1280], P('fsdp', 'tp'), may hold values from -0.15625 to 0.15625
- w_down: bfloat16 [1280, 1280], P('tp', 'fsdp'), may hold values from -0.15625 to 0.15625
- cotangent: bfloat16 [8192, 1280], P(('fsdp', 'tp')), may hold values from -6 to 6
Outputs:
- result: bfloat16 [8192, 1280], P(('fsdp', 'tp'))
- grad_tokens: float32 [8192, 1280], P(('fsdp', 'tp'))
- grad_gain_attn: float32 [1280], replicated
- grad_gain_mlp: float32 [1280], replicated
- grad_query_scale: float32 [80], replicated
- grad_w_query: float32 [1280, 1280], P('fsdp', 'tp')
- grad_w_key: float32 [1280, 1280], P('fsdp', 'tp')
- grad_w_value: float32 [1280, 1280], P('fsdp', 'tp')
- grad_w_out: float32 [1280, 1280], P('tp', 'fsdp')
- grad_w_up: float32 [1280, 1280], P('fsdp', 'tp')
- grad_w_down: float32 [1280, 1280], P('tp', 'fsdp')
Inputs may be any that keep to these rules, and one draw needn't show every extreme that they name: `seg_starts`: in each row the starts rise strictly and the first is 0; a series runs from its start to the next start, the last to the row's end. In the first row the last series has one position.
All inputs are finite; a program needn't handle non-finite values.
Results may differ from a plain program's by a relative error of at most 0.012.
Values may be sent and summed in bfloat16 or wider, within the bound.
No kernel may reach another device: no remote copies, remote signals or barrier semaphores. Data moves between devices by JAX's collectives and lax.ppermute only.
A program may use at most 128 MiB of HBM per device.

v0:
```python
import math

import jax
import jax.numpy as jnp
from jax import lax
from jax.sharding import PartitionSpec as P

HD = 80


epsilon = 1e-06
softplus_unit = 1.442695041


def inverse_rms(values):
    return lax.rsqrt(jnp.mean(values * values, axis=-1, keepdims=True) + epsilon)


def norm_backward(resid, inv_scale, gain, dnormed):
    weighted = dnormed * gain
    cubed = inv_scale * inv_scale * inv_scale
    dresid = inv_scale * weighted - resid * cubed * jnp.mean(
        weighted * resid, axis=-1, keepdims=True
    )
    dgain = jnp.sum(dnormed * resid * inv_scale, axis=0)
    return (dresid, dgain)


def segment_ids(starts, length):
    positions = jnp.arange(length, dtype=jnp.int32)
    inside = (starts[None, :] <= positions[:, None]).astype(jnp.int32)
    return (positions, jnp.sum(inside, axis=1) - 1)


def block_scores(query_blk, block_pos, block_series, key_b, positions, series):
    scores = jnp.einsum("qhd,khd->hqk", query_blk, key_b, preferred_element_type=jnp.float32)
    allowed = (positions[None, :] <= block_pos[:, None]) & (
        series[None, :] == block_series[:, None]
    )
    return jnp.where(allowed[None], scores, -1e30)


def attend_forward(query_b, key_b, value_b, positions, series, block_rows):
    num_blocks = query_b.shape[0] // block_rows
    local_heads = query_b.shape[1]

    def one_block(inputs):
        query_blk, block_pos, block_series = inputs
        scores = block_scores(query_blk, block_pos, block_series, key_b, positions, series)
        row_max = jnp.max(scores, axis=-1, keepdims=True)
        exponent = jnp.exp(scores - row_max)
        total = jnp.sum(exponent, axis=-1, keepdims=True)
        soft_b = (exponent / total).astype(jnp.bfloat16)
        mixed = jnp.einsum("hqk,khd->qhd", soft_b, value_b, preferred_element_type=jnp.float32)
        return (mixed, row_max + jnp.log(total))

    mixed, logsum = lax.map(
        one_block,
        (
            query_b.reshape(num_blocks, block_rows, local_heads, HD),
            positions.reshape(num_blocks, block_rows),
            series.reshape(num_blocks, block_rows),
        ),
    )
    return (mixed.reshape(query_b.shape[0], local_heads * HD), logsum)


def attend_backward(query_b, key_b, value_b, dmixed, logsum, positions, series, block_rows):
    num_blocks = query_b.shape[0] // block_rows
    local_heads = query_b.shape[1]

    def one_block(carry, inputs):
        dkey, dvalue = carry
        query_blk, dmixed_blk, block_pos, block_series, logsum_blk = inputs
        scores = block_scores(query_blk, block_pos, block_series, key_b, positions, series)
        soft = jnp.exp(scores - logsum_blk)
        dsoft = jnp.einsum("qhd,khd->hqk", dmixed_blk, value_b, preferred_element_type=jnp.float32)
        inner = jnp.sum(soft * dsoft, axis=-1, keepdims=True)
        dscores = (soft * (dsoft - inner)).astype(jnp.bfloat16)
        dquery_blk = jnp.einsum("hqk,khd->qhd", dscores, key_b, preferred_element_type=jnp.float32)
        dkey = dkey + jnp.einsum(
            "hqk,qhd->khd", dscores, query_blk, preferred_element_type=jnp.float32
        )
        dvalue = dvalue + jnp.einsum(
            "hqk,qhd->khd",
            soft.astype(jnp.bfloat16),
            dmixed_blk,
            preferred_element_type=jnp.float32,
        )
        return ((dkey, dvalue), dquery_blk)

    zeros = jnp.zeros(key_b.shape, jnp.float32)
    inputs = (
        query_b.reshape(num_blocks, block_rows, local_heads, HD),
        dmixed.reshape(num_blocks, block_rows, local_heads, HD),
        positions.reshape(num_blocks, block_rows),
        series.reshape(num_blocks, block_rows),
        logsum,
    )
    (dkey, dvalue), dquery = lax.scan(one_block, (zeros, zeros), inputs)
    return (dquery.reshape(query_b.shape), dkey, dvalue)


def on_device(
    tokens,
    seg_starts,
    gain_attn,
    gain_mlp,
    query_scale,
    w_query,
    w_key,
    w_value,
    w_out,
    w_up,
    w_down,
    cotangent,
):
    gathered = (
        lax.all_gather(w_query, "fsdp", axis=0, tiled=True),
        lax.all_gather(w_key, "fsdp", axis=0, tiled=True),
        lax.all_gather(w_value, "fsdp", axis=0, tiled=True),
        lax.all_gather(w_out, "fsdp", axis=1, tiled=True),
        lax.all_gather(w_up, "fsdp", axis=0, tiled=True),
        lax.all_gather(w_down, "fsdp", axis=1, tiled=True),
    )
    full_query, full_key, full_value, full_out, full_up, full_down = gathered
    local_rows = tokens.shape[0]
    row_length = local_rows * lax.axis_size("tp")
    block_rows = min(512, row_length)
    local_heads = full_query.shape[1] // HD
    positions, series = segment_ids(seg_starts[0], row_length)
    resid = tokens.astype(jnp.float32)
    scale_one = inverse_rms(resid)
    normed_one = (resid * scale_one * gain_attn).astype(jnp.bfloat16)
    gathered_one = lax.all_gather(normed_one, "tp", axis=0, tiled=True)
    query = jnp.dot(gathered_one, full_query, preferred_element_type=jnp.float32).reshape(
        row_length, local_heads, HD
    )
    scaling = softplus_unit / math.sqrt(HD) * jax.nn.softplus(query_scale)
    query_b = (query * scaling).astype(jnp.bfloat16)
    key_b = (
        jnp.dot(gathered_one, full_key, preferred_element_type=jnp.float32)
        .astype(jnp.bfloat16)
        .reshape(row_length, local_heads, HD)
    )
    value_b = (
        jnp.dot(gathered_one, full_value, preferred_element_type=jnp.float32)
        .astype(jnp.bfloat16)
        .reshape(row_length, local_heads, HD)
    )
    mixed, logsum = attend_forward(query_b, key_b, value_b, positions, series, block_rows)
    mixed_b = mixed.astype(jnp.bfloat16)
    attn_part = jnp.dot(mixed_b, full_out, preferred_element_type=jnp.float32)
    middle = resid + lax.psum_scatter(attn_part, "tp", scatter_dimension=0, tiled=True)
    scale_two = inverse_rms(middle)
    normed_two = (middle * scale_two * gain_mlp).astype(jnp.bfloat16)
    wide_up, wide_down = (full_up, full_down)
    mlp_input = lax.all_gather(normed_two, "tp", axis=0, tiled=True)
    upward = jnp.dot(mlp_input, wide_up, preferred_element_type=jnp.float32)
    activated, gelu_back = jax.vjp(jax.nn.gelu, upward)
    hidden_b = activated.astype(jnp.bfloat16)
    mlp_part = jnp.dot(hidden_b, wide_down, preferred_element_type=jnp.float32)
    mlp_sum = lax.psum_scatter(
        mlp_part.astype(jnp.bfloat16), "tp", scatter_dimension=0, tiled=True
    ).astype(jnp.float32)
    result = (middle + mlp_sum).astype(jnp.bfloat16)
    dlower = lax.all_gather(cotangent, "tp", axis=0, tiled=True)
    grad_down_here = jnp.einsum("rf,rd->fd", hidden_b, dlower, preferred_element_type=jnp.float32)
    dhidden = jnp.einsum("rd,fd->rf", dlower, wide_down, preferred_element_type=jnp.float32)
    dupward = gelu_back(dhidden)[0].astype(jnp.bfloat16)
    grad_up_here = jnp.einsum("rd,rf->df", mlp_input, dupward, preferred_element_type=jnp.float32)
    dnorm_part = jnp.einsum("rf,df->rd", dupward, wide_up, preferred_element_type=jnp.float32)
    dnormed_two = lax.psum_scatter(dnorm_part, "tp", scatter_dimension=0, tiled=True)
    grad_up_part, grad_down_part = (grad_up_here, grad_down_here)
    dresid_two, dgain_two = norm_backward(middle, scale_two, gain_mlp, dnormed_two)
    dmiddle = cotangent.astype(jnp.float32) + dresid_two
    dattn = lax.all_gather(dmiddle.astype(jnp.bfloat16), "tp", axis=0, tiled=True)
    grad_out_part = jnp.einsum("rh,rd->hd", mixed_b, dattn, preferred_element_type=jnp.float32)
    dmixed = jnp.einsum("rd,hd->rh", dattn, full_out, preferred_element_type=jnp.float32).astype(
        jnp.bfloat16
    )
    dquery_scaled, dkey, dvalue = attend_backward(
        query_b, key_b, value_b, dmixed, logsum, positions, series, block_rows
    )
    dscaling = jnp.sum(dquery_scaled * query, axis=(0, 1))
    dquery = (dquery_scaled * scaling).astype(jnp.bfloat16).reshape(row_length, local_heads * HD)
    dkey_b = dkey.astype(jnp.bfloat16).reshape(row_length, local_heads * HD)
    dvalue_b = dvalue.astype(jnp.bfloat16).reshape(row_length, local_heads * HD)
    grad_query_part = jnp.einsum(
        "rd,rh->dh", gathered_one, dquery, preferred_element_type=jnp.float32
    )
    grad_key_part = jnp.einsum(
        "rd,rh->dh", gathered_one, dkey_b, preferred_element_type=jnp.float32
    )
    grad_value_part = jnp.einsum(
        "rd,rh->dh", gathered_one, dvalue_b, preferred_element_type=jnp.float32
    )
    dnorm_one_part = jnp.einsum("rh,dh->rd", dquery, full_query, preferred_element_type=jnp.float32)
    dnorm_one_part = dnorm_one_part + jnp.einsum(
        "rh,dh->rd", dkey_b, full_key, preferred_element_type=jnp.float32
    )
    dnorm_one_part = dnorm_one_part + jnp.einsum(
        "rh,dh->rd", dvalue_b, full_value, preferred_element_type=jnp.float32
    )
    dnormed_one = lax.psum_scatter(dnorm_one_part, "tp", scatter_dimension=0, tiled=True)
    dresid_one, dgain_one = norm_backward(resid, scale_one, gain_attn, dnormed_one)
    grad_tokens = dmiddle + dresid_one
    summed = (
        lax.psum_scatter(grad_query_part, "fsdp", scatter_dimension=0, tiled=True),
        lax.psum_scatter(grad_key_part, "fsdp", scatter_dimension=0, tiled=True),
        lax.psum_scatter(grad_value_part, "fsdp", scatter_dimension=0, tiled=True),
        lax.psum_scatter(grad_out_part, "fsdp", scatter_dimension=1, tiled=True),
        lax.psum_scatter(grad_up_part, "fsdp", scatter_dimension=0, tiled=True),
        lax.psum_scatter(grad_down_part, "fsdp", scatter_dimension=1, tiled=True),
    )
    dscale_param = dscaling * (softplus_unit / math.sqrt(HD)) * jax.nn.sigmoid(query_scale)
    grad_gain_attn, grad_gain_mlp, grad_query_scale = lax.psum(
        (dgain_one, dgain_two, dscale_param), ("fsdp", "tp")
    )
    return (
        result,
        grad_tokens,
        grad_gain_attn,
        grad_gain_mlp,
        grad_query_scale,
        summed[0],
        summed[1],
        summed[2],
        summed[3],
        summed[4],
        summed[5],
    )


def solution(mesh):
    placed = (
        P(("fsdp", "tp"), None),
        P("fsdp", None),
        P(),
        P(),
        P(),
        P("fsdp", "tp"),
        P("fsdp", "tp"),
        P("fsdp", "tp"),
        P("tp", "fsdp"),
        P("fsdp", "tp"),
        P("tp", "fsdp"),
        P(("fsdp", "tp"), None),
    )
    return jax.shard_map(
        on_device,
        mesh=mesh,
        in_specs=placed,
        out_specs=(
            P(("fsdp", "tp"), None),
            P(("fsdp", "tp"), None),
            P(),
            P(),
            P(),
            P("fsdp", "tp"),
            P("fsdp", "tp"),
            P("fsdp", "tp"),
            P("tp", "fsdp"),
            P("fsdp", "tp"),
            P("tp", "fsdp"),
        ),
        check_vma=False,
    )
```

profile of v0, /device:TPU:0, one launch (start us, length us, event | category | flops | bytes accessed | tf_op | source)
XLA Modules:
  0.0 971.8 jit_solution(16609251986696414168)
XLA Ops:
  7.2 1.3 fusion.19
  9.1 2.1 fusion.21
  11.3 0.7 all-gather.17.cloned.1.call-update
  12.1 0.7 all-gather.13.cloned.1.call-update
  14.8 23.6 %all-gather.11.cloned.1.call-done = bf16[512,1280]{1,0:T(8,128)(2,1)} async-done(((bf16[256,1280]{1,0:T(8,128)(2,1)}), bf16[512,1280]{1,0:T(8,128)(2,1)}) %all-gather.11.cloned.1.call-update) | async-done | bytes 1310736 | tf_op jit(solution)/shard_map/all_gather | solution.py:135
  38.4 42.1 %all-gather.17.cloned.1.call-done = bf16[1280,640]{1,0:T(8,128)(2,1)} async-done(((bf16[80,640]{1,0:T(8,128)(2,1)}), bf16[1280,640]{1,0:T(8,128)(2,1)}) %all-gather.17.cloned.1.call-update) | async-done | bytes 1638416 | tf_op jit(solution)/shard_map/all_gather | solution.py:120
  80.5 3.0 convolution_convert_fusion.3
  83.8 37.7 %all-gather.13.cloned.1.call-done = bf16[1280,640]{1,0:T(8,128)(2,1)} async-done(((bf16[80,640]{1,0:T(8,128)(2,1)}), bf16[1280,640]{1,0:T(8,128)(2,1)}) %all-gather.13.cloned.1.call-update) | async-done | bytes 1638416 | tf_op jit(solution)/shard_map/all_gather | solution.py:121
  121.5 2.6 convolution_convert_fusion.4
  124.4 38.0 %all-gather.15.cloned.1.call-done = bf16[1280,640]{1,0:T(8,128)(2,1)} async-done(((bf16[80,640]{1,0:T(8,128)(2,1)}), bf16[1280,640]{1,0:T(8,128)(2,1)}) %all-gather.15.cloned.1.call-update) | async-done | bytes 1638416 | tf_op jit(solution)/shard_map/all_gather | solution.py:119
  162.4 2.5 fusion.35
  164.9 1.5 select_reduce_fusion
  166.4 1.5 fusion
  167.9 1.8 copy-done
  169.7 2.3 fusion.8
  172.0 31.2 %all-gather.19.cloned.1.call-done = bf16[640,1280]{0,1:T(8,128)(2,1)} async-done(((bf16[640,80]{0,1:T(8,128)(2,1)}), bf16[640,1280]{0,1:T(8,128)(2,1)}) %all-gather.19.cloned.1.call-update) | async-done | bytes 1638416 | tf_op jit(solution)/shard_map/all_gather | solution.py:122
  203.3 4.2 fusion.36
  207.6 0.7 all-gather.27.cloned.1.call-update
  208.4 0.7 all-gather.25.cloned.1.call-update
  209.1 0.7 all-gather.23.cloned.1.call-update
  209.8 34.4 %reduce-scatter.11.cloned.1.call-done = f32[256,1280]{1,0:T(8,128)} async-done(((f32[512,1280]{1,0:T(8,128)}), f32[256,1280]{1,0:T(8,128)}) %reduce-scatter.11.cloned.1.call-update) | async-done | bytes 1310736 | tf_op jit(solution)/shard_map/reduce_scatter | solution.py:154
  244.2 1.6 multiply_reduce_fusion.4
  246.9 1.7 multiply_convert_fusion.3
  248.9 21.2 %all-gather.27.cloned.1.call-done = bf16[512,1280]{1,0:T(8,128)(2,1)} async-done(((bf16[256,1280]{1,0:T(8,128)(2,1)}), bf16[512,1280]{1,0:T(8,128)(2,1)}) %all-gather.27.cloned.1.call-update) | async-done | bytes 1310736 | tf_op jit(solution)/shard_map/all_gather | solution.py:167
  270.1 42.4 %all-gather.25.cloned.1.call-done = bf16[640,1280]{0,1:T(8,128)(2,1)} async-done(((bf16[640,80]{0,1:T(8,128)(2,1)}), bf16[640,1280]{0,1:T(8,128)(2,1)}) %all-gather.25.cloned.1.call-update) | async-done | bytes 1638416 | tf_op jit(solution)/shard_map/all_gather | solution.py:124
  312.5 4.1 fusion.37
  316.5 37.2 %all-gather.23.cloned.1.call-done = bf16[1280,640]{1,0:T(8,128)(2,1)} async-done(((bf16[80,640]{1,0:T(8,128)(2,1)}), bf16[1280,640]{1,0:T(8,128)(2,1)}) %all-gather.23.cloned.1.call-update) | async-done | bytes 1638416 | tf_op jit(solution)/shard_map/all_gather | solution.py:123
  353.7 25.2 %all-gather.21.cloned.1.call-done = bf16[512,1280]{1,0:T(8,128)(2,1)} async-done(((bf16[256,1280]{1,0:T(8,128)(2,1)}), bf16[512,1280]{1,0:T(8,128)(2,1)}) %all-gather.21.cloned.1.call-update) | async-done | bytes 1310736 | tf_op jit(solution)/shard_map/all_gather | solution.py:158
  378.9 5.1 fusion.18
  384.0 0.8 copy-done.15
  384.9 2.7 fusion.38
  387.6 4.3 convolution_convert_fusion
  392.0 33.3 %reduce-scatter.15.cloned.1.call-done = f32[256,1280]{1,0:T(8,128)} async-done(((f32[512,1280]{1,0:T(8,128)}), f32[256,1280]{1,0:T(8,128)}) %reduce-scatter.15.cloned.1.call-update) | async-done | bytes 1310736 | tf_op jit(solution)/shard_map/reduce_scatter | solution.py:173
  425.3 2.3 multiply_reduce_fusion.2
  428.1 22.5 %reduce-scatter.13.cloned.1.call-done = bf16[256,1280]{1,0:T(8,128)(2,1)} async-done(((bf16[512,1280]{1,0:T(8,128)(2,1)}), bf16[256,1280]{1,0:T(8,128)(2,1)}) %reduce-scatter.13.cloned.1.call-update) | async-done | bytes 655376 | tf_op jit(solution)/shard_map/reduce_scatter | solution.py:163
  450.6 3.7 fusion.34
  454.4 1.3 log_add_fusion
  455.7 23.0 %all-gather.29.cloned.1.call-done = bf16[512,1280]{1,0:T(8,128)(2,1)} async-done(((bf16[256,1280]{1,0:T(8,128)(2,1)}), bf16[512,1280]{1,0:T(8,128)(2,1)}) %all-gather.29.cloned.1.call-update) | async-done | bytes 1310736 | tf_op jit(solution)/shard_map/all_gather | solution.py:177
  478.8 3.0 convolution_convert_fusion.2
  482.5 5.4 fusion.9
  488.0 4.9 multiply_reduce_fusion
  493.0 2.6 multiply_convert_fusion
  495.7 0.9 multiply_reduce_fusion.1
  496.6 1.4 convolution_convert_fusion.1
  498.0 1.2 fusion.39
  499.7 1.2 convolution_add_fusion.1
  501.1 2.7 convolution_add_fusion
  503.9 4.4 fusion.44
  508.6 5.1 fusion.33
  513.8 4.5 fusion.43
  518.3 2.9 fusion.42
  521.3 1.0 copy-done.6
  522.3 3.0 fusion.41
  525.4 2.9 fusion.40
  529.0 12.6 %reduce-scatter.17.cloned.1.call-done = f32[256,1280]{1,0:T(8,128)} async-done(((f32[512,1280]{1,0:T(8,128)}), f32[256,1280]{1,0:T(8,128)}) %reduce-scatter.17.cloned.1.call-update) | async-done | bytes 1310736 | tf_op jit(solution)/shard_map/reduce_scatter | solution.py:205
  541.6 1.7 fusion.27
  543.3 39.8 %all-reduce = (f32[1280]{0:T(1024)}, f32[1280]{0:T(1024)}, f32[80]{0:T(128)}) all-reduce(f32[1280]{0:T(1024)S(1)} %get-tuple-element.69, f32[1280]{0:T(1024)S(1)} %copy-done.19, f32[80]{0:T(128)S(1)} %divide_multiply_fusion), channel_id=1, replica_groups=mesh['fsdp'=16,'tp'=2] {'fsdp','tp'}, use_global_device_ids=true, to_apply=%region_13.14 | all-reduce | flops 2640 | bytes 21120 | tf_op jit(solution)/shard_map/psum | solution.py:217
  583.1 2.7 fusion.24
  585.9 27.4 %reduce-scatter.27.cloned.1.call-done = f32[80,640]{1,0:T(8,128)} async-done(((f32[1280,640]{1,0:T(8,128)}), f32[80,640]{1,0:T(8,128)}) %reduce-scatter.27.cloned.1.call-update) | async-done | bytes 204816 | tf_op jit(solution)/shard_map/reduce_scatter | solution.py:213
  613.3 70.5 %reduce-scatter.29.cloned.1.call-done = f32[640,80]{0,1:T(8,128)} async-done(((f32[640,1280]{0,1:T(8,128)}), f32[640,80]{0,1:T(8,128)}) %reduce-scatter.29.cloned.1.call-update) | async-done | bytes 204816 | tf_op jit(solution)/shard_map/reduce_scatter | solution.py:214
  683.7 70.0 %reduce-scatter.25.cloned.1.call-done = f32[640,80]{0,1:T(8,128)} async-done(((f32[640,1280]{0,1:T(8,128)}), f32[640,80]{0,1:T(8,128)}) %reduce-scatter.25.cloned.1.call-update) | async-done | bytes 204816 | tf_op jit(solution)/shard_map/reduce_scatter | solution.py:212
  753.8 70.5 %reduce-scatter.23.cloned.1.call-done = f32[80,640]{1,0:T(8,128)} async-done(((f32[1280,640]{1,0:T(8,128)}), f32[80,640]{1,0:T(8,128)}) %reduce-scatter.23.cloned.1.call-update) | async-done | bytes 204816 | tf_op jit(solution)/shard_map/reduce_scatter | solution.py:211
  824.3 70.2 %reduce-scatter.21.cloned.1.call-done = f32[80,640]{1,0:T(8,128)} async-done(((f32[1280,640]{1,0:T(8,128)}), f32[80,640]{1,0:T(8,128)}) %reduce-scatter.21.cloned.1.call-update) | async-done | bytes 204816 | tf_op jit(solution)/shard_map/reduce_scatter | solution.py:210
  894.5 70.5 %reduce-scatter.19.cloned.1.call-done = f32[80,640]{1,0:T(8,128)} async-done(((f32[1280,640]{1,0:T(8,128)}), f32[80,640]{1,0:T(8,128)}) %reduce-scatter.19.cloned.1.call-update) | async-done | bytes 204816 | tf_op jit(solution)/shard_map/reduce_scatter | solution.py:209
  (111 shorter events, 8.2 us)
Async XLA Ops:
  7.2 31.2 %all-gather.11.cloned.1.call-start = ((), (), s32[]{:S(2)}) async-start(), calls=%async_computation.10 | async-start | bytes 1966080 | tf_op jit(solution)/shard_map/all_gather | solution.py:135
  8.5 5.5 copy-start.29
  8.5 6.0 copy-start.26
  9.1 5.4 copy-start.21
  11.3 69.2 %all-gather.17.cloned.1.call-start = ((), (), s32[]{:S(2)}) async-start(), calls=%async_computation.13 | async-start | bytes 1740800 | tf_op jit(solution)/shard_map/all_gather | solution.py:120
  12.0 109.5 %all-gather.13.cloned.1.call-start = ((), (), s32[]{:S(2)}) async-start(), calls=%async_computation.11 | async-start | bytes 1740800 | tf_op jit(solution)/shard_map/all_gather | solution.py:121
  12.8 149.6 %all-gather.15.cloned.1.call-start = ((), (), s32[]{:S(2)}) async-start(), calls=%async_computation.12 | async-start | bytes 1740800 | tf_op jit(solution)/shard_map/all_gather | solution.py:119
  13.4 189.9 %all-gather.19.cloned.1.call-start = ((), (), s32[]{:S(2)}) async-start(), calls=%async_computation.14 | async-start | bytes 1740800 | tf_op jit(solution)/shard_map/all_gather | solution.py:122
  13.9 230.3 %reduce-scatter.11.cloned.1.call-start = ((), (), s32[]{:S(2)}) async-start(), calls=%async_computation.15 | async-start | bytes 3932160 | tf_op jit(solution)/shard_map/reduce_scatter | solution.py:154
  83.5 38.0 %copy-start.1 = (bf16[512,1280]{1,0:T(8,128)(2,1)S(1)}, bf16[512,1280]{1,0:T(8,128)(2,1)}, u32[]{:S(2)}) copy-start(bf16[512,1280]{1,0:T(8,128)(2,1)} %all-gather.11.cloned.1.call-done) | copy-start | bytes 3932164
  83.8 81.1 %copy-start.7 = (bf16[512,640]{0,1:T(8,128)(2,1)}, bf16[512,640]{0,1:T(8,128)(2,1)S(1)}, u32[]{:S(2)}) copy-start(bf16[512,640]{0,1:T(8,128)(2,1)S(1)} %copy.45) | copy-start | bytes 1966084
  124.4 43.5 %copy-start.10 = (bf16[512,640]{0,1:T(8,128)(2,1)}, bf16[512,640]{0,1:T(8,128)(2,1)S(1)}, u32[]{:S(2)}) copy-start(bf16[512,640]{0,1:T(8,128)(2,1)S(1)} %copy.43) | copy-start | bytes 1966084
  124.4 40.5 %copy-start.23 = (f32[80]{0:T(128)S(1)}, f32[80]{0:T(128)}, u32[]{:S(2)}) copy-start(f32[80]{0:T(128)} %fusion.29) | copy-start | bytes 964
  164.9 1.5 copy-start.3
  166.4 3.3 copy-start
  167.9 4.1 copy-start.18
  172.0 35.5 %copy-start.12 = (bf16[8,80,512]{2,1,0:T(8,128)(2,1)}, bf16[8,80,512]{2,1,0:T(8,128)(2,1)S(1)}, u32[]{:S(2)}) copy-start(bf16[8,80,512]{2,1,0:T(8,128)(2,1)S(1)} %fusion.8) | copy-start | bytes 1966084
  207.5 36.7 %copy-start.2 = (bf16[256,1280]{1,0:T(8,128)(2,1)S(1)}, bf16[256,1280]{1,0:T(8,128)(2,1)}, u32[]{:S(2)}) copy-start(bf16[256,1280]{1,0:T(8,128)(2,1)} %param.12) | copy-start | bytes 1966084
  207.6 62.5 %all-gather.27.cloned.1.call-start = ((), (), s32[]{:S(2)}) async-start(), calls=%async_computation.20 | async-start | bytes 1966080 | tf_op jit(solution)/shard_map/all_gather | solution.py:167
  208.3 104.1 %all-gather.25.cloned.1.call-start = ((), (), s32[]{:S(2)}) async-start(), calls=%async_computation.18 | async-start | bytes 1740800 | tf_op jit(solution)/shard_map/all_gather | solution.py:124
  209.1 144.7 %all-gather.23.cloned.1.call-start = ((), (), s32[]{:S(2)}) async-start(), calls=%async_computation.17 | async-start | bytes 1740800 | tf_op jit(solution)/shard_map/all_gather | solution.py:123
  209.8 169.1 %all-gather.21.cloned.1.call-start = ((), (), s32[]{:S(2)}) async-start(), calls=%async_computation.16 | async-start | bytes 1966080 | tf_op jit(solution)/shard_map/all_gather | solution.py:158
  246.4 0.6 copy-start.20
  248.7 176.7 %reduce-scatter.15.cloned.1.call-start = ((), (), s32[]{:S(2)}) async-start(), calls=%async_computation.21 | async-start | bytes 3932160 | tf_op jit(solution)/shard_map/reduce_scatter | solution.py:173
  378.9 5.9 copy-start.28
  384.0 0.8 copy-start.15
  387.6 63.1 %reduce-scatter.13.cloned.1.call-start = ((), (), s32[]{:S(2)}) async-start(), calls=%async_computation.19 | async-start | bytes 1966080 | tf_op jit(solution)/shard_map/reduce_scatter | solution.py:163
  391.9 86.8 %all-gather.29.cloned.1.call-start = ((), (), s32[]{:S(2)}) async-start(), calls=%async_computation.22 | async-start | bytes 1966080 | tf_op jit(solution)/shard_map/all_gather | solution.py:177
  454.4 87.2 %reduce-scatter.17.cloned.1.call-start = ((), (), s32[]{:S(2)}) async-start(), calls=%async_computation.23 | async-start | bytes 3932160 | tf_op jit(solution)/shard_map/reduce_scatter | solution.py:205
  481.8 0.7 copy-start.16
  482.5 5.5 copy-start.11
  482.5 10.4 %slice-start = ((s8[8388608]{0:T(1024)(128)(4,1)}), s8[4194304]{0:T(1024)(128)(4,1)S(1)}, s32[]{:S(2)}) async-start(s8[8388608]{0:T(1024)(128)(4,1)} %bitcast.59), calls=%async_computation.30 | async-start | bytes 8388608
  488.0 5.0 slice-start.1
  492.9 2.7 copy-start.4
  493.0 2.7 copy-start.8
  493.0 2.7 copy-start.24
  496.6 1.4 copy-start.27
  498.0 1.3 copy-start.5
  498.0 1.7 copy-start.13
  499.7 1.4 copy-start.14
  503.9 109.4 %reduce-scatter.27.cloned.1.call-start = ((), (), s32[]{:S(2)}) async-start(), calls=%async_computation.28 | async-start | bytes 3481600 | tf_op jit(solution)/shard_map/reduce_scatter | solution.py:213
  508.3 175.4 %reduce-scatter.29.cloned.1.call-start = ((), (), s32[]{:S(2)}) async-start(), calls=%async_computation.29 | async-start | bytes 3481600 | tf_op jit(solution)/shard_map/reduce_scatter | solution.py:214
  513.7 240.0 %reduce-scatter.25.cloned.1.call-start = ((), (), s32[]{:S(2)}) async-start(), calls=%async_computation.27 | async-start | bytes 3481600 | tf_op jit(solution)/shard_map/reduce_scatter | solution.py:212
  518.2 306.1 %reduce-scatter.23.cloned.1.call-start = ((), (), s32[]{:S(2)}) async-start(), calls=%async_computation.26 | async-start | bytes 3481600 | tf_op jit(solution)/shard_map/reduce_scatter | solution.py:211
  521.2 1.1 copy-start.6
  521.2 373.2 %reduce-scatter.21.cloned.1.call-start = ((), (), s32[]{:S(2)}) async-start(), calls=%async_computation.25 | async-start | bytes 3481600 | tf_op jit(solution)/shard_map/reduce_scatter | solution.py:210
  525.4 439.6 %reduce-scatter.19.cloned.1.call-start = ((), (), s32[]{:S(2)}) async-start(), calls=%async_computation.24 | async-start | bytes 3481600 | tf_op jit(solution)/shard_map/reduce_scatter | solution.py:209
  528.3 0.7 copy-start.30
  528.3 13.3 %copy-start.17 = (f32[1280]{0:T(1024)S(1)}, f32[1280]{0:T(1024)}, u32[]{:S(2)}) copy-start(f32[1280]{0:T(1024)} %param.14) | copy-start | bytes 15364
  528.3 13.3 %copy-start.22 = (f32[256]{0:T(256)S(1)}, f32[256]{0:T(256)}, u32[]{:S(2)}) copy-start(f32[256]{0:T(256)} %copy-done.21) | copy-start | bytes 3076
  528.4 14.9 %copy-start.19 = (f32[1280]{0:T(1024)S(1)}, f32[1280]{0:T(1024)}, u32[]{:S(2)}) copy-start(f32[1280]{0:T(1024)} %get-tuple-element.67) | copy-start | bytes 15364
  528.4 54.7 %copy-start.9 = (f32[256,1280]{1,0:T(8,128)S(1)}, f32[256,1280]{1,0:T(8,128)}, u32[]{:S(2)}) copy-start(f32[256,1280]{1,0:T(8,128)} %get-tuple-element.75) | copy-start | bytes 3932164
  528.4 54.7 %copy-start.25 = (f32[256]{0:T(256)S(1)}, f32[256]{0:T(256)}, u32[]{:S(2)}) copy-start(f32[256]{0:T(256)} %get-tuple-element.94) | copy-start | bytes 3076
Sparse Core Ops, SparseCore 0:
  11.4 26.9 all-gather.10
  40.6 39.9 all-gather.16
  82.7 38.8 all-gather.12
  123.6 38.8 all-gather.14
  164.4 38.8 all-gather.18
  207.7 36.4 reduce-scatter.10
  245.8 24.2 all-gather.26
  272.5 39.9 all-gather.24
  314.9 38.8 all-gather.22
  355.8 23.1 all-gather.20
  387.7 37.5 reduce-scatter.14
  427.4 23.1 reduce-scatter.12
  454.5 24.2 all-gather.28
  504.0 37.5 reduce-scatter.16
  545.8 67.3 reduce-scatter.26
  618.0 65.6 reduce-scatter.28
  688.0 65.7 reduce-scatter.24
  758.5 65.7 reduce-scatter.22
  828.7 65.7 reduce-scatter.20
  899.2 65.7 reduce-scatter.18
where the time goes:
time: 973 us; the launch traced here: 972 us
  waiting for transfers between devices  808 us (83%)
  matrix products  75.9 us (8%)
  blocking collectives  39.8 us (4%)
  other arithmetic  25.1 us (3%)
  between operations  14.7 us (2%)
    reduce_scatter x1, waiting for transfers between devices, on_device(): lax.psum_scatter(grad_value_part, 'fsdp', scatter_dimension=0, tiled=True)  70.5 us
    reduce_scatter x1, waiting for transfers between devices, on_device(): lax.psum_scatter(grad_query_part, 'fsdp', scatter_dimension=0, tiled=True)  70.5 us
    reduce_scatter x1, waiting for transfers between devices, on_device(): lax.psum_scatter(grad_down_part, 'fsdp', scatter_dimension=1, tiled=True)  70.5 us
    reduce_scatter x1, waiting for transfers between devices, on_device(): lax.psum_scatter(grad_key_part, 'fsdp', scatter_dimension=0, tiled=True)  70.2 us
    reduce_scatter x1, waiting for transfers between devices, on_device(): lax.psum_scatter(grad_out_part, 'fsdp', scatter_dimension=1, tiled=True)  70 us
    all_gather x1, waiting for transfers between devices, on_device(): lax.all_gather(w_down, 'fsdp', axis=1, tiled=True)  42.4 us
    all_gather x1, waiting for transfers between devices, on_device(): lax.all_gather(w_key, 'fsdp', axis=0, tiled=True)  42.1 us
    psum x1, blocking collectives, on_device(): lax.psum((dgain_one, dgain_two, dscale_param), ('fsdp', 'tp'))  39.8 us
  transfers between devices with their start and end apart: 20, of which 20 were waited for; matrix products, arithmetic and copies ran while one was open for 6% of the time, Pallas kernels for 0%

commit v1 on v0

--- a/solution.py
+++ b/solution.py
@@ -1,8 +1,11 @@
+import functools
 import math
 
 import jax
 import jax.numpy as jnp
 from jax import lax
+from jax.experimental import pallas as pl
+from jax.experimental.pallas import tpu as pltpu
 from jax.sharding import PartitionSpec as P
 
 HD = 80
@@ -232,7 +235,713 @@
     )
 
 
+BF16, F32 = jnp.bfloat16, jnp.float32
+RING = (0, 2, 4, 6, 7, 5, 3, 1)
+CORES = tuple((i, i ^ 1) for i in range(16))
+AROUND = tuple((2 * RING[i], 2 * RING[(i + 1) % 8]) for i in range(8)) + tuple(
+    (2 * RING[i] + 1, 2 * RING[(i + 7) % 8] + 1) for i in range(8)
+)
+VMEM = pl.BlockSpec(memory_space=pltpu.VMEM)
+HELD = pl.BlockSpec(memory_space=pltpu.VMEM)
+LIMIT = 30 * 2**20
+UNROLL = (4, 8)
+SMEM = pl.BlockSpec(memory_space=pltpu.SMEM)
+ANY = pl.BlockSpec(memory_space=pl.ANY)
+LEAVE = (9, 6, 7, 4, 5, 2, 3, 1)
+STAY = (8, 14, 15, 12, 13, 10, 11, 0)
+STEPS = (1, 2, 2, 2, 1)
+FAR_STEPS = (1, 2, 2, 3)
+
+
+def sibling(value):
+    return lax.ppermute(value, "fsdp", CORES)
+
+
+def around(value):
+    return lax.ppermute(value, "fsdp", AROUND)
+
+
+def across(value):
+    return lax.ppermute(value, "tp", ((0, 1), (1, 0)))
+
+
+def arrival_order(rows):
+    index = lax.axis_index("fsdp")
+    chip, core = index // 2, lax.rem(index, 2)
+    place = jnp.where(lax.rem(chip, 2) == 0, chip // 2, 7 - chip // 2)
+    sign = 1 - 2 * core
+
+    def shard(step, which):
+        at = lax.rem(place + step + 16, 8)
+        return 2 * jnp.where(at < 4, 2 * at, 15 - 2 * at) + which
+
+    order = [shard(0, core), shard(0, 1 - core)]
+    for step in (1, 2, 3):
+        order += [shard(-step * sign, core), shard(-step * sign, 1 - core)]
+    order += [shard(4, core), shard(4, 1 - core)]
+    for step in (1, 2, 3):
+        order += [shard(step * sign, 1 - core), shard(step * sign, core)]
+    return jnp.stack([rows * o for o in order] + [lax.axis_index("tp")]).astype(jnp.int32)
+
+
+def after(value, *others):
+    return lax.optimization_barrier((value, *others))[0]
+
+
+def pack_kernel(query, key, value, out, up, down, early, late):
+    cols = query.shape[1]
+    for n, ref in enumerate((query, key, value)):
+        early[:, n * cols : (n + 1) * cols] = ref[...]
+    late[:, :cols] = out[...]
+    late[:, cols : 2 * cols] = up[...]
+    late[:, 2 * cols :] = down[...]
+
+
+def all_after(values, *others):
+    return lax.optimization_barrier((*values, *others))[: len(values)]
+
+
+def ring_gather(early, late, tokens, prepare):
+    rows = early.shape[0]
+    first = [early, sibling(early)]
+    here = [late, sibling(after(late, first[1]))]
+    other_tokens = across(tokens)
+    there = [across(after(late, other_tokens))]
+    first.append(around(jnp.concatenate(first)))
+    here.append(around(jnp.concatenate(here)))
+    first.append(around(after(first[2], other_tokens)))
+    here.append(around(here[2]))
+    there.append(across(here[2]))
+    first.append(around(after(first[3], there[0])))
+    here.append(around(here[3]))
+    there.append(across(here[3]))
+    prepared = prepare(other_tokens)
+    first.append(around(after(first[4][:rows], prepared, there[1])))
+    here.append(around(here[4][:rows]))
+    there.append(across(here[4]))
+    there.append(across(here[5]))
+    first += [sibling(after(first[5], here[5]))] + [sibling(first[n]) for n in (2, 3, 4)]
+    return (first, here, there, prepared, other_tokens)
+
+
+def swap_late(here, there, *wait):
+    there = [there[0], sibling(there[0])] + there[1:]
+    return [
+        got + [sibling(after(got[n], *wait)) for n in (5, 2, 3, 4)] for got in (here, there)
+    ]
+
+
+def total(*terms):
+    out = terms[0].astype(F32)
+    for term in terms[1:]:
+        out = out + term.astype(F32)
+    return out
+
+
+class Scatter:
+    def __init__(self, parts, far=None, note=None):
+        self.came_from = [sibling(part) for part in parts[:5]]
+        self.stay = parts[5:]
+        self.far = far
+        self.rows, self.cols = self.stay[0].shape
+        self.came = None
+        self.note = note
+        self.notes = []
+
+    def step(self, number, *wait):
+        terms = [self.stay[number], self.came_from[number]]
+        rows = STEPS[number] * self.rows
+        note = self.note is not None
+        if self.far is not None:
+            terms.append(self.far[number])
+        if self.came is not None:
+            terms.append(self.came)
+        elif note:
+            terms.append(self.note)
+        if number == 0 and note:
+            body = first_kernel
+        else:
+            body = functools.partial(add_kernel, number, note)
+        out = struct(rows + (16 if note else 0), self.cols)
+        sent = call(body, terms, [HELD] * len(terms), [(out, HELD)], [], 10**6)[0]
+        self.sent = sent
+        came = around(after(sent, *wait) if wait else sent)
+        if note:
+            self.notes.append(came[rows:])
+        self.came = came
+        return came
+
+    def finish(self):
+        rows = self.rows
+        came = self.came
+        terms = [self.stay[4], self.came_from[4], came[rows : 2 * rows], sibling(came[:rows])]
+        if self.far is not None:
+            terms.append(self.far[4])
+        return total(*terms)
+
+
+def dot(a, b, dims):
+    return lax.dot_general(a, b, (dims, ((), ())), preferred_element_type=F32)
+
+
+NN, NT = ((1,), (0,)), ((1,), (1,))
+
+
+def put_shards(order, pieces, target, sems):
+    rows = pieces[0].shape[0]
+    copies = []
+    for n, piece in enumerate(pieces[:2]):
+        to = pl.ds(pl.multiple_of(order[n], 16), rows)
+        copies.append(load(piece, target.at[to, :], sems.at[n]))
+    n = 2
+    for piece in pieces[2:]:
+        for part in range(piece.shape[0] // rows):
+            to = pl.ds(pl.multiple_of(order[n], 16), rows)
+            target[to, :] = piece[part * rows : (part + 1) * rows, :]
+            n += 1
+    wait_all(copies)
+
+
+def load(source, target, sem):
+    copy = pltpu.make_async_copy(source, target, sem)
+    copy.start()
+    return copy
+
+
+def wait_all(copies):
+    for copy in copies:
+        copy.wait()
+
+
+def allowed_bias(starts, bias):
+    length = bias.shape[0]
+    key_pos = lax.broadcasted_iota(jnp.int32, (length, 1), 0)
+    query_pos = lax.broadcasted_iota(jnp.int32, (1, length), 1)
+    key_series = jnp.zeros((length, 1), jnp.int32)
+    query_series = jnp.zeros((1, length), jnp.int32)
+    for n in range(starts.shape[1]):
+        key_series += (starts[0, n] <= key_pos).astype(jnp.int32)
+        query_series += (starts[0, n] <= query_pos).astype(jnp.int32)
+    allowed = (key_pos <= query_pos) & (key_series == query_series)
+    bias[...] = jnp.where(allowed, 0.0, -1e30).astype(F32)
+
+
+def attend_kernel(heads, order, starts, scaling, normed, *rest):
+    pieces, rest = rest[:10], rest[10:]
+    keep, send, logsum, proj_out, weights_out, proj_t, weights, bias, scores, mixed, sems = rest
+    cols = heads * HD
+    length = normed.shape[0]
+    allowed_bias(starts, bias)
+    put_shards(order, pieces, weights, sems)
+    stores = [load(weights, weights_out, sems.at[2])]
+    for n in range(3):
+        part = dot(normed[...], weights[:, n * cols : (n + 1) * cols], NN)
+        if n == 0:
+            part = part * scaling[...]
+        proj_t[n * cols : (n + 1) * cols, :] = part.astype(BF16).T
+    stores.append(load(proj_t, proj_out, sems.at[3]))
+    blocks = ((0, length // 2), (length // 2, length))
+
+    def rows(n, h):
+        return pl.ds(pl.multiple_of(n * cols + h * HD, 16), HD)
+
+    def one_head(h, slot):
+        query = proj_t[rows(0, h), :]
+        key = proj_t[rows(1, h), :].T
+        value = proj_t[rows(2, h), :]
+        for start, stop in blocks:
+            scores[slot, :stop, start:stop] = dot(key[:stop], query[:, start:stop], NN)
+        for start, stop in blocks:
+            part = scores[slot, :stop, start:stop] + bias[:stop, start:stop]
+            row_max = jnp.max(part, axis=0, keepdims=True)
+            exponent = jnp.exp(part - row_max)
+            total = jnp.sum(exponent, axis=0, keepdims=True)
+            soft_b = (exponent * (1.0 / total)).astype(BF16)
+            mixed[rows(0, h), start:stop] = dot(value[:, :stop], soft_b, NN).astype(BF16)
+            logsum[h, :, start:stop] = row_max + jnp.log(total)
+
+    @pl.loop(0, heads // UNROLL[0])
+    def _(block):
+        for n in range(UNROLL[0]):
+            one_head(block * UNROLL[0] + n, n)
+
+    half = order[16]
+    low, high = mixed[:, : length // 2], mixed[:, length // 2 :]
+    keep[...] = jnp.where(half == 0, low, high)
+    send[...] = jnp.where(half == 0, high, low)
+    wait_all(stores)
+
+
+def assemble_kernel(order, *rest):
+    here, there, (weights, sems) = rest[:10], rest[10:20], rest[20:]
+    put_shards(order, here, weights.at[0], sems)
+    put_shards(order, there, weights.at[1], sems)
+
+
+def middle_kernel(
+    tokens, cot, gain, keep, came, weights,
+    dkeep, dsend, hidden_o, dup_o, normed_o, dattn_o, mixed_o, middle_o, dgain_o, dmiddle_out,
+    dhidden, dmiddle_o, sem,
+):
+    cols = keep.shape[0]
+    out, up, down = (slice(n * cols, (n + 1) * cols) for n in range(3))
+
+    def half(n):
+        return pl.ds(pl.multiple_of(n * cols, 128), cols)
+
+    mixed_o[:, :cols] = keep[...].T
+    mixed_o[:, cols:] = came[...].T
+    middle_o[...] = tokens[...].astype(F32)
+
+    @pl.loop(0, 2)
+    def _(n):
+        middle_o[...] += dot(mixed_o[:, half(n)], weights[n, :, out], NT)
+        dhidden[:, half(n)] = dot(cot[...], weights[n, :, down], NN)
+
+    middle = middle_o[...]
+    scale = lax.rsqrt(jnp.mean(middle * middle, axis=-1, keepdims=True) + epsilon)
+    normed_o[...] = (middle * scale * gain[...]).astype(BF16)
+
+    @pl.loop(0, 2)
+    def _(n):
+        u = dot(normed_o[...], weights[n, :, up], NN)
+        root = math.sqrt(2.0 / math.pi)
+        square = u * u
+        tanh = jnp.tanh(root * u * (1.0 + 0.044715 * square))
+        gate = 0.5 * (1.0 + tanh)
+        hidden_o[:, half(n)] = (u * gate).astype(BF16)
+        slope = gate + 0.5 * u * (1.0 - tanh * tanh) * (root * (1.0 + 3 * 0.044715 * square))
+        dup_o[:, half(n)] = (dhidden[:, half(n)] * slope).astype(BF16)
+
+    dmiddle_o[...] = jnp.zeros_like(dmiddle_o)
+
+    @pl.loop(0, 2)
+    def _(n):
+        dmiddle_o[...] += dot(dup_o[:, half(n)], weights[n, :, up], NT)
+
+    dnormed = dmiddle_o[...]
+    middle = middle_o[...]
+    dgain_o[...] = jnp.sum(dnormed * middle * scale, axis=0, keepdims=True)
+    weighted = dnormed * gain[...]
+    mean = jnp.mean(weighted * middle, axis=-1, keepdims=True)
+    dmiddle = cot[...].astype(F32) + scale * weighted - middle * (scale * scale * scale * mean)
+    dmiddle_o[...] = dmiddle
+    store = load(dmiddle_o, dmiddle_out, sem)
+    dattn_o[...] = dmiddle.astype(BF16)
+    for n, ref in enumerate((dkeep, dsend)):
+        ref[...] = dot(dattn_o[...], weights[n, :, out], NN).astype(BF16).T
+    store.wait()
+
+
+def by_arrival(order, source_t, target, rows):
+    for n, which in enumerate(LEAVE + STAY):
+        target[n * rows : (n + 1) * rows, :] = source_t[
+            pl.ds(pl.multiple_of(order[which], 16), rows), :
+        ]
+
+
+def split_rows(steps, rows, at=0):
+    out = []
+    for count in steps:
+        out.append(slice(at, at + count * rows))
+        at += count * rows
+    return out
+
+
+def late_grads_kernel(order, hidden, dup, normed, dattn, mixed, middle, weights, cot, *rest):
+    outs, (grads, result, left_t, left, sems) = rest[:19], rest[19:]
+    cols = dup.shape[1] // 2
+    rows = dup.shape[1] // 16
+    pairs = ((dattn, mixed), (normed, dup), (cot, hidden))
+    for n, (a, _) in enumerate(pairs):
+        left_t[...] = a[...].T
+        by_arrival(order, left_t, left.at[n], rows)
+    stores = []
+    for leaves in range(2):
+        top = leaves * 8 * rows
+        part = slice(top, top + 8 * rows)
+        for side, steps, start in ((1, FAR_STEPS, 10), (0, STEPS, 0)):
+            for n, (_, b) in enumerate(pairs):
+                grads[side, part, n * cols : (n + 1) * cols] = dot(
+                    left[n, part, :], b[:, side * cols : (side + 1) * cols], NN
+                ).astype(BF16)
+            start += leaves * len(steps)
+            for k, at in enumerate(split_rows(steps, rows, top)):
+                stores.append(load(grads.at[side, at, :], outs[start + k], sems.at[start + k]))
+    total = middle[...]
+    for side in range(2):
+        at = slice(side * cols, (side + 1) * cols)
+        total = total + dot(hidden[:, at], weights[side, :, 2 * cols :], NT)
+    result[...] = total.astype(BF16)
+    stores.append(load(result, outs[18], sems.at[18]))
+    wait_all(stores)
+
+
+def attend_back_kernel(
+    heads, order, starts, scaling_col, keep, came, logsum, proj_in, weights_in, tokens_in, other_in,
+    dscaling, dgain, dproj_out, keep_out, send_out,
+    weights, proj_t, bias, dmixed, dproj_t, scores, dsofts, dproj, kept, sent, tokens, sems,
+):
+    fetch = load(proj_in, proj_t, sems.at[0])
+    fetch_late = [
+        load(weights_in, weights, sems.at[1]),
+        load(tokens_in, tokens.at[0], sems.at[2]),
+        load(other_in, tokens.at[1], sems.at[3]),
+    ]
+    cols = heads * HD
+    length = proj_t.shape[1]
+    rows = length // 2
+    allowed_bias(starts, bias)
+    half = order[16]
+    dmixed[:, :rows] = jnp.where(half == 0, keep[...], came[...])
+    dmixed[:, rows:] = jnp.where(half == 0, came[...], keep[...])
+    fetch.wait()
+    dscaling[...] = jnp.zeros_like(dscaling)
+
+    def place(n, h):
+        return pl.ds(pl.multiple_of(n * cols + h * HD, 16), HD)
+
+    def one_head(h, slot):
+        query = proj_t[place(0, h), :]
+        key_t = proj_t[place(1, h), :]
+        key = key_t.T
+        value = proj_t[place(2, h), :].T
+        grad = dmixed[place(0, h), :]
+        for start, stop in ((0, rows), (rows, length)):
+            scores[slot, :stop, start:stop] = dot(key[:stop], query[:, start:stop], NN)
+            dsofts[slot, :stop, start:stop] = dot(value[:stop], grad[:, start:stop], NN)
+        parts = []
+        for start, stop in ((rows, length), (0, rows)):
+            soft = scores[slot, :stop, start:stop] + bias[:stop, start:stop]
+            soft = jnp.exp(soft - logsum[h, :, start:stop])
+            dsoft = dsofts[slot, :stop, start:stop]
+            inner = jnp.sum(soft * dsoft, axis=0, keepdims=True)
+            dscores = (soft * (dsoft - inner)).astype(BF16)
+            dquery = dot(key_t[:, :stop], dscores, NN)
+            dscaling[...] += jnp.sum(
+                dquery * query[:, start:stop].astype(F32), axis=1, keepdims=True
+            )
+            dproj_t[place(0, h), start:stop] = (dquery * scaling_col[...]).astype(BF16)
+            parts.append(
+                (dot(dscores, query[:, start:stop], NT), dot(soft.astype(BF16), grad[:, start:stop], NT))
+            )
+        for n in range(2):
+            both = jnp.concatenate([parts[0][n][:rows] + parts[1][n], parts[0][n][rows:]], axis=0)
+            dproj_t[place(n + 1, h), :] = both.astype(BF16).T
+
+    @pl.loop(0, heads // UNROLL[1])
+    def _(block):
+        for n in range(UNROLL[1]):
+            one_head(block * UNROLL[1] + n, n % 2)
+
+    dproj[...] = dproj_t[...].T
+    stores = [load(dproj, dproj_out, sems.at[4])]
+    wait_all(fetch_late)
+    parts = []
+    total = jnp.zeros(dgain.shape, F32)
+    for n in range(2):
+        part = dot(dproj[n * rows : (n + 1) * rows, :], weights[...], NT)
+        resid = jnp.where(half == n, tokens[0], tokens[1]).astype(F32)
+        scale = lax.rsqrt(jnp.mean(resid * resid, axis=-1, keepdims=True) + epsilon)
+        total = total + jnp.sum(part * resid * scale, axis=0, keepdims=True)
+        parts.append(part)
+    dgain[...] = total
+    sent[...] = jnp.where(half == 0, parts[1], parts[0]).astype(BF16)
+    stores.append(load(sent, send_out, sems.at[5]))
+    kept[...] = jnp.where(half == 0, parts[0], parts[1])
+    stores.append(load(kept, keep_out, sems.at[6]))
+    wait_all(stores)
+
+
+def early_grads_kernel(order, normed, dproj_in, *rest):
+    outs, (dproj, grads, left_t, left, sems) = rest[:10], rest[10:]
+    fetch = load(dproj_in, dproj, sems.at[10])
+    rows = normed.shape[1] // 16
+    left_t[...] = normed[...].T
+    by_arrival(order, left_t, left, rows)
+    fetch.wait()
+    stores = []
+    for leaves in range(2):
+        top = leaves * 8 * rows
+        part = slice(top, top + 8 * rows)
+        grads[part, :] = dot(left[part, :], dproj[...], NN).astype(BF16)
+        for k, at in enumerate(split_rows(STEPS, rows, top)):
+            n = 5 * leaves + k
+            stores.append(load(grads.at[at, :], outs[n], sems.at[n]))
+    wait_all(stores)
+
+
+def first_kernel(stay, came, note, out):
+    rows = stay.shape[0]
+    out[:rows, :] = (stay[...].astype(F32) + came[...].astype(F32)).astype(BF16)
+    out[rows:, :] = note[...]
+
+
+def add_kernel(number, note, *rest):
+    *terms, out = rest
+    rows = terms[0].shape[0]
+    late = terms.pop() if number > 0 else None
+    part = terms[0][...].astype(F32)
+    for term in terms[1:]:
+        part = part + term[...].astype(F32)
+    if number == 1:
+        half = rows // 2
+        out[:half, :] = part[:half].astype(BF16)
+        out[half:rows, :] = (part[half:] + late[:half, :].astype(F32)).astype(BF16)
+    else:
+        if late is not None:
+            part = part + late[:rows, :].astype(F32)
+        out[:rows, :] = part.astype(BF16)
+    if note:
+        out[rows:, :] = late[late.shape[0] - 16 :, :]
+
+
+def pair_kernel(one, other, out):
+    out[...] = (one[...].astype(F32) + other[...].astype(F32)).astype(BF16)
+
+
+def struct(*shape, kind=BF16):
+    return jax.ShapeDtypeStruct(shape, kind)
+
+
+def call(body, inputs, spaces, outputs, scratch, flops):
+    place = {id(HELD): pltpu.VMEM, id(ANY): pltpu.HBM, id(VMEM): pltpu.HBM}
+    inputs = [
+        pltpu.with_memory_space_constraint(value, place[id(space)]) if id(space) in place else value
+        for value, space in zip(inputs, spaces)
+    ]
+    return pl.pallas_call(
+        body,
+        out_shape=[place[id(space)](out.shape, out.dtype) for out, space in outputs],
+        in_specs=[VMEM if space is HELD else space for space in spaces],
+        out_specs=[VMEM if space is HELD else space for _, space in outputs],
+        scratch_shapes=scratch,
+        compiler_params=pltpu.CompilerParams(vmem_limit_bytes=LIMIT),
+        cost_estimate=pl.CostEstimate(flops=flops * 4, bytes_accessed=2**22, transcendentals=0),
+    )(*inputs)
+
+
+def in_order(half, own, other, axis=0):
+    return jnp.where(
+        half == 0,
+        jnp.concatenate([own, other], axis=axis),
+        jnp.concatenate([other, own], axis=axis),
+    )
+
+
+def on_slice(
+    tokens,
+    seg_starts,
+    gain_attn,
+    gain_mlp,
+    query_scale,
+    w_query,
+    w_key,
+    w_value,
+    w_out,
+    w_up,
+    w_down,
+    cotangent,
+):
+    half = lax.axis_index("tp")
+    rows, width = tokens.shape
+    shard, cols = w_query.shape
+    length = 2 * rows
+    heads = cols // HD
+    dma = pltpu.SemaphoreType.DMA
+    order = arrival_order(shard)
+    early, late = call(
+        pack_kernel,
+        [w_query, w_key, w_value, w_out.T, w_up, w_down.T],
+        [VMEM] * 6,
+        [(struct(shard, 3 * cols), VMEM)] * 2,
+        [],
+        10**6,
+    )
+
+    def prepare(other_tokens):
+        row_tokens = in_order(half, tokens, other_tokens).astype(F32)
+        return (row_tokens * inverse_rms(row_tokens) * gain_attn).astype(BF16)
+
+    first, here, there, normed, other_tokens = ring_gather(early, late, tokens, prepare)
+    scaling = softplus_unit / math.sqrt(HD) * jax.nn.softplus(query_scale)
+    keep, send, logsum, proj_t, w_in = call(
+        functools.partial(attend_kernel, heads),
+        [after(order, there[2]), seg_starts, jnp.tile(scaling, heads)[None, :], normed]
+        + first,
+        [SMEM] * 2 + [HELD] * 2 + [ANY] * 2 + [HELD] * 8,
+        [
+            (struct(cols, rows), HELD),
+            (struct(cols, rows), HELD),
+            (struct(heads, 1, length, kind=F32), HELD),
+            (struct(3 * cols, length), ANY),
+            (struct(width, 3 * cols), ANY),
+        ],
+        [
+            pltpu.VMEM((3 * cols, length), BF16),
+            pltpu.VMEM((width, 3 * cols), BF16),
+            pltpu.VMEM((length, length), F32),
+            pltpu.VMEM((UNROLL[0], length, length), F32),
+            pltpu.VMEM((cols, length), BF16),
+            dma((4,)),
+        ],
+        8 * 10**9,
+    )
+    came = across(send)
+    here, there = swap_late(here, there, logsum)
+    w_late = call(
+        assemble_kernel,
+        [after(order, came), *here, *there],
+        [SMEM] + ([ANY] * 2 + [HELD] * 8) * 2,
+        [(struct(2, width, 3 * cols), HELD)],
+        [dma((2,))],
+        10**6,
+    )[0]
+    act = struct(rows, width)
+    dkeep, dsend, *saved, dgain_two, dmiddle = call(
+        middle_kernel,
+        [tokens, cotangent, gain_mlp[None, :], keep, came, w_late],
+        [HELD] * 6,
+        [(struct(cols, rows), HELD)] * 2
+        + [(act, HELD)] * 5
+        + [
+            (struct(rows, width, kind=F32), HELD),
+            (struct(1, width, kind=F32), HELD),
+            (struct(rows, width, kind=F32), ANY),
+        ],
+        [pltpu.VMEM((rows, width), F32), pltpu.VMEM((rows, width), F32), dma],
+        8 * 10**9,
+    )
+    dcame = across(dsend)
+    *parts, result = call(
+        late_grads_kernel,
+        [order, *saved, w_late, cotangent],
+        [SMEM] + [HELD] * 8,
+        [(struct(n * shard, 3 * cols), ANY) for n in STEPS * 2 + FAR_STEPS * 2] + [(act, ANY)],
+        [
+            pltpu.VMEM((2, width, 3 * cols), BF16),
+            pltpu.VMEM((rows, width), BF16),
+            pltpu.VMEM((width, rows), BF16),
+            pltpu.VMEM((3, width, rows), BF16),
+            dma((19,)),
+        ],
+        6 * 10**9,
+    )
+    *parts, result = all_after((*parts, result), dcame)
+    far = []
+    for n, steps in enumerate(FAR_STEPS):
+        pair = [parts[14 + n], sibling(parts[10 + n])]
+        sent = call(pair_kernel, pair, [HELD] * 2, [(struct(steps * shard, 3 * cols), HELD)], [], 10**6)
+        far.append(across(sent[0]))
+    far_last = far.pop()
+    far += [far_last[: 2 * shard], far_last[2 * shard :]]
+    late_sum = Scatter(parts[:10], far)
+    late_one = late_sum.step(0)
+    dscaling, dgain_one, dproj, dnormed, dnormed_send = call(
+        functools.partial(attend_back_kernel, heads),
+        [
+            after(order, late_sum.came_from[0]),
+            seg_starts,
+            scaling[:, None],
+            dkeep,
+            dcame,
+            logsum,
+            proj_t,
+            w_in,
+            tokens,
+            other_tokens,
+        ],
+        [SMEM] * 2 + [HELD] * 4 + [ANY] * 4,
+        [
+            (struct(HD, 1, kind=F32), HELD),
+            (struct(1, width, kind=F32), HELD),
+            (struct(length, 3 * cols), ANY),
+            (struct(rows, width, kind=F32), ANY),
+            (act, ANY),
+        ],
+        [
+            pltpu.VMEM((width, 3 * cols), BF16),
+            pltpu.VMEM((3 * cols, length), BF16),
+            pltpu.VMEM((length, length), F32),
+            pltpu.VMEM((cols, length), BF16),
+            pltpu.VMEM((3 * cols, length), BF16),
+            pltpu.VMEM((2, length, length), F32),
+            pltpu.VMEM((2, length, length), F32),
+            pltpu.VMEM((length, 3 * cols), BF16),
+            pltpu.VMEM((rows, width), F32),
+            pltpu.VMEM((rows, width), BF16),
+            pltpu.VMEM((2, rows, width), BF16),
+            dma((7,)),
+        ],
+        12 * 10**9,
+    )
+    dscaling, dgain_one, dproj, dnormed, dnormed_send = all_after(
+        (dscaling, dgain_one, dproj, dnormed, dnormed_send), *far[:2]
+    )
+    dscale_param = (
+        dscaling[:, 0] / scaling * (softplus_unit / math.sqrt(HD)) * jax.nn.sigmoid(query_scale)
+    )
+    note = jnp.concatenate(
+        [
+            jnp.concatenate([dgain_one, jnp.pad(dscale_param[None, :], ((0, 0), (0, cols - HD)))], axis=1),
+            jnp.pad(dgain_two, ((0, 0), (0, cols))),
+        ]
+    )
+    parts = call(
+        early_grads_kernel,
+        [order, normed, dproj],
+        [SMEM, HELD, ANY],
+        [(struct(n * shard, 3 * cols), ANY) for n in STEPS + STEPS],
+        [
+            pltpu.VMEM((length, 3 * cols), BF16),
+            pltpu.VMEM((width, 3 * cols), BF16),
+            pltpu.VMEM((width, length), BF16),
+            pltpu.VMEM((width, length), BF16),
+            dma((11,)),
+        ],
+        5 * 10**9,
+    )
+    note = note + sibling(after(note, parts[1]))
+    high = lax.reduce_precision(note, 8, 7)
+    coded = jnp.concatenate([high, note - high, jnp.zeros((12, 3 * cols), F32)]).astype(BF16)
+    parts = all_after(parts, late_one, far[2])
+    late_two = late_sum.step(1)
+    early_sum = Scatter(parts, note=coded)
+    early_sum.step(0)
+    late_three = late_sum.step(2)
+    dnormed = dnormed + across(dnormed_send).astype(F32)
+    resid = tokens.astype(F32)
+    dresid_one, _ = norm_backward(resid, inverse_rms(resid), gain_attn, dnormed)
+    early_sum.step(1, late_two)
+    late_four = late_sum.step(3)
+    early_sum.step(2, late_three)
+    early_sum.step(3, late_four)
+    dlate = late_sum.finish()
+    din = early_sum.finish()
+    mine = early_sum.notes
+    core = lax.rem(lax.axis_index("fsdp"), 2)
+    heard = total(*mine[:3]) + jnp.where(core == 0, 1.0, 0.0) * mine[3].astype(F32)
+    heard = heard[:2] + heard[2:4]
+    heard = heard + sibling(heard)
+    small = note + heard
+    small = small + across(small)
+    return (
+        result,
+        dmiddle + dresid_one,
+        small[0, :width],
+        small[1, :width],
+        small[0, width : width + HD],
+        din[:, :cols],
+        din[:, cols : 2 * cols],
+        din[:, 2 * cols :],
+        dlate[:, :cols].T,
+        dlate[:, cols : 2 * cols],
+        dlate[:, 2 * cols :].T,
+    )
+
+
 def solution(mesh):
+    body = on_slice if dict(mesh.shape) == {"fsdp": 16, "tp": 2} else on_device
     placed = (
         P(("fsdp", "tp"), None),
         P("fsdp", None),
@@ -248,7 +957,7 @@
         P(("fsdp", "tp"), None),
     )
     return jax.shard_map(
-        on_device,
+        body,
         mesh=mesh,
         in_specs=placed,
         out_specs=(

time: 973 us -> 229 us (0.24)
  waiting for transfers between devices: 808 us -> 100 us
  matrix products: 75.9 us -> 0 us
  Pallas kernels: 0 us -> 56.1 us
  starting transfers between devices: 1.21 us -> 47.4 us
  blocking collectives: 39.8 us -> 0 us
  other arithmetic: 25.1 us -> 10.6 us
  between operations: 14.7 us -> 1.81 us
    reduce_scatter x10 -> x0, waiting for transfers between devices: 482 us -> none  [the longest x1 70.5 us: on_device(): lax.psum_scatter(grad_value_part, 'fsdp', scatter_dimension=0, tiled=True)]
    all_gather x10 -> x0, waiting for transfers between devices: 322 us -> none  [the longest x1 42.4 us: on_device(): lax.all_gather(w_down, 'fsdp', axis=1, tiled=True)]
    ppermute x0 -> x63, waiting for transfers between devices: none -> 100 us  [the longest x16 47.5 us: around(): return lax.ppermute(value, 'fsdp', AROUND)]
    dot_general x24 -> x0, matrix products: 75.9 us -> none  [the longest x1 5.44 us: one_block(): jnp.einsum('hqk,qhd->khd', soft.astype(jnp.bfloat16), dmixed_blk, preferr...]
    pallas_call x0 -> x19, Pallas kernels: none -> 56.1 us  [call(): pl.pallas_call(body, out_shape=[place[id(space)](out.shape, out.dtype) fo...]
    ppermute x0 -> x63, starting transfers between devices: none -> 47.4 us  [the longest x16 20.1 us: around(): return lax.ppermute(value, 'fsdp', AROUND)]
    psum x1 -> x0, blocking collectives: 39.8 us -> none  [on_device(): lax.psum((dgain_one, dgain_two, dscale_param), ('fsdp', 'tp'))]
  transfers between devices with their start and end apart: 20 -> 63, of which waited for: 20 -> 27; matrix products, arithmetic and copies ran while one was open for 6% -> 7% of each run, Pallas kernels for 0% -> 19%
where the time goes in v1:
time: 229 us; the launch traced here: 226 us
  waiting for transfers between devices  100 us (44%)
  Pallas kernels  56.1 us (24%)
  starting transfers between devices  47.4 us (21%)
  other arithmetic  10.6 us (5%)
  local copies, waits for them, and re-layouts  9.71 us (4%)
    pallas_call x19, Pallas kernels, call(): pl.pallas_call(body, out_shape=[place[id(space)](out.shape, out.dtype) fo...  56.1 us
    ppermute x16, waiting for transfers between devices, around(): return lax.ppermute(value, 'fsdp', AROUND)  47.5 us
    ppermute x14, waiting for transfers between devices, across(): return lax.ppermute(value, 'tp', ((0, 1), (1, 0)))  44.7 us
    ppermute x16, starting transfers between devices, around(): return lax.ppermute(value, 'fsdp', AROUND)  20.1 us
    ppermute x14, starting transfers between devices, across(): return lax.ppermute(value, 'tp', ((0, 1), (1, 0)))  17.7 us
    ppermute x33, starting transfers between devices, sibling(): return lax.ppermute(value, 'fsdp', CORES)  9.7 us
    ppermute x33, waiting for transfers between devices, sibling(): return lax.ppermute(value, 'fsdp', CORES)  8.24 us
  transfers between devices with their start and end apart: 63, of which 27 were waited for; matrix products, arithmetic and copies ran while one was open for 7% of the time, Pallas kernels for 19%

profile of v1, /device:TPU:0, one launch (start us, length us, event | category | flops | bytes accessed | tf_op | source)
XLA Modules:
  0.0 226.1 jit_solution(1026423145325312338)
XLA Ops:
  0.6 2.0 shard_map.203
  3.1 1.4 collective-permute-done.rest_1_
  4.9 2.6 %collective-permute-start.5 = (bf16[256,1280]{1,0:T(8,128)(2,1)}, bf16[256,1280]{1,0:T(8,128)(2,1)S(1)}, u32[]{:S(2)}, u32[]{:S(2)}) collective-permute-start(bf16[256,1280]{1,0:T(8,128)(2,1)} %tokens_in.1), channel_id=1, source_target_pairs={{0,1},{1,0},{2,3},{3,2},{4,5},{5,4},{6,7},{7,6},{8,9},{9,8},{10,11... | collective-permute-start | bytes 1966088 | tf_op jit(solution)/shard_map/ppermute | solution.py:265
  7.5 1.0 pad_maximum_fusion.1
  8.6 1.6 collective-permute-start.6
  10.3 1.6 collective-permute-start.2
  11.9 11.1 %collective-permute-done.5.other_in = bf16[256,1280]{1,0:T(8,128)(2,1)S(1)} collective-permute-done((bf16[256,1280]{1,0:T(8,128)(2,1)}, bf16[256,1280]{1,0:T(8,128)(2,1)S(1)}, u32[]{:S(2)}, u32[]{:S(2)}) %collective-permute-start.5) | collective-permute-done | bytes 655392 | tf_op jit(solution)/shard_map/ppermute | solution.py:265
  23.0 1.8 collective-permute-start.7
  25.4 1.6 collective-permute-start.3
  28.4 1.1 collective-permute-start.10
  29.5 7.6 %collective-permute-done.8.rest_10_ = bf16[80,1920]{1,0:T(8,128)(2,1)S(1)} collective-permute-done((bf16[80,1920]{1,0:T(8,128)(2,1)S(1)}, bf16[80,1920]{1,0:T(8,128)(2,1)S(1)}, u32[]{:S(2)}, u32[]{:S(2)}) %collective-permute-start.8) | collective-permute-done | bytes 307232 | tf_op jit(solution)/shard_map/ppermute | solution.py:265
  37.1 1.6 collective-permute-start.9
  38.7 1.3 collective-permute-done.3.rest_3_
  40.1 1.8 collective-permute-start.12
  41.9 1.8 fusion.2.normed
  43.7 3.9 %collective-permute-done.9.rest_4_ = bf16[160,1920]{1,0:T(8,128)(2,1)} collective-permute-done((bf16[160,1920]{1,0:T(8,128)(2,1)}, bf16[160,1920]{1,0:T(8,128)(2,1)}, u32[]{:S(2)}, u32[]{:S(2)}) %collective-permute-start.9) | collective-permute-done | bytes 614432 | tf_op jit(solution)/shard_map/ppermute | solution.py:261
  47.6 1.0 slice.92
  48.6 1.6 collective-permute-start.11
  51.2 2.8 %collective-permute-done.12.rest_4_ = bf16[160,1920]{1,0:T(8,128)(2,1)S(1)} collective-permute-done((bf16[160,1920]{1,0:T(8,128)(2,1)}, bf16[160,1920]{1,0:T(8,128)(2,1)S(1)}, u32[]{:S(2)}, u32[]{:S(2)}) %collective-permute-start.12) | collective-permute-done | bytes 614432 | tf_op jit(solution)/shard_map/ppermute | solution.py:261
  54.1 1.8 collective-permute-start.13
  55.9 1.6 collective-permute-done.11.rest_5_
  57.5 3.7 %collective-permute-done.13.rest_5_ = bf16[80,1920]{1,0:T(8,128)(2,1)S(1)} collective-permute-done((bf16[80,1920]{1,0:T(8,128)(2,1)S(1)}, bf16[80,1920]{1,0:T(8,128)(2,1)S(1)}, u32[]{:S(2)}, u32[]{:S(2)}) %collective-permute-start.13) | collective-permute-done | bytes 307232 | tf_op jit(solution)/shard_map/ppermute | solution.py:261
  61.5 3.2 %collective-permute-done.4.rest_13_ = bf16[160,1920]{1,0:T(8,128)(2,1)} collective-permute-done((bf16[160,1920]{1,0:T(8,128)(2,1)}, bf16[160,1920]{1,0:T(8,128)(2,1)}, u32[]{:S(2)}, u32[]{:S(2)}) %collective-permute-start.4) | collective-permute-done | bytes 614432 | tf_op jit(solution)/shard_map/ppermute | solution.py:265
  64.7 1.1 collective-permute-start.24
  66.8 10.9 %shard_map.204 = (bf16[640,256]{1,0:T(8,128)(2,1)S(1)}, bf16[640,256]{1,0:T(8,128)(2,1)S(1)}, f32[8,1,512]{2,1,0:T(1,128)S(1)}, bf16[1920,512]{1,0:T(8,128)(2,1)}, bf16[1280,1920]{1,0:T(8,128)(2,1)}) custom-call(s32[17]{0:T(128)S(1)} %stack.71.order, s32[1,8]{1,0:T(1,128)S(1)} %copy-done.24, f32[1,640]{1,0:T(1,128)S(1)} %broadcast_in_dim_tile.3.scaling, ...), custom_call_target="tpu_custom_call" | custom-call | flops 32000000000 | bytes 4194304 | tf_op jit(solution)/shard_map/pallas_call | solution.py:713
  77.7 3.5 %collective-permute-done.24.rest_14_ = bf16[160,1920]{1,0:T(8,128)(2,1)S(1)} collective-permute-done((bf16[160,1920]{1,0:T(8,128)(2,1)S(1)}, bf16[160,1920]{1,0:T(8,128)(2,1)S(1)}, u32[]{:S(2)}, u32[]{:S(2)}) %collective-permute-start.24) | collective-permute-done | bytes 614432 | tf_op jit(solution)/shard_map/ppermute | solution.py:265
  81.2 1.3 collective-permute-start.18
  82.7 1.9 collective-permute-done.25.rest_15_
  85.2 1.0 collective-permute-done.26.rest_16_
  86.8 4.7 %collective-permute-done.18.came = bf16[640,256]{1,0:T(8,128)(2,1)S(1)} collective-permute-done((bf16[640,256]{1,0:T(8,128)(2,1)S(1)}, bf16[640,256]{1,0:T(8,128)(2,1)S(1)}, u32[]{:S(2)}, u32[]{:S(2)}) %collective-permute-start.18) | collective-permute-done | bytes 327712 | tf_op jit(solution)/shard_map/ppermute | solution.py:265
  92.1 2.5 %collective-permute-done.21.rest_8_ = bf16[160,1920]{1,0:T(8,128)(2,1)S(1)} collective-permute-done((bf16[160,1920]{1,0:T(8,128)(2,1)}, bf16[160,1920]{1,0:T(8,128)(2,1)S(1)}, u32[]{:S(2)}, u32[]{:S(2)}) %collective-permute-start.21) | collective-permute-done | bytes 614432 | tf_op jit(solution)/shard_map/ppermute | solution.py:257
  94.6 3.4 %shard_map.205.weights = bf16[2,1280,1920]{2,1,0:T(8,128)(2,1)S(1)} custom-call(s32[17]{0:T(128)S(1)} %stack.71.order, bf16[80,1920]{1,0:T(8,128)(2,1)} %get-tuple-element.122.rest_0_, bf16[80,1920]{1,0:T(8,128)(2,1)} %copy-done.34, bf16[160,1920]{1,0:T(8,128)(2,1)S(1)} %collective-permute-done.2.rest_2_, bf16[160,1920]{1,0:T(8,128)(2,1)} %collective-permute-done.3.rest_3_, ...), custom_call_target="tpu_custom_call" | custom-call | flops 4000000 | bytes 4194304 | tf_op jit(solution)/shard_map/pallas_call | solution.py:713
  98.0 8.5 %shard_map.206 = (bf16[640,256]{1,0:T(8,128)(2,1)S(1)}, bf16[640,256]{1,0:T(8,128)(2,1)S(1)}, bf16[256,1280]{1,0:T(8,128)(2,1)S(1)}, bf16[256,1280]{1,0:T(8,128)...) custom-call(bf16[256,1280]{1,0:T(8,128)(2,1)S(1)} %copy-done, ...), custom_call_target="tpu_custom_call" | custom-call | flops 32000000000 | bytes 4194304 | tf_op jit(solution)/shard_map/pallas_call | solution.py:713
  106.5 1.3 collective-permute-start.30
  107.8 6.5 %shard_map.207 = (bf16[80,1920]{1,0:T(8,128)(2,1)}, bf16[160,1920]{1,0:T(8,128)(2,1)}, bf16[160,1920]{1,0:T(8,128)(2,1)}, bf16[160,1920]{1,0:T(8,128)(2,1)}, bf1...) custom-call(s32[17]{0:T(128)S(1)} %stack.71.order, ...), custom_call_target="tpu_custom_call" | custom-call | flops 24000000000 | bytes 4194304 | tf_op jit(solution)/shard_map/pallas_call | solution.py:713
  114.3 2.0 collective-permute-done.30.came
  118.3 1.8 collective-permute-done.32.other
  121.2 1.3 collective-permute-start.33
  123.6 12.5 %shard_map.208 = (f32[80,1]{1,0:T(8,128)S(1)}, f32[1,1280]{1,0:T(1,128)S(1)}, bf16[512,1920]{1,0:T(8,128)(2,1)}, f32[256,1280]{1,0:T(8,128)}, bf16[256,1280]{1,0:T(8,128)(2,1)}) custom-call(s32[17]{0:T(128)S(1)} %stack.71.order, s32[1,8]{1,0:T(1,128)S(1)} %copy-done.25, f32[80,1]{1,0:T(8,128)S(1)} %copy.24.scaling_col, bf16[640,256]{1,0:T(8,128)(2,1)S(1)} %copy-done.27, ...), custom_call_target="tpu_custom_call" | custom-call | flops 48000000000 | bytes 4194304 | tf_op jit(solution)/shard_map/pallas_call | solution.py:713
  136.7 1.1 shard_map.212
  137.8 1.5 collective-permute-start.38
  139.5 1.1 collective-permute-start.40
  140.6 3.5 %collective-permute-done.35.rest_2_ = bf16[160,1920]{1,0:T(8,128)(2,1)S(1)} collective-permute-done((bf16[160,1920]{1,0:T(8,128)(2,1)S(1)}, bf16[160,1920]{1,0:T(8,128)(2,1)S(1)}, u32[]{:S(2)}, u32[]{:S(2)}) %collective-permute-start.35) | collective-permute-done | bytes 614432 | tf_op jit(solution)/shard_map/ppermute | solution.py:265
  144.9 6.8 %shard_map.211 = (bf16[80,1920]{1,0:T(8,128)(2,1)}, bf16[160,1920]{1,0:T(8,128)(2,1)}, bf16[160,1920]{1,0:T(8,128)(2,1)}, bf16[160,1920]{1,0:T(8,128)(2,1)}, bf1...) custom-call(s32[17]{0:T(128)S(1)} %stack.71.order, ...), custom_call_target="tpu_custom_call" | custom-call | flops 20000000000 | bytes 4194304 | tf_op jit(solution)/shard_map/pallas_call | solution.py:713
  152.7 1.1 copy-done.12
  153.7 1.6 shard_map.216
  155.3 2.1 collective-permute-start.45
  157.4 2.1 collective-permute-start.41
  159.6 1.1 collective-permute-done.41.came
  161.6 1.8 collective-permute-start.54
  163.4 8.0 %collective-permute-done.42.rest_2_ = bf16[96,1920]{1,0:T(8,128)(2,1)S(1)} collective-permute-done((bf16[96,1920]{1,0:T(8,128)(2,1)S(1)}, bf16[96,1920]{1,0:T(8,128)(2,1)S(1)}, u32[]{:S(2)}, u32[]{:S(2)}) %collective-permute-start.42) | collective-permute-done | bytes 368672 | tf_op jit(solution)/shard_map/ppermute | solution.py:261
  172.2 1.6 collective-permute-start.49
  175.3 7.2 %collective-permute-done.46.rest_2_ = bf16[176,1920]{1,0:T(8,128)(2,1)S(1)} collective-permute-done((bf16[176,1920]{1,0:T(8,128)(2,1)S(1)}, bf16[176,1920]{1,0:T(8,128)(2,1)S(1)}, u32[]{:S(2)}, u32[]{:S(2)}) %collective-permute-start.46) | collective-permute-done | bytes 675872 | tf_op jit(solution)/shard_map/ppermute | solution.py:261
  182.7 6.3 %collective-permute-done.49.rest_3_ = bf16[160,1920]{1,0:T(8,128)(2,1)S(1)} collective-permute-done((bf16[160,1920]{1,0:T(8,128)(2,1)S(1)}, bf16[160,1920]{1,0:T(8,128)(2,1)S(1)}, u32[]{:S(2)}, u32[]{:S(2)}) %collective-permute-start.49) | collective-permute-done | bytes 614432 | tf_op jit(solution)/shard_map/ppermute | solution.py:261
  189.7 1.1 shard_map.221
  190.9 1.1 collective-permute-start.55
  192.6 6.2 %collective-permute-done.36 = bf16[256,1280]{1,0:T(8,128)(2,1)} collective-permute-done((bf16[256,1280]{1,0:T(8,128)(2,1)}, bf16[256,1280]{1,0:T(8,128)(2,1)}, u32[]{:S(2)}, u32[]{:S(2)}) %collective-permute-start.36) | collective-permute-done | bytes 655392 | tf_op jit(solution)/shard_map/ppermute | solution.py:265
  199.2 2.0 fusion.3
  201.5 5.1 %collective-permute-done.55 = bf16[160,1920]{1,0:T(8,128)(2,1)} collective-permute-done((bf16[160,1920]{1,0:T(8,128)(2,1)}, bf16[160,1920]{1,0:T(8,128)(2,1)}, u32[]{:S(2)}, u32[]{:S(2)}) %collective-permute-start.55) | collective-permute-done | bytes 614432 | tf_op jit(solution)/shard_map/ppermute | solution.py:261
  206.7 2.6 %fusion.6 = f32[256,1280]{1,0:T(8,128)} fusion(f32[256,1280]{1,0:T(8,128)S(1)} %copy-done.32, bf16[256,1280]{1,0:T(8,128)(2,1)S(1)} %copy-done.1, f32[256,1280]{1,0:T(8,128)S(1)} %copy-done.30, bf16[256,1280]{1,0:T(8,128)(2,1)} %collective-permute-done.36, f32[256]{0:T(256)S(1)} %broadcast_multiply_fusion, f32[256]{0:T(256)S(1)} %get-tuple-element.236, ...), kind=kLoop, calls=%fused_computation.11 | loop fusion | flops 2949120 | bytes 5251072 | tf_op jit(solution)/shard_map/add | solution.py:930
  209.3 1.0 slice.110
  210.4 7.0 %collective-permute-done.56 = bf16[176,1920]{1,0:T(8,128)(2,1)S(1)} collective-permute-done((bf16[176,1920]{1,0:T(8,128)(2,1)S(1)}, bf16[176,1920]{1,0:T(8,128)(2,1)S(1)}, u32[]{:S(2)}, u32[]{:S(2)}) %collective-permute-start.56) | collective-permute-done | bytes 675872 | tf_op jit(solution)/shard_map/ppermute | solution.py:261
  218.4 1.3 convert_add_fusion
  219.7 1.8 collective-permute-start.58
  (222 shorter events, 24.1 us)
Async XLA Ops:
  2.6 1.9 collective-permute-start
  4.5 5.7 %collective-permute-start.1 = (bf16[80,1920]{1,0:T(8,128)(2,1)}, bf16[80,1920]{1,0:T(8,128)(2,1)S(1)}, u32[]{:S(2)}, u32[]{:S(2)}) collective-permute-start(bf16[80,1920]{1,0:T(8,128)(2,1)} %get-tuple-element.122.rest_0_), channel_id=1, source_target_pairs={{0,2},{2,0},{4,6},{6,4},{8,10},{10,8},{12,14},{14,12},{16,18},{18,... | collective-permute-start | bytes 921608 | tf_op jit(solution)/shard_map/ppermute | solution.py:257
  4.9 18.1 %collective-permute-start.5 = (bf16[256,1280]{1,0:T(8,128)(2,1)}, bf16[256,1280]{1,0:T(8,128)(2,1)S(1)}, u32[]{:S(2)}, u32[]{:S(2)}) collective-permute-start(bf16[256,1280]{1,0:T(8,128)(2,1)} %tokens_in.1), channel_id=1, source_target_pairs={{0,1},{1,0},{2,3},{3,2},{4,5},{5,4},{6,7},{7,6},{8,9},{9,8},{10,11... | collective-permute-start | bytes 1966088 | tf_op jit(solution)/shard_map/ppermute | solution.py:265
  8.6 33.3 %copy-start.42 = (f32[1280]{0:T(1024)S(1)}, f32[1280]{0:T(1024)}, u32[]{:S(2)}) copy-start(f32[1280]{0:T(1024)} %param.14) | copy-start | bytes 15364
  8.6 14.4 %collective-permute-start.6 = (bf16[160,1920]{1,0:T(8,128)(2,1)S(1)}, bf16[160,1920]{1,0:T(8,128)(2,1)}, u32[]{:S(2)}, u32[]{:S(2)}) collective-permute-start(bf16[160,1920]{1,0:T(8,128)(2,1)S(1)} %pad_maximum_fusion.1), channel_id=1, source_target_pairs={{0,8},{8,16},{16,24},{24,28},{28,20},{20,12},{12,4},{4,0},{2,6},{1... | collective-permute-start | bytes 1843208 | tf_op jit(solution)/shard_map/ppermute | solution.py:261
  10.3 15.1 %collective-permute-start.2 = (bf16[160,1920]{1,0:T(8,128)(2,1)S(1)}, bf16[160,1920]{1,0:T(8,128)(2,1)S(1)}, u32[]{:S(2)}, u32[]{:S(2)}) collective-permute-start(bf16[160,1920]{1,0:T(8,128)(2,1)S(1)} %pad_maximum_fusion), channel_id=1, source_target_pairs={{0,8},{8,16},{16,24},{24,28},{28,20},{20,12},{12,4},{4,0},{2,6},{1... | collective-permute-start | bytes 1843208 | tf_op jit(solution)/shard_map/ppermute | solution.py:261
  23.0 14.1 %collective-permute-start.7 = (bf16[160,1920]{1,0:T(8,128)(2,1)}, bf16[160,1920]{1,0:T(8,128)(2,1)}, u32[]{:S(2)}, u32[]{:S(2)}) collective-permute-start(bf16[160,1920]{1,0:T(8,128)(2,1)} %collective-permute-done.6.rest_2_), channel_id=1, source_target_pairs={{0,8},{8,16},{16,24},{24,28},{28,20},{20,12},{12,4},{4,0},{2,6},{1... | collective-permute-start | bytes 1843208 | tf_op jit(solution)/shard_map/ppermute | solution.py:261
  25.4 14.7 %collective-permute-start.3 = (bf16[160,1920]{1,0:T(8,128)(2,1)S(1)}, bf16[160,1920]{1,0:T(8,128)(2,1)}, u32[]{:S(2)}, u32[]{:S(2)}) collective-permute-start(bf16[160,1920]{1,0:T(8,128)(2,1)S(1)} %collective-permute-done.2.rest_2_), channel_id=1, source_target_pairs={{0,8},{8,16},{16,24},{24,28},{28,20},{20,12},{12,4},{4,0},{2,6},{1... | collective-permute-start | bytes 1843208 | tf_op jit(solution)/shard_map/ppermute | solution.py:261
  26.9 10.2 %collective-permute-start.8 = (bf16[80,1920]{1,0:T(8,128)(2,1)S(1)}, bf16[80,1920]{1,0:T(8,128)(2,1)S(1)}, u32[]{:S(2)}, u32[]{:S(2)}) collective-permute-start(bf16[80,1920]{1,0:T(8,128)(2,1)S(1)} %copy-done.33), channel_id=1, source_target_pairs={{0,1},{1,0},{2,3},{3,2},{4,5},{5,4},{6,7},{7,6},{8,9},{9,8},{10,11... | collective-permute-start | bytes 921608 | tf_op jit(solution)/shard_map/ppermute | solution.py:265
  28.4 20.2 %collective-permute-start.10 = (bf16[160,1920]{1,0:T(8,128)(2,1)S(1)}, bf16[160,1920]{1,0:T(8,128)(2,1)S(1)}, u32[]{:S(2)}, u32[]{:S(2)}) collective-permute-start(bf16[160,1920]{1,0:T(8,128)(2,1)S(1)} %collective-permute-done.2.rest_2_), channel_id=1, source_target_pairs={{0,1},{1,0},{2,3},{3,2},{4,5},{5,4},{6,7},{7,6},{8,9},{9,8},{10,11... | collective-permute-start | bytes 1843208 | tf_op jit(solution)/shard_map/ppermute | solution.py:265
  37.1 10.5 %collective-permute-start.9 = (bf16[160,1920]{1,0:T(8,128)(2,1)}, bf16[160,1920]{1,0:T(8,128)(2,1)}, u32[]{:S(2)}, u32[]{:S(2)}) collective-permute-start(bf16[160,1920]{1,0:T(8,128)(2,1)} %collective-permute-done.7.rest_3_), channel_id=1, source_target_pairs={{0,8},{8,16},{16,24},{24,28},{28,20},{20,12},{12,4},{4,0},{2,6},{1... | collective-permute-start | bytes 1843208 | tf_op jit(solution)/shard_map/ppermute | solution.py:261
  40.1 14.0 %collective-permute-start.12 = (bf16[160,1920]{1,0:T(8,128)(2,1)}, bf16[160,1920]{1,0:T(8,128)(2,1)S(1)}, u32[]{:S(2)}, u32[]{:S(2)}) collective-permute-start(bf16[160,1920]{1,0:T(8,128)(2,1)} %collective-permute-done.3.rest_3_), channel_id=1, source_target_pairs={{0,8},{8,16},{16,24},{24,28},{28,20},{20,12},{12,4},{4,0},{2,6},{1... | collective-permute-start | bytes 1843208 | tf_op jit(solution)/shard_map/ppermute | solution.py:261
  48.6 8.9 %collective-permute-start.11 = (bf16[80,1920]{1,0:T(8,128)(2,1)S(1)}, bf16[80,1920]{1,0:T(8,128)(2,1)}, u32[]{:S(2)}, u32[]{:S(2)}) collective-permute-start(bf16[80,1920]{1,0:T(8,128)(2,1)S(1)} %slice.92), channel_id=1, source_target_pairs={{0,8},{8,16},{16,24},{24,28},{28,20},{20,12},{12,4},{4,0},{2,6},{1... | collective-permute-start | bytes 921608 | tf_op jit(solution)/shard_map/ppermute | solution.py:261
  50.3 14.4 %collective-permute-start.4 = (bf16[160,1920]{1,0:T(8,128)(2,1)}, bf16[160,1920]{1,0:T(8,128)(2,1)}, u32[]{:S(2)}, u32[]{:S(2)}) collective-permute-start(bf16[160,1920]{1,0:T(8,128)(2,1)} %collective-permute-done.3.rest_3_), channel_id=1, source_target_pairs={{0,1},{1,0},{2,3},{3,2},{4,5},{5,4},{6,7},{7,6},{8,9},{9,8},{10,11... | collective-permute-start | bytes 1843208 | tf_op jit(solution)/shard_map/ppermute | solution.py:265
  51.2 14.6 %collective-permute-start.15 = (bf16[160,1920]{1,0:T(8,128)(2,1)}, bf16[160,1920]{1,0:T(8,128)(2,1)}, u32[]{:S(2)}, u32[]{:S(2)}) collective-permute-start(bf16[160,1920]{1,0:T(8,128)(2,1)} %collective-permute-done.6.rest_2_), channel_id=1, source_target_pairs={{0,2},{2,0},{4,6},{6,4},{8,10},{10,8},{12,14},{14,12},{16,18},{18,... | collective-permute-start | bytes 1843208 | tf_op jit(solution)/shard_map/ppermute | solution.py:257
  54.1 7.1 %collective-permute-start.13 = (bf16[80,1920]{1,0:T(8,128)(2,1)S(1)}, bf16[80,1920]{1,0:T(8,128)(2,1)S(1)}, u32[]{:S(2)}, u32[]{:S(2)}) collective-permute-start(bf16[80,1920]{1,0:T(8,128)(2,1)S(1)} %slice.93), channel_id=1, source_target_pairs={{0,8},{8,16},{16,24},{24,28},{28,20},{20,12},{12,4},{4,0},{2,6},{1... | collective-permute-start | bytes 921608 | tf_op jit(solution)/shard_map/ppermute | solution.py:261
  55.9 10.8 %collective-permute-start.16 = (bf16[160,1920]{1,0:T(8,128)(2,1)}, bf16[160,1920]{1,0:T(8,128)(2,1)}, u32[]{:S(2)}, u32[]{:S(2)}) collective-permute-start(bf16[160,1920]{1,0:T(8,128)(2,1)} %collective-permute-done.7.rest_3_), channel_id=1, source_target_pairs={{0,2},{2,0},{4,6},{6,4},{8,10},{10,8},{12,14},{14,12},{16,18},{18,... | collective-permute-start | bytes 1843208 | tf_op jit(solution)/shard_map/ppermute | solution.py:257
  57.5 9.3 %collective-permute-start.17 = (bf16[160,1920]{1,0:T(8,128)(2,1)}, bf16[160,1920]{1,0:T(8,128)(2,1)}, u32[]{:S(2)}, u32[]{:S(2)}) collective-permute-start(bf16[160,1920]{1,0:T(8,128)(2,1)} %collective-permute-done.9.rest_4_), channel_id=1, source_target_pairs={{0,2},{2,0},{4,6},{6,4},{8,10},{10,8},{12,14},{14,12},{16,18},{18,... | collective-permute-start | bytes 1843208 | tf_op jit(solution)/shard_map/ppermute | solution.py:257
  61.2 5.5 %collective-permute-start.14 = (bf16[80,1920]{1,0:T(8,128)(2,1)}, bf16[80,1920]{1,0:T(8,128)(2,1)}, u32[]{:S(2)}, u32[]{:S(2)}) collective-permute-start(bf16[80,1920]{1,0:T(8,128)(2,1)} %collective-permute-done.11.rest_5_), channel_id=1, source_target_pairs={{0,2},{2,0},{4,6},{6,4},{8,10},{10,8},{12,14},{14,12},{16,18},{18,... | collective-permute-start | bytes 921608 | tf_op jit(solution)/shard_map/ppermute | solution.py:257
  64.7 16.5 %collective-permute-start.24 = (bf16[160,1920]{1,0:T(8,128)(2,1)S(1)}, bf16[160,1920]{1,0:T(8,128)(2,1)S(1)}, u32[]{:S(2)}, u32[]{:S(2)}) collective-permute-start(bf16[160,1920]{1,0:T(8,128)(2,1)S(1)} %collective-permute-done.12.rest_4_), channel_id=1, source_target_pairs={{0,1},{1,0},{2,3},{3,2},{4,5},{5,4},{6,7},{7,6},{8,9},{9,8},{10,11... | collective-permute-start | bytes 1843208 | tf_op jit(solution)/shard_map/ppermute | solution.py:265
  65.8 18.8 %collective-permute-start.25 = (bf16[80,1920]{1,0:T(8,128)(2,1)S(1)}, bf16[80,1920]{1,0:T(8,128)(2,1)S(1)}, u32[]{:S(2)}, u32[]{:S(2)}) collective-permute-start(bf16[80,1920]{1,0:T(8,128)(2,1)S(1)} %collective-permute-done.13.rest_5_), channel_id=1, source_target_pairs={{0,1},{1,0},{2,3},{3,2},{4,5},{5,4},{6,7},{7,6},{8,9},{9,8},{10,11... | collective-permute-start | bytes 921608 | tf_op jit(solution)/shard_map/ppermute | solution.py:265
  81.2 10.3 %collective-permute-start.29 = (bf16[160,1920]{1,0:T(8,128)(2,1)S(1)}, bf16[160,1920]{1,0:T(8,128)(2,1)S(1)}, u32[]{:S(2)}, u32[]{:S(2)}) collective-permute-start(bf16[160,1920]{1,0:T(8,128)(2,1)S(1)} %collective-permute-done.24.rest_14_), channel_id=1, source_target_pairs={{0,2},{2,0},{4,6},{6,4},{8,10},{10,8},{12,14},{14,12},{16,18},{18,... | collective-permute-start | bytes 1843208 | tf_op jit(solution)/shard_map/ppermute | solution.py:257
  81.2 10.3 %collective-permute-start.18 = (bf16[640,256]{1,0:T(8,128)(2,1)S(1)}, bf16[640,256]{1,0:T(8,128)(2,1)S(1)}, u32[]{:S(2)}, u32[]{:S(2)}) collective-permute-start(bf16[640,256]{1,0:T(8,128)(2,1)S(1)} %get-tuple-element.127), channel_id=1, source_target_pairs={{0,1},{1,0},{2,3},{3,2},{4,5},{5,4},{6,7},{7,6},{8,9},{9,8},{10,11... | collective-permute-start | bytes 983048 | tf_op jit(solution)/shard_map/ppermute | solution.py:265
  82.5 2.7 %collective-permute-start.23 = (bf16[80,1920]{1,0:T(8,128)(2,1)S(1)}, bf16[80,1920]{1,0:T(8,128)(2,1)S(1)}, u32[]{:S(2)}, u32[]{:S(2)}) collective-permute-start(bf16[80,1920]{1,0:T(8,128)(2,1)S(1)} %copy-done.37), channel_id=1, source_target_pairs={{0,2},{2,0},{4,6},{6,4},{8,10},{10,8},{12,14},{14,12},{16,18},{18,... | collective-permute-start | bytes 921608 | tf_op jit(solution)/shard_map/ppermute | solution.py:257
  84.6 1.6 collective-permute-start.26
  84.6 2.0 collective-permute-start.19
  85.1 6.9 %collective-permute-start.28 = (bf16[160,1920]{1,0:T(8,128)(2,1)}, bf16[160,1920]{1,0:T(8,128)(2,1)S(1)}, u32[]{:S(2)}, u32[]{:S(2)}) collective-permute-start(bf16[160,1920]{1,0:T(8,128)(2,1)} %collective-permute-done.4.rest_13_), channel_id=1, source_target_pairs={{0,2},{2,0},{4,6},{6,4},{8,10},{10,8},{12,14},{14,12},{16,18},{18,... | collective-permute-start | bytes 1843208 | tf_op jit(solution)/shard_map/ppermute | solution.py:257
  86.2 5.8 %collective-permute-start.27 = (bf16[160,1920]{1,0:T(8,128)(2,1)S(1)}, bf16[160,1920]{1,0:T(8,128)(2,1)S(1)}, u32[]{:S(2)}, u32[]{:S(2)}) collective-permute-start(bf16[160,1920]{1,0:T(8,128)(2,1)S(1)} %copy-done.14), channel_id=1, source_target_pairs={{0,2},{2,0},{4,6},{6,4},{8,10},{10,8},{12,14},{14,12},{16,18},{18,... | collective-permute-start | bytes 1843208 | tf_op jit(solution)/shard_map/ppermute | solution.py:257
  86.7 5.4 %collective-permute-start.22 = (bf16[160,1920]{1,0:T(8,128)(2,1)S(1)}, bf16[160,1920]{1,0:T(8,128)(2,1)S(1)}, u32[]{:S(2)}, u32[]{:S(2)}) collective-permute-start(bf16[160,1920]{1,0:T(8,128)(2,1)S(1)} %collective-permute-done.12.rest_4_), channel_id=1, source_target_pairs={{0,2},{2,0},{4,6},{6,4},{8,10},{10,8},{12,14},{14,12},{16,18},{18,... | collective-permute-start | bytes 1843208 | tf_op jit(solution)/shard_map/ppermute | solution.py:257
  91.5 3.0 %collective-permute-start.21 = (bf16[160,1920]{1,0:T(8,128)(2,1)}, bf16[160,1920]{1,0:T(8,128)(2,1)S(1)}, u32[]{:S(2)}, u32[]{:S(2)}) collective-permute-start(bf16[160,1920]{1,0:T(8,128)(2,1)} %collective-permute-done.3.rest_3_), channel_id=1, source_target_pairs={{0,2},{2,0},{4,6},{6,4},{8,10},{10,8},{12,14},{14,12},{16,18},{18,... | collective-permute-start | bytes 1843208 | tf_op jit(solution)/shard_map/ppermute | solution.py:257
  91.5 3.0 %collective-permute-start.20 = (bf16[160,1920]{1,0:T(8,128)(2,1)S(1)}, bf16[160,1920]{1,0:T(8,128)(2,1)S(1)}, u32[]{:S(2)}, u32[]{:S(2)}) collective-permute-start(bf16[160,1920]{1,0:T(8,128)(2,1)S(1)} %collective-permute-done.2.rest_2_), channel_id=1, source_target_pairs={{0,2},{2,0},{4,6},{6,4},{8,10},{10,8},{12,14},{14,12},{16,18},{18,... | collective-permute-start | bytes 1843208 | tf_op jit(solution)/shard_map/ppermute | solution.py:257
  106.5 9.8 %collective-permute-start.30 = (bf16[640,256]{1,0:T(8,128)(2,1)S(1)}, bf16[640,256]{1,0:T(8,128)(2,1)S(1)}, u32[]{:S(2)}, u32[]{:S(2)}) collective-permute-start(bf16[640,256]{1,0:T(8,128)(2,1)S(1)} %get-tuple-element.163), channel_id=1, source_target_pairs={{0,1},{1,0},{2,3},{3,2},{4,5},{5,4},{6,7},{7,6},{8,9},{9,8},{10,11... | collective-permute-start | bytes 983048 | tf_op jit(solution)/shard_map/ppermute | solution.py:265
  117.0 5.5 %collective-permute-start.34 = (bf16[160,1920]{1,0:T(8,128)(2,1)}, bf16[160,1920]{1,0:T(8,128)(2,1)S(1)}, u32[]{:S(2)}, u32[]{:S(2)}) collective-permute-start(bf16[160,1920]{1,0:T(8,128)(2,1)} %get-tuple-element.179), channel_id=1, source_target_pairs={{0,2},{2,0},{4,6},{6,4},{8,10},{10,8},{12,14},{14,12},{16,18},{18,... | collective-permute-start | bytes 1843208 | tf_op jit(solution)/shard_map/ppermute | solution.py:257
  117.0 3.1 %collective-permute-start.32 = (bf16[80,1920]{1,0:T(8,128)(2,1)}, bf16[80,1920]{1,0:T(8,128)(2,1)S(1)}, u32[]{:S(2)}, u32[]{:S(2)}) collective-permute-start(bf16[80,1920]{1,0:T(8,128)(2,1)} %get-tuple-element.177), channel_id=1, source_target_pairs={{0,2},{2,0},{4,6},{6,4},{8,10},{10,8},{12,14},{14,12},{16,18},{18,... | collective-permute-start | bytes 921608 | tf_op jit(solution)/shard_map/ppermute | solution.py:257
  117.6 5.0 %collective-permute-start.31 = (bf16[80,1920]{1,0:T(8,128)(2,1)}, bf16[80,1920]{1,0:T(8,128)(2,1)}, u32[]{:S(2)}, u32[]{:S(2)}) collective-permute-start(bf16[80,1920]{1,0:T(8,128)(2,1)} %get-tuple-element.166), channel_id=1, source_target_pairs={{0,2},{2,0},{4,6},{6,4},{8,10},{10,8},{12,14},{14,12},{16,18},{18,... | collective-permute-start | bytes 921608 | tf_op jit(solution)/shard_map/ppermute | solution.py:257
  117.7 34.9 %collective-permute-start.44 = (bf16[160,1920]{1,0:T(8,128)(2,1)}, bf16[160,1920]{1,0:T(8,128)(2,1)}, u32[]{:S(2)}, u32[]{:S(2)}) collective-permute-start(bf16[160,1920]{1,0:T(8,128)(2,1)} %get-tuple-element.205), channel_id=1, source_target_pairs={{0,2},{2,0},{4,6},{6,4},{8,10},{10,8},{12,14},{14,12},{16,18},{18,... | collective-permute-start | bytes 1843208 | tf_op jit(solution)/shard_map/ppermute | solution.py:257
  118.3 21.1 %collective-permute-start.39 = (bf16[160,1920]{1,0:T(8,128)(2,1)}, bf16[160,1920]{1,0:T(8,128)(2,1)S(1)}, u32[]{:S(2)}, u32[]{:S(2)}) collective-permute-start(bf16[160,1920]{1,0:T(8,128)(2,1)} %get-tuple-element.199), channel_id=1, source_target_pairs={{0,2},{2,0},{4,6},{6,4},{8,10},{10,8},{12,14},{14,12},{16,18},{18,... | collective-permute-start | bytes 1843208 | tf_op jit(solution)/shard_map/ppermute | solution.py:257
  121.2 15.4 %collective-permute-start.33 = (bf16[80,1920]{1,0:T(8,128)(2,1)S(1)}, bf16[80,1920]{1,0:T(8,128)(2,1)S(1)}, u32[]{:S(2)}, u32[]{:S(2)}) collective-permute-start(bf16[80,1920]{1,0:T(8,128)(2,1)S(1)} %shard_map.209), channel_id=1, source_target_pairs={{0,1},{1,0},{2,3},{3,2},{4,5},{5,4},{6,7},{7,6},{8,9},{9,8},{10,11... | collective-permute-start | bytes 921608 | tf_op jit(solution)/shard_map/ppermute | solution.py:265
  122.7 21.3 %collective-permute-start.35 = (bf16[160,1920]{1,0:T(8,128)(2,1)S(1)}, bf16[160,1920]{1,0:T(8,128)(2,1)S(1)}, u32[]{:S(2)}, u32[]{:S(2)}) collective-permute-start(bf16[160,1920]{1,0:T(8,128)(2,1)S(1)} %shard_map.210), channel_id=1, source_target_pairs={{0,1},{1,0},{2,3},{3,2},{4,5},{5,4},{6,7},{7,6},{8,9},{9,8},{10,11... | collective-permute-start | bytes 1843208 | tf_op jit(solution)/shard_map/ppermute | solution.py:265
  137.8 14.8 %collective-permute-start.38 = (bf16[80,1920]{1,0:T(8,128)(2,1)S(1)}, bf16[80,1920]{1,0:T(8,128)(2,1)}, u32[]{:S(2)}, u32[]{:S(2)}) collective-permute-start(bf16[80,1920]{1,0:T(8,128)(2,1)S(1)} %shard_map.212), channel_id=1, source_target_pairs={{0,8},{8,16},{16,24},{24,28},{28,20},{20,12},{12,4},{4,0},{2,6},{1... | collective-permute-start | bytes 921608 | tf_op jit(solution)/shard_map/ppermute | solution.py:261
  139.5 17.9 %collective-permute-start.40 = (bf16[160,1920]{1,0:T(8,128)(2,1)S(1)}, bf16[160,1920]{1,0:T(8,128)(2,1)S(1)}, u32[]{:S(2)}, u32[]{:S(2)}) collective-permute-start(bf16[160,1920]{1,0:T(8,128)(2,1)S(1)} %shard_map.213), channel_id=1, source_target_pairs={{0,1},{1,0},{2,3},{3,2},{4,5},{5,4},{6,7},{7,6},{8,9},{9,8},{10,11... | collective-permute-start | bytes 1843208 | tf_op jit(solution)/shard_map/ppermute | solution.py:265
  151.9 7.6 %collective-permute-start.37 = (f32[2,1920]{1,0:T(2,128)S(1)}, f32[2,1920]{1,0:T(2,128)S(1)}, u32[]{:S(2)}, u32[]{:S(2)}) collective-permute-start(f32[2,1920]{1,0:T(2,128)S(1)} %fusion.10), channel_id=1, source_target_pairs={{0,2},{2,0},{4,6},{6,4},{8,10},{10,8},{12,14},{14,12},{16,18},{18,... | collective-permute-start | bytes 46088 | tf_op jit(solution)/shard_map/ppermute | solution.py:257
  152.1 9.2 %collective-permute-start.53 = (bf16[240,1920]{1,0:T(8,128)(2,1)}, bf16[240,1920]{1,0:T(8,128)(2,1)S(1)}, u32[]{:S(2)}, u32[]{:S(2)}) collective-permute-start(bf16[240,1920]{1,0:T(8,128)(2,1)} %get-tuple-element.217), channel_id=1, source_target_pairs={{0,2},{2,0},{4,6},{6,4},{8,10},{10,8},{12,14},{14,12},{16,18},{18,... | collective-permute-start | bytes 2764808 | tf_op jit(solution)/shard_map/ppermute | solution.py:257
  152.6 19.2 %collective-permute-start.48 = (bf16[160,1920]{1,0:T(8,128)(2,1)}, bf16[160,1920]{1,0:T(8,128)(2,1)S(1)}, u32[]{:S(2)}, u32[]{:S(2)}) collective-permute-start(bf16[160,1920]{1,0:T(8,128)(2,1)} %get-tuple-element.210), channel_id=1, source_target_pairs={{0,2},{2,0},{4,6},{6,4},{8,10},{10,8},{12,14},{14,12},{16,18},{18,... | collective-permute-start | bytes 1843208 | tf_op jit(solution)/shard_map/ppermute | solution.py:257
  155.3 16.3 %collective-permute-start.45 = (bf16[160,1920]{1,0:T(8,128)(2,1)S(1)}, bf16[160,1920]{1,0:T(8,128)(2,1)S(1)}, u32[]{:S(2)}, u32[]{:S(2)}) collective-permute-start(bf16[160,1920]{1,0:T(8,128)(2,1)S(1)} %shard_map.216), channel_id=1, source_target_pairs={{0,8},{8,16},{16,24},{24,28},{28,20},{20,12},{12,4},{4,0},{2,6},{1... | collective-permute-start | bytes 1843208 | tf_op jit(solution)/shard_map/ppermute | solution.py:261
  157.4 3.3 %collective-permute-start.41 = (bf16[80,1920]{1,0:T(8,128)(2,1)S(1)}, bf16[80,1920]{1,0:T(8,128)(2,1)S(1)}, u32[]{:S(2)}, u32[]{:S(2)}) collective-permute-start(bf16[80,1920]{1,0:T(8,128)(2,1)S(1)} %copy-done.48), channel_id=1, source_target_pairs={{0,2},{2,0},{4,6},{6,4},{8,10},{10,8},{12,14},{14,12},{16,18},{18,... | collective-permute-start | bytes 921608 | tf_op jit(solution)/shard_map/ppermute | solution.py:257
  159.5 2.1 collective-permute-start.43
  160.7 14.0 %collective-permute-start.47 = (bf16[160,1920]{1,0:T(8,128)(2,1)S(1)}, bf16[160,1920]{1,0:T(8,128)(2,1)S(1)}, u32[]{:S(2)}, u32[]{:S(2)}) collective-permute-start(bf16[160,1920]{1,0:T(8,128)(2,1)S(1)} %copy-done.46), channel_id=1, source_target_pairs={{0,2},{2,0},{4,6},{6,4},{8,10},{10,8},{12,14},{14,12},{16,18},{18,... | collective-permute-start | bytes 1843208 | tf_op jit(solution)/shard_map/ppermute | solution.py:257
  161.3 10.1 %collective-permute-start.42 = (bf16[96,1920]{1,0:T(8,128)(2,1)S(1)}, bf16[96,1920]{1,0:T(8,128)(2,1)S(1)}, u32[]{:S(2)}, u32[]{:S(2)}) collective-permute-start(bf16[96,1920]{1,0:T(8,128)(2,1)S(1)} %shard_map.214), channel_id=1, source_target_pairs={{0,8},{8,16},{16,24},{24,28},{28,20},{20,12},{12,4},{4,0},{2,6},{1... | collective-permute-start | bytes 1105928 | tf_op jit(solution)/shard_map/ppermute | solution.py:261
  161.6 28.0 %collective-permute-start.54 = (bf16[240,1920]{1,0:T(8,128)(2,1)S(1)}, bf16[240,1920]{1,0:T(8,128)(2,1)S(1)}, u32[]{:S(2)}, u32[]{:S(2)}) collective-permute-start(bf16[240,1920]{1,0:T(8,128)(2,1)S(1)} %shard_map.220), channel_id=1, source_target_pairs={{0,1},{1,0},{2,3},{3,2},{4,5},{5,4},{6,7},{7,6},{8,9},{9,8},{10,11... | collective-permute-start | bytes 2764808 | tf_op jit(solution)/shard_map/ppermute | solution.py:265
  171.6 10.9 %collective-permute-start.46 = (bf16[176,1920]{1,0:T(8,128)(2,1)S(1)}, bf16[176,1920]{1,0:T(8,128)(2,1)S(1)}, u32[]{:S(2)}, u32[]{:S(2)}) collective-permute-start(bf16[176,1920]{1,0:T(8,128)(2,1)S(1)} %shard_map.215), channel_id=1, source_target_pairs={{0,8},{8,16},{16,24},{24,28},{28,20},{20,12},{12,4},{4,0},{2,6},{1... | collective-permute-start | bytes 2027528 | tf_op jit(solution)/shard_map/ppermute | solution.py:261
  172.2 16.9 %collective-permute-start.49 = (bf16[160,1920]{1,0:T(8,128)(2,1)S(1)}, bf16[160,1920]{1,0:T(8,128)(2,1)S(1)}, u32[]{:S(2)}, u32[]{:S(2)}) collective-permute-start(bf16[160,1920]{1,0:T(8,128)(2,1)S(1)} %shard_map.218), channel_id=1, source_target_pairs={{0,8},{8,16},{16,24},{24,28},{28,20},{20,12},{12,4},{4,0},{2,6},{1... | collective-permute-start | bytes 1843208 | tf_op jit(solution)/shard_map/ppermute | solution.py:261
  173.8 16.0 %collective-permute-start.52 = (bf16[160,1920]{1,0:T(8,128)(2,1)S(1)}, bf16[160,1920]{1,0:T(8,128)(2,1)S(1)}, u32[]{:S(2)}, u32[]{:S(2)}) collective-permute-start(bf16[160,1920]{1,0:T(8,128)(2,1)S(1)} %copy-done.45), channel_id=1, source_target_pairs={{0,2},{2,0},{4,6},{6,4},{8,10},{10,8},{12,14},{14,12},{16,18},{18,... | collective-permute-start | bytes 1843208 | tf_op jit(solution)/shard_map/ppermute | solution.py:257
  174.7 24.0 %collective-permute-start.36 = (bf16[256,1280]{1,0:T(8,128)(2,1)}, bf16[256,1280]{1,0:T(8,128)(2,1)}, u32[]{:S(2)}, u32[]{:S(2)}) collective-permute-start(bf16[256,1280]{1,0:T(8,128)(2,1)} %get-tuple-element.181), channel_id=1, source_target_pairs={{0,1},{1,0},{2,3},{3,2},{4,5},{5,4},{6,7},{7,6},{8,9},{9,8},{10,11... | collective-permute-start | bytes 1966088 | tf_op jit(solution)/shard_map/ppermute | solution.py:265
  189.1 12.1 %collective-permute-start.50 = (bf16[176,1920]{1,0:T(8,128)(2,1)S(1)}, bf16[176,1920]{1,0:T(8,128)(2,1)S(1)}, u32[]{:S(2)}, u32[]{:S(2)}) collective-permute-start(bf16[176,1920]{1,0:T(8,128)(2,1)S(1)} %shard_map.217), channel_id=1, source_target_pairs={{0,8},{8,16},{16,24},{24,28},{28,20},{20,12},{12,4},{4,0},{2,6},{1... | collective-permute-start | bytes 2027528 | tf_op jit(solution)/shard_map/ppermute | solution.py:261
  189.1 12.0 %collective-permute-start.51 = (bf16[160,1920]{1,0:T(8,128)(2,1)}, bf16[160,1920]{1,0:T(8,128)(2,1)S(1)}, u32[]{:S(2)}, u32[]{:S(2)}) collective-permute-start(bf16[160,1920]{1,0:T(8,128)(2,1)} %get-tuple-element.213), channel_id=1, source_target_pairs={{0,2},{2,0},{4,6},{6,4},{8,10},{10,8},{12,14},{14,12},{16,18},{18,... | collective-permute-start | bytes 1843208 | tf_op jit(solution)/shard_map/ppermute | solution.py:257
  190.9 15.7 %collective-permute-start.55 = (bf16[160,1920]{1,0:T(8,128)(2,1)}, bf16[160,1920]{1,0:T(8,128)(2,1)}, u32[]{:S(2)}, u32[]{:S(2)}) collective-permute-start(bf16[160,1920]{1,0:T(8,128)(2,1)} %shard_map.221), channel_id=1, source_target_pairs={{0,8},{8,16},{16,24},{24,28},{28,20},{20,12},{12,4},{4,0},{2,6},{1... | collective-permute-start | bytes 1843208 | tf_op jit(solution)/shard_map/ppermute | solution.py:261
  192.0 26.4 %collective-permute-start.61 = (bf16[80,1920]{1,0:T(8,128)(2,1)}, bf16[80,1920]{1,0:T(8,128)(2,1)S(1)}, u32[]{:S(2)}, u32[]{:S(2)}) collective-permute-start(bf16[80,1920]{1,0:T(8,128)(2,1)} %get-tuple-element.222), channel_id=1, source_target_pairs={{0,2},{2,0},{4,6},{6,4},{8,10},{10,8},{12,14},{14,12},{16,18},{18,... | collective-permute-start | bytes 921608 | tf_op jit(solution)/shard_map/ppermute | solution.py:257
  198.8 25.9 %collective-permute-start.59 = (bf16[80,1920]{1,0:T(8,128)(2,1)}, bf16[80,1920]{1,0:T(8,128)(2,1)S(1)}, u32[]{:S(2)}, u32[]{:S(2)}) collective-permute-start(bf16[80,1920]{1,0:T(8,128)(2,1)} %get-tuple-element.220), channel_id=1, source_target_pairs={{0,2},{2,0},{4,6},{6,4},{8,10},{10,8},{12,14},{14,12},{16,18},{18,... | collective-permute-start | bytes 921608 | tf_op jit(solution)/shard_map/ppermute | solution.py:257
  206.6 10.8 %collective-permute-start.56 = (bf16[176,1920]{1,0:T(8,128)(2,1)S(1)}, bf16[176,1920]{1,0:T(8,128)(2,1)S(1)}, u32[]{:S(2)}, u32[]{:S(2)}) collective-permute-start(bf16[176,1920]{1,0:T(8,128)(2,1)S(1)} %shard_map.219), channel_id=1, source_target_pairs={{0,8},{8,16},{16,24},{24,28},{28,20},{20,12},{12,4},{4,0},{2,6},{1... | collective-permute-start | bytes 2027528 | tf_op jit(solution)/shard_map/ppermute | solution.py:261
  210.3 8.1 %collective-permute-start.62 = (bf16[80,1920]{1,0:T(8,128)(2,1)S(1)}, bf16[80,1920]{1,0:T(8,128)(2,1)S(1)}, u32[]{:S(2)}, u32[]{:S(2)}) collective-permute-start(bf16[80,1920]{1,0:T(8,128)(2,1)S(1)} %slice.110), channel_id=1, source_target_pairs={{0,2},{2,0},{4,6},{6,4},{8,10},{10,8},{12,14},{14,12},{16,18},{18,... | collective-permute-start | bytes 921608 | tf_op jit(solution)/shard_map/ppermute | solution.py:257
  218.3 1.4 collective-permute-start.57
  219.7 3.8 %collective-permute-start.58 = (f32[2,1920]{1,0:T(2,128)S(1)}, f32[2,1920]{1,0:T(2,128)S(1)}, u32[]{:S(2)}, u32[]{:S(2)}) collective-permute-start(f32[2,1920]{1,0:T(2,128)S(1)} %add_add_fusion), channel_id=1, source_target_pairs={{0,1},{1,0},{2,3},{3,2},{4,5},{5,4},{6,7},{7,6},{8,9},{9,8},{10,11... | collective-permute-start | bytes 46088 | tf_op jit(solution)/shard_map/ppermute | solution.py:265
  222.3 2.3 %collective-permute-start.60 = (bf16[80,1920]{1,0:T(8,128)(2,1)S(1)}, bf16[80,1920]{1,0:T(8,128)(2,1)S(1)}, u32[]{:S(2)}, u32[]{:S(2)}) collective-permute-start(bf16[80,1920]{1,0:T(8,128)(2,1)S(1)} %slice.105), channel_id=1, source_target_pairs={{0,2},{2,0},{4,6},{6,4},{8,10},{10,8},{12,14},{14,12},{16,18},{18,... | collective-permute-start | bytes 921608 | tf_op jit(solution)/shard_map/ppermute | solution.py:257
  (50 other events, 444.4 us)

commit v2 on v1

--- a/solution.py
+++ b/solution.py
@@ -554,8 +554,8 @@
     rows = dup.shape[1] // 16
     pairs = ((dattn, mixed), (normed, dup), (cot, hidden))
     for n, (a, _) in enumerate(pairs):
-        left_t[...] = a[...].T
-        by_arrival(order, left_t, left.at[n], rows)
+        left_t[n, :, :] = a[...].T
+        by_arrival(order, left_t.at[n], left.at[n], rows)
     stores = []
     for leaves in range(2):
         top = leaves * 8 * rows
@@ -821,17 +821,18 @@
         [
             pltpu.VMEM((2, width, 3 * cols), BF16),
             pltpu.VMEM((rows, width), BF16),
-            pltpu.VMEM((width, rows), BF16),
+            pltpu.VMEM((3, width, rows), BF16),
             pltpu.VMEM((3, width, rows), BF16),
             dma((19,)),
         ],
         6 * 10**9,
     )
     *parts, result = all_after((*parts, result), dcame)
-    far = []
+    far, far_sent = [], []
     for n, steps in enumerate(FAR_STEPS):
         pair = [parts[14 + n], sibling(parts[10 + n])]
         sent = call(pair_kernel, pair, [HELD] * 2, [(struct(steps * shard, 3 * cols), HELD)], [], 10**6)
+        far_sent += sent
         far.append(across(sent[0]))
     far_last = far.pop()
     far += [far_last[: 2 * shard], far_last[2 * shard :]]
@@ -889,7 +890,7 @@
     )
     parts = call(
         early_grads_kernel,
-        [order, normed, dproj],
+        [after(order, far_sent[2]), normed, dproj],
         [SMEM, HELD, ANY],
         [(struct(n * shard, 3 * cols), ANY) for n in STEPS + STEPS],
         [
@@ -904,18 +905,21 @@
     note = note + sibling(after(note, parts[1]))
     high = lax.reduce_precision(note, 8, 7)
     coded = jnp.concatenate([high, note - high, jnp.zeros((12, 3 * cols), F32)]).astype(BF16)
-    parts = all_after(parts, late_one, far[2])
+    parts = all_after(parts, late_one)
     late_two = late_sum.step(1)
     early_sum = Scatter(parts, note=coded)
     early_sum.step(0)
     late_three = late_sum.step(2)
-    dnormed = dnormed + across(dnormed_send).astype(F32)
+    early_sum.came = after(early_sum.came, late_two)
+    early_sum.step(1)
+    late_four = late_sum.step(3)
+    early_three = early_sum.step(2)
+    dnormed = dnormed + after(across(dnormed_send), early_three).astype(F32)
     resid = tokens.astype(F32)
     dresid_one, _ = norm_backward(resid, inverse_rms(resid), gain_attn, dnormed)
-    early_sum.step(1, late_two)
-    late_four = late_sum.step(3)
-    early_sum.step(2, late_three)
-    early_sum.step(3, late_four)
+    early_sum.came = after(early_sum.came, late_three, far[3])
+    early_sum.step(3)
+    late_sum.came = after(late_sum.came, early_sum.sent)
     dlate = late_sum.finish()
     din = early_sum.finish()
     mine = early_sum.notes

time: 229 us -> 222 us (0.969)
  starting transfers between devices: 47.4 us -> 43.1 us
    ppermute x16, waiting for transfers between devices: 47.5 us -> 41.7 us  [around(): return lax.ppermute(value, 'fsdp', AROUND)]
    ppermute x16, starting transfers between devices: 20.1 us -> 16.8 us  [around(): return lax.ppermute(value, 'fsdp', AROUND)]
    ppermute x14, waiting for transfers between devices: 44.7 us -> 47.9 us  [across(): return lax.ppermute(value, 'tp', ((0, 1), (1, 0)))]
    ppermute x14, starting transfers between devices: 17.7 us -> 15.4 us  [across(): return lax.ppermute(value, 'tp', ((0, 1), (1, 0)))]
  transfers between devices with their start and end apart: 63 -> 63, of which waited for: 27 -> 29; matrix products, arithmetic and copies ran while one was open for 7% -> 7% of each run, Pallas kernels for 19% -> 19%
where the time goes in v2:
time: 222 us; the launch traced here: 219 us
  waiting for transfers between devices  98.9 us (45%)
  Pallas kernels  55.9 us (25%)
  starting transfers between devices  43.1 us (19%)
  other arithmetic  10.3 us (5%)
  local copies, waits for them, and re-layouts  8.57 us (4%)
    pallas_call x19, Pallas kernels, call(): pl.pallas_call(body, out_shape=[place[id(space)](out.shape, out.dtype) fo...  55.9 us
    ppermute x14, waiting for transfers between devices, across(): return lax.ppermute(value, 'tp', ((0, 1), (1, 0)))  47.9 us
    ppermute x16, waiting for transfers between devices, around(): return lax.ppermute(value, 'fsdp', AROUND)  41.7 us
    ppermute x16, starting transfers between devices, around(): return lax.ppermute(value, 'fsdp', AROUND)  16.8 us
    ppermute x14, starting transfers between devices, across(): return lax.ppermute(value, 'tp', ((0, 1), (1, 0)))  15.4 us
    ppermute x33, starting transfers between devices, sibling(): return lax.ppermute(value, 'fsdp', CORES)  11 us
    ppermute x33, waiting for transfers between devices, sibling(): return lax.ppermute(value, 'fsdp', CORES)  9.28 us
  transfers between devices with their start and end apart: 63, of which 29 were waited for; matrix products, arithmetic and copies ran while one was open for 7% of the time, Pallas kernels for 19%

profile of v2, /device:TPU:0, one launch (start us, length us, event | category | flops | bytes accessed | tf_op | source)
XLA Modules:
  0.0 218.6 jit_solution(12809247125343953006)
XLA Ops:
  0.6 2.0 shard_map.203
  3.1 1.4 collective-permute-done.rest_1_
  4.9 2.6 %collective-permute-start.5 = (bf16[256,1280]{1,0:T(8,128)(2,1)}, bf16[256,1280]{1,0:T(8,128)(2,1)S(1)}, u32[]{:S(2)}, u32[]{:S(2)}) collective-permute-start(bf16[256,1280]{1,0:T(8,128)(2,1)} %tokens_in.1), channel_id=1, source_target_pairs={{0,1},{1,0},{2,3},{3,2},{4,5},{5,4},{6,7},{7,6},{8,9},{9,8},{10,11... | collective-permute-start | bytes 1966088 | tf_op jit(solution)/shard_map/ppermute | solution.py:265
  7.5 1.0 pad_maximum_fusion.1
  8.6 1.6 collective-permute-start.6
  10.3 1.6 collective-permute-start.2
  11.9 11.1 %collective-permute-done.5.other_in = bf16[256,1280]{1,0:T(8,128)(2,1)S(1)} collective-permute-done((bf16[256,1280]{1,0:T(8,128)(2,1)}, bf16[256,1280]{1,0:T(8,128)(2,1)S(1)}, u32[]{:S(2)}, u32[]{:S(2)}) %collective-permute-start.5) | collective-permute-done | bytes 655392 | tf_op jit(solution)/shard_map/ppermute | solution.py:265
  23.0 1.8 collective-permute-start.7
  25.4 1.6 collective-permute-start.3
  28.4 1.1 collective-permute-start.10
  29.5 7.6 %collective-permute-done.8.rest_10_ = bf16[80,1920]{1,0:T(8,128)(2,1)S(1)} collective-permute-done((bf16[80,1920]{1,0:T(8,128)(2,1)S(1)}, bf16[80,1920]{1,0:T(8,128)(2,1)S(1)}, u32[]{:S(2)}, u32[]{:S(2)}) %collective-permute-start.8) | collective-permute-done | bytes 307232 | tf_op jit(solution)/shard_map/ppermute | solution.py:265
  37.1 1.6 collective-permute-start.9
  38.7 1.3 collective-permute-done.3.rest_3_
  40.1 1.8 collective-permute-start.12
  41.9 1.8 fusion.2.normed
  43.7 3.9 %collective-permute-done.9.rest_4_ = bf16[160,1920]{1,0:T(8,128)(2,1)} collective-permute-done((bf16[160,1920]{1,0:T(8,128)(2,1)}, bf16[160,1920]{1,0:T(8,128)(2,1)}, u32[]{:S(2)}, u32[]{:S(2)}) %collective-permute-start.9) | collective-permute-done | bytes 614432 | tf_op jit(solution)/shard_map/ppermute | solution.py:261
  47.6 1.0 slice.92
  48.6 1.6 collective-permute-start.11
  51.2 2.8 %collective-permute-done.12.rest_4_ = bf16[160,1920]{1,0:T(8,128)(2,1)S(1)} collective-permute-done((bf16[160,1920]{1,0:T(8,128)(2,1)}, bf16[160,1920]{1,0:T(8,128)(2,1)S(1)}, u32[]{:S(2)}, u32[]{:S(2)}) %collective-permute-start.12) | collective-permute-done | bytes 614432 | tf_op jit(solution)/shard_map/ppermute | solution.py:261
  54.1 1.8 collective-permute-start.13
  55.9 1.6 collective-permute-done.11.rest_5_
  57.5 3.7 %collective-permute-done.13.rest_5_ = bf16[80,1920]{1,0:T(8,128)(2,1)S(1)} collective-permute-done((bf16[80,1920]{1,0:T(8,128)(2,1)S(1)}, bf16[80,1920]{1,0:T(8,128)(2,1)S(1)}, u32[]{:S(2)}, u32[]{:S(2)}) %collective-permute-start.13) | collective-permute-done | bytes 307232 | tf_op jit(solution)/shard_map/ppermute | solution.py:261
  61.5 3.2 %collective-permute-done.4.rest_13_ = bf16[160,1920]{1,0:T(8,128)(2,1)} collective-permute-done((bf16[160,1920]{1,0:T(8,128)(2,1)}, bf16[160,1920]{1,0:T(8,128)(2,1)}, u32[]{:S(2)}, u32[]{:S(2)}) %collective-permute-start.4) | collective-permute-done | bytes 614432 | tf_op jit(solution)/shard_map/ppermute | solution.py:265
  64.7 1.1 collective-permute-start.24
  66.8 10.9 %shard_map.204 = (bf16[640,256]{1,0:T(8,128)(2,1)S(1)}, bf16[640,256]{1,0:T(8,128)(2,1)S(1)}, f32[8,1,512]{2,1,0:T(1,128)S(1)}, bf16[1920,512]{1,0:T(8,128)(2,1)}, bf16[1280,1920]{1,0:T(8,128)(2,1)}) custom-call(s32[17]{0:T(128)S(1)} %stack.71.order, s32[1,8]{1,0:T(1,128)S(1)} %copy-done.24, f32[1,640]{1,0:T(1,128)S(1)} %broadcast_in_dim_tile.3.scaling, ...), custom_call_target="tpu_custom_call" | custom-call | flops 32000000000 | bytes 4194304 | tf_op jit(solution)/shard_map/pallas_call | solution.py:713
  77.7 3.5 %collective-permute-done.24.rest_14_ = bf16[160,1920]{1,0:T(8,128)(2,1)S(1)} collective-permute-done((bf16[160,1920]{1,0:T(8,128)(2,1)S(1)}, bf16[160,1920]{1,0:T(8,128)(2,1)S(1)}, u32[]{:S(2)}, u32[]{:S(2)}) %collective-permute-start.24) | collective-permute-done | bytes 614432 | tf_op jit(solution)/shard_map/ppermute | solution.py:265
  81.2 1.3 collective-permute-start.18
  82.7 1.9 collective-permute-done.25.rest_15_
  85.2 1.0 collective-permute-done.26.rest_16_
  86.8 4.7 %collective-permute-done.18.came = bf16[640,256]{1,0:T(8,128)(2,1)S(1)} collective-permute-done((bf16[640,256]{1,0:T(8,128)(2,1)S(1)}, bf16[640,256]{1,0:T(8,128)(2,1)S(1)}, u32[]{:S(2)}, u32[]{:S(2)}) %collective-permute-start.18) | collective-permute-done | bytes 327712 | tf_op jit(solution)/shard_map/ppermute | solution.py:265
  92.1 2.5 %collective-permute-done.21.rest_8_ = bf16[160,1920]{1,0:T(8,128)(2,1)S(1)} collective-permute-done((bf16[160,1920]{1,0:T(8,128)(2,1)}, bf16[160,1920]{1,0:T(8,128)(2,1)S(1)}, u32[]{:S(2)}, u32[]{:S(2)}) %collective-permute-start.21) | collective-permute-done | bytes 614432 | tf_op jit(solution)/shard_map/ppermute | solution.py:257
  94.6 3.4 %shard_map.205.weights = bf16[2,1280,1920]{2,1,0:T(8,128)(2,1)S(1)} custom-call(s32[17]{0:T(128)S(1)} %stack.71.order, bf16[80,1920]{1,0:T(8,128)(2,1)} %get-tuple-element.124.rest_0_, bf16[80,1920]{1,0:T(8,128)(2,1)} %copy-done.34, bf16[160,1920]{1,0:T(8,128)(2,1)S(1)} %collective-permute-done.2.rest_2_, bf16[160,1920]{1,0:T(8,128)(2,1)} %collective-permute-done.3.rest_3_, ...), custom_call_target="tpu_custom_call" | custom-call | flops 4000000 | bytes 4194304 | tf_op jit(solution)/shard_map/pallas_call | solution.py:713
  98.0 8.5 %shard_map.206 = (bf16[640,256]{1,0:T(8,128)(2,1)S(1)}, bf16[640,256]{1,0:T(8,128)(2,1)S(1)}, bf16[256,1280]{1,0:T(8,128)(2,1)S(1)}, bf16[256,1280]{1,0:T(8,128)...) custom-call(bf16[256,1280]{1,0:T(8,128)(2,1)S(1)} %copy-done, ...), custom_call_target="tpu_custom_call" | custom-call | flops 32000000000 | bytes 4194304 | tf_op jit(solution)/shard_map/pallas_call | solution.py:713
  106.5 1.3 collective-permute-start.30
  107.8 6.5 %shard_map.207 = (bf16[80,1920]{1,0:T(8,128)(2,1)}, bf16[160,1920]{1,0:T(8,128)(2,1)}, bf16[160,1920]{1,0:T(8,128)(2,1)}, bf16[160,1920]{1,0:T(8,128)(2,1)}, bf1...) custom-call(s32[17]{0:T(128)S(1)} %stack.71.order, ...), custom_call_target="tpu_custom_call" | custom-call | flops 24000000000 | bytes 4194304 | tf_op jit(solution)/shard_map/pallas_call | solution.py:713
  114.3 2.0 collective-permute-done.30.came
  118.3 1.8 collective-permute-done.32.other
  121.2 1.3 collective-permute-start.33
  123.6 12.5 %shard_map.208 = (f32[80,1]{1,0:T(8,128)S(1)}, f32[1,1280]{1,0:T(1,128)S(1)}, bf16[512,1920]{1,0:T(8,128)(2,1)}, f32[256,1280]{1,0:T(8,128)}, bf16[256,1280]{1,0:T(8,128)(2,1)}) custom-call(s32[17]{0:T(128)S(1)} %stack.71.order, s32[1,8]{1,0:T(1,128)S(1)} %copy-done.25, f32[80,1]{1,0:T(8,128)S(1)} %copy.24.scaling_col, bf16[640,256]{1,0:T(8,128)(2,1)S(1)} %copy-done.27, ...), custom_call_target="tpu_custom_call" | custom-call | flops 48000000000 | bytes 4194304 | tf_op jit(solution)/shard_map/pallas_call | solution.py:713
  136.7 1.1 shard_map.213
  137.8 1.5 collective-permute-start.38
  139.5 4.3 %collective-permute-done.35.rest_2_ = bf16[160,1920]{1,0:T(8,128)(2,1)S(1)} collective-permute-done((bf16[160,1920]{1,0:T(8,128)(2,1)S(1)}, bf16[160,1920]{1,0:T(8,128)(2,1)S(1)}, u32[]{:S(2)}, u32[]{:S(2)}) %collective-permute-start.35) | collective-permute-done | bytes 614432 | tf_op jit(solution)/shard_map/ppermute | solution.py:265
  144.6 6.9 %shard_map.212 = (bf16[80,1920]{1,0:T(8,128)(2,1)}, bf16[160,1920]{1,0:T(8,128)(2,1)}, bf16[160,1920]{1,0:T(8,128)(2,1)}, bf16[160,1920]{1,0:T(8,128)(2,1)}, bf1...) custom-call(s32[17]{0:T(128)S(1)} %stack.71.order, ...), custom_call_target="tpu_custom_call" | custom-call | flops 20000000000 | bytes 4194304 | tf_op jit(solution)/shard_map/pallas_call | solution.py:713
  152.5 1.3 collective-permute-start.50
  153.8 1.4 shard_map.215
  155.2 1.2 collective-permute-start.45
  156.4 2.6 %collective-permute-start.41 = (bf16[80,1920]{1,0:T(8,128)(2,1)S(1)}, bf16[80,1920]{1,0:T(8,128)(2,1)S(1)}, u32[]{:S(2)}, u32[]{:S(2)}) collective-permute-start(bf16[80,1920]{1,0:T(8,128)(2,1)S(1)} %copy-done.48), channel_id=1, source_target_pairs={{0,2},{2,0},{4,6},{6,4},{8,10},{10,8},{12,14},{14,12},{16,18},{18,... | collective-permute-start | bytes 921608 | tf_op jit(solution)/shard_map/ppermute | solution.py:257
  159.1 1.2 collective-permute-done.41.came
  161.2 6.1 %collective-permute-done.45.rest_3_ = bf16[160,1920]{1,0:T(8,128)(2,1)S(1)} collective-permute-done((bf16[160,1920]{1,0:T(8,128)(2,1)S(1)}, bf16[160,1920]{1,0:T(8,128)(2,1)S(1)}, u32[]{:S(2)}, u32[]{:S(2)}) %collective-permute-start.45) | collective-permute-done | bytes 614432 | tf_op jit(solution)/shard_map/ppermute | solution.py:261
  167.6 3.7 %collective-permute-done.43.rest_2_ = bf16[96,1920]{1,0:T(8,128)(2,1)S(1)} collective-permute-done((bf16[96,1920]{1,0:T(8,128)(2,1)S(1)}, bf16[96,1920]{1,0:T(8,128)(2,1)S(1)}, u32[]{:S(2)}, u32[]{:S(2)}) %collective-permute-start.43) | collective-permute-done | bytes 368672 | tf_op jit(solution)/shard_map/ppermute | solution.py:261
  171.5 1.0 collective-permute-start.39
  174.2 8.1 %collective-permute-done.46.rest_2_ = bf16[176,1920]{1,0:T(8,128)(2,1)S(1)} collective-permute-done((bf16[176,1920]{1,0:T(8,128)(2,1)S(1)}, bf16[176,1920]{1,0:T(8,128)(2,1)S(1)}, u32[]{:S(2)}, u32[]{:S(2)}) %collective-permute-start.46) | collective-permute-done | bytes 675872 | tf_op jit(solution)/shard_map/ppermute | solution.py:261
  183.0 7.7 %collective-permute-done.53 = bf16[240,1920]{1,0:T(8,128)(2,1)S(1)} collective-permute-done((bf16[240,1920]{1,0:T(8,128)(2,1)S(1)}, bf16[240,1920]{1,0:T(8,128)(2,1)S(1)}, u32[]{:S(2)}, u32[]{:S(2)}) %collective-permute-start.53) | collective-permute-done | bytes 921632 | tf_op jit(solution)/shard_map/ppermute | solution.py:265
  190.8 1.1 shard_map.221
  191.9 2.2 %collective-permute-start.59 = (bf16[80,1920]{1,0:T(8,128)(2,1)}, bf16[80,1920]{1,0:T(8,128)(2,1)S(1)}, u32[]{:S(2)}, u32[]{:S(2)}) collective-permute-start(bf16[80,1920]{1,0:T(8,128)(2,1)} %get-tuple-element.223), channel_id=1, source_target_pairs={{0,2},{2,0},{4,6},{6,4},{8,10},{10,8},{12,14},{14,12},{16,18},{18,... | collective-permute-start | bytes 921608 | tf_op jit(solution)/shard_map/ppermute | solution.py:257
  194.1 2.0 collective-permute-done.47.rest_2_
  196.4 6.4 %collective-permute-done.61 = bf16[160,1920]{1,0:T(8,128)(2,1)} collective-permute-done((bf16[160,1920]{1,0:T(8,128)(2,1)}, bf16[160,1920]{1,0:T(8,128)(2,1)}, u32[]{:S(2)}, u32[]{:S(2)}) %collective-permute-start.61) | collective-permute-done | bytes 614432 | tf_op jit(solution)/shard_map/ppermute | solution.py:261
  202.8 1.0 slice.87
  203.9 1.6 fusion.3
  205.6 2.7 %fusion.6 = f32[256,1280]{1,0:T(8,128)} fusion(f32[256,1280]{1,0:T(8,128)S(1)} %copy-done.32, bf16[256,1280]{1,0:T(8,128)(2,1)S(1)} %copy-done.1, f32[256,1280]{1,0:T(8,128)S(1)} %copy-done.30, bf16[256,1280]{1,0:T(8,128)(2,1)} %collective-permute-done.36, f32[256]{0:T(256)S(1)} %broadcast_multiply_fusion, f32[256]{0:T(256)S(1)} %get-tuple-element.240, ...), kind=kLoop, calls=%fused_computation.11 | loop fusion | flops 2949120 | bytes 5251072 | tf_op jit(solution)/shard_map/add | solution.py:934
  208.3 1.7 collective-permute-done.54
  210.9 1.3 convert_add_fusion
  212.3 1.0 collective-permute-start.56
  214.4 1.7 collective-permute-done.56
  (222 shorter events, 22.0 us)
Async XLA Ops:
  2.6 1.9 collective-permute-start
  4.5 5.7 %collective-permute-start.1 = (bf16[80,1920]{1,0:T(8,128)(2,1)}, bf16[80,1920]{1,0:T(8,128)(2,1)S(1)}, u32[]{:S(2)}, u32[]{:S(2)}) collective-permute-start(bf16[80,1920]{1,0:T(8,128)(2,1)} %get-tuple-element.124.rest_0_), channel_id=1, source_target_pairs={{0,2},{2,0},{4,6},{6,4},{8,10},{10,8},{12,14},{14,12},{16,18},{18,... | collective-permute-start | bytes 921608 | tf_op jit(solution)/shard_map/ppermute | solution.py:257
  4.9 18.1 %collective-permute-start.5 = (bf16[256,1280]{1,0:T(8,128)(2,1)}, bf16[256,1280]{1,0:T(8,128)(2,1)S(1)}, u32[]{:S(2)}, u32[]{:S(2)}) collective-permute-start(bf16[256,1280]{1,0:T(8,128)(2,1)} %tokens_in.1), channel_id=1, source_target_pairs={{0,1},{1,0},{2,3},{3,2},{4,5},{5,4},{6,7},{7,6},{8,9},{9,8},{10,11... | collective-permute-start | bytes 1966088 | tf_op jit(solution)/shard_map/ppermute | solution.py:265
  8.6 33.3 %copy-start.42 = (f32[1280]{0:T(1024)S(1)}, f32[1280]{0:T(1024)}, u32[]{:S(2)}) copy-start(f32[1280]{0:T(1024)} %param.14) | copy-start | bytes 15364
  8.6 14.4 %collective-permute-start.6 = (bf16[160,1920]{1,0:T(8,128)(2,1)S(1)}, bf16[160,1920]{1,0:T(8,128)(2,1)}, u32[]{:S(2)}, u32[]{:S(2)}) collective-permute-start(bf16[160,1920]{1,0:T(8,128)(2,1)S(1)} %pad_maximum_fusion.1), channel_id=1, source_target_pairs={{0,8},{8,16},{16,24},{24,28},{28,20},{20,12},{12,4},{4,0},{2,6},{1... | collective-permute-start | bytes 1843208 | tf_op jit(solution)/shard_map/ppermute | solution.py:261
  10.3 15.1 %collective-permute-start.2 = (bf16[160,1920]{1,0:T(8,128)(2,1)S(1)}, bf16[160,1920]{1,0:T(8,128)(2,1)S(1)}, u32[]{:S(2)}, u32[]{:S(2)}) collective-permute-start(bf16[160,1920]{1,0:T(8,128)(2,1)S(1)} %pad_maximum_fusion), channel_id=1, source_target_pairs={{0,8},{8,16},{16,24},{24,28},{28,20},{20,12},{12,4},{4,0},{2,6},{1... | collective-permute-start | bytes 1843208 | tf_op jit(solution)/shard_map/ppermute | solution.py:261
  23.0 14.1 %collective-permute-start.7 = (bf16[160,1920]{1,0:T(8,128)(2,1)}, bf16[160,1920]{1,0:T(8,128)(2,1)}, u32[]{:S(2)}, u32[]{:S(2)}) collective-permute-start(bf16[160,1920]{1,0:T(8,128)(2,1)} %collective-permute-done.6.rest_2_), channel_id=1, source_target_pairs={{0,8},{8,16},{16,24},{24,28},{28,20},{20,12},{12,4},{4,0},{2,6},{1... | collective-permute-start | bytes 1843208 | tf_op jit(solution)/shard_map/ppermute | solution.py:261
  25.4 14.7 %collective-permute-start.3 = (bf16[160,1920]{1,0:T(8,128)(2,1)S(1)}, bf16[160,1920]{1,0:T(8,128)(2,1)}, u32[]{:S(2)}, u32[]{:S(2)}) collective-permute-start(bf16[160,1920]{1,0:T(8,128)(2,1)S(1)} %collective-permute-done.2.rest_2_), channel_id=1, source_target_pairs={{0,8},{8,16},{16,24},{24,28},{28,20},{20,12},{12,4},{4,0},{2,6},{1... | collective-permute-start | bytes 1843208 | tf_op jit(solution)/shard_map/ppermute | solution.py:261
  26.9 10.2 %collective-permute-start.8 = (bf16[80,1920]{1,0:T(8,128)(2,1)S(1)}, bf16[80,1920]{1,0:T(8,128)(2,1)S(1)}, u32[]{:S(2)}, u32[]{:S(2)}) collective-permute-start(bf16[80,1920]{1,0:T(8,128)(2,1)S(1)} %copy-done.33), channel_id=1, source_target_pairs={{0,1},{1,0},{2,3},{3,2},{4,5},{5,4},{6,7},{7,6},{8,9},{9,8},{10,11... | collective-permute-start | bytes 921608 | tf_op jit(solution)/shard_map/ppermute | solution.py:265
  28.4 20.2 %collective-permute-start.10 = (bf16[160,1920]{1,0:T(8,128)(2,1)S(1)}, bf16[160,1920]{1,0:T(8,128)(2,1)S(1)}, u32[]{:S(2)}, u32[]{:S(2)}) collective-permute-start(bf16[160,1920]{1,0:T(8,128)(2,1)S(1)} %collective-permute-done.2.rest_2_), channel_id=1, source_target_pairs={{0,1},{1,0},{2,3},{3,2},{4,5},{5,4},{6,7},{7,6},{8,9},{9,8},{10,11... | collective-permute-start | bytes 1843208 | tf_op jit(solution)/shard_map/ppermute | solution.py:265
  37.1 10.5 %collective-permute-start.9 = (bf16[160,1920]{1,0:T(8,128)(2,1)}, bf16[160,1920]{1,0:T(8,128)(2,1)}, u32[]{:S(2)}, u32[]{:S(2)}) collective-permute-start(bf16[160,1920]{1,0:T(8,128)(2,1)} %collective-permute-done.7.rest_3_), channel_id=1, source_target_pairs={{0,8},{8,16},{16,24},{24,28},{28,20},{20,12},{12,4},{4,0},{2,6},{1... | collective-permute-start | bytes 1843208 | tf_op jit(solution)/shard_map/ppermute | solution.py:261
  40.1 14.0 %collective-permute-start.12 = (bf16[160,1920]{1,0:T(8,128)(2,1)}, bf16[160,1920]{1,0:T(8,128)(2,1)S(1)}, u32[]{:S(2)}, u32[]{:S(2)}) collective-permute-start(bf16[160,1920]{1,0:T(8,128)(2,1)} %collective-permute-done.3.rest_3_), channel_id=1, source_target_pairs={{0,8},{8,16},{16,24},{24,28},{28,20},{20,12},{12,4},{4,0},{2,6},{1... | collective-permute-start | bytes 1843208 | tf_op jit(solution)/shard_map/ppermute | solution.py:261
  48.6 8.9 %collective-permute-start.11 = (bf16[80,1920]{1,0:T(8,128)(2,1)S(1)}, bf16[80,1920]{1,0:T(8,128)(2,1)}, u32[]{:S(2)}, u32[]{:S(2)}) collective-permute-start(bf16[80,1920]{1,0:T(8,128)(2,1)S(1)} %slice.92), channel_id=1, source_target_pairs={{0,8},{8,16},{16,24},{24,28},{28,20},{20,12},{12,4},{4,0},{2,6},{1... | collective-permute-start | bytes 921608 | tf_op jit(solution)/shard_map/ppermute | solution.py:261
  50.3 14.4 %collective-permute-start.4 = (bf16[160,1920]{1,0:T(8,128)(2,1)}, bf16[160,1920]{1,0:T(8,128)(2,1)}, u32[]{:S(2)}, u32[]{:S(2)}) collective-permute-start(bf16[160,1920]{1,0:T(8,128)(2,1)} %collective-permute-done.3.rest_3_), channel_id=1, source_target_pairs={{0,1},{1,0},{2,3},{3,2},{4,5},{5,4},{6,7},{7,6},{8,9},{9,8},{10,11... | collective-permute-start | bytes 1843208 | tf_op jit(solution)/shard_map/ppermute | solution.py:265
  51.2 14.6 %collective-permute-start.15 = (bf16[160,1920]{1,0:T(8,128)(2,1)}, bf16[160,1920]{1,0:T(8,128)(2,1)}, u32[]{:S(2)}, u32[]{:S(2)}) collective-permute-start(bf16[160,1920]{1,0:T(8,128)(2,1)} %collective-permute-done.6.rest_2_), channel_id=1, source_target_pairs={{0,2},{2,0},{4,6},{6,4},{8,10},{10,8},{12,14},{14,12},{16,18},{18,... | collective-permute-start | bytes 1843208 | tf_op jit(solution)/shard_map/ppermute | solution.py:257
  54.1 7.1 %collective-permute-start.13 = (bf16[80,1920]{1,0:T(8,128)(2,1)S(1)}, bf16[80,1920]{1,0:T(8,128)(2,1)S(1)}, u32[]{:S(2)}, u32[]{:S(2)}) collective-permute-start(bf16[80,1920]{1,0:T(8,128)(2,1)S(1)} %slice.93), channel_id=1, source_target_pairs={{0,8},{8,16},{16,24},{24,28},{28,20},{20,12},{12,4},{4,0},{2,6},{1... | collective-permute-start | bytes 921608 | tf_op jit(solution)/shard_map/ppermute | solution.py:261
  55.9 10.8 %collective-permute-start.16 = (bf16[160,1920]{1,0:T(8,128)(2,1)}, bf16[160,1920]{1,0:T(8,128)(2,1)}, u32[]{:S(2)}, u32[]{:S(2)}) collective-permute-start(bf16[160,1920]{1,0:T(8,128)(2,1)} %collective-permute-done.7.rest_3_), channel_id=1, source_target_pairs={{0,2},{2,0},{4,6},{6,4},{8,10},{10,8},{12,14},{14,12},{16,18},{18,... | collective-permute-start | bytes 1843208 | tf_op jit(solution)/shard_map/ppermute | solution.py:257
  57.5 9.3 %collective-permute-start.17 = (bf16[160,1920]{1,0:T(8,128)(2,1)}, bf16[160,1920]{1,0:T(8,128)(2,1)}, u32[]{:S(2)}, u32[]{:S(2)}) collective-permute-start(bf16[160,1920]{1,0:T(8,128)(2,1)} %collective-permute-done.9.rest_4_), channel_id=1, source_target_pairs={{0,2},{2,0},{4,6},{6,4},{8,10},{10,8},{12,14},{14,12},{16,18},{18,... | collective-permute-start | bytes 1843208 | tf_op jit(solution)/shard_map/ppermute | solution.py:257
  61.2 5.5 %collective-permute-start.14 = (bf16[80,1920]{1,0:T(8,128)(2,1)}, bf16[80,1920]{1,0:T(8,128)(2,1)}, u32[]{:S(2)}, u32[]{:S(2)}) collective-permute-start(bf16[80,1920]{1,0:T(8,128)(2,1)} %collective-permute-done.11.rest_5_), channel_id=1, source_target_pairs={{0,2},{2,0},{4,6},{6,4},{8,10},{10,8},{12,14},{14,12},{16,18},{18,... | collective-permute-start | bytes 921608 | tf_op jit(solution)/shard_map/ppermute | solution.py:257
  64.7 16.5 %collective-permute-start.24 = (bf16[160,1920]{1,0:T(8,128)(2,1)S(1)}, bf16[160,1920]{1,0:T(8,128)(2,1)S(1)}, u32[]{:S(2)}, u32[]{:S(2)}) collective-permute-start(bf16[160,1920]{1,0:T(8,128)(2,1)S(1)} %collective-permute-done.12.rest_4_), channel_id=1, source_target_pairs={{0,1},{1,0},{2,3},{3,2},{4,5},{5,4},{6,7},{7,6},{8,9},{9,8},{10,11... | collective-permute-start | bytes 1843208 | tf_op jit(solution)/shard_map/ppermute | solution.py:265
  65.8 18.8 %collective-permute-start.25 = (bf16[80,1920]{1,0:T(8,128)(2,1)S(1)}, bf16[80,1920]{1,0:T(8,128)(2,1)S(1)}, u32[]{:S(2)}, u32[]{:S(2)}) collective-permute-start(bf16[80,1920]{1,0:T(8,128)(2,1)S(1)} %collective-permute-done.13.rest_5_), channel_id=1, source_target_pairs={{0,1},{1,0},{2,3},{3,2},{4,5},{5,4},{6,7},{7,6},{8,9},{9,8},{10,11... | collective-permute-start | bytes 921608 | tf_op jit(solution)/shard_map/ppermute | solution.py:265
  81.2 10.3 %collective-permute-start.29 = (bf16[160,1920]{1,0:T(8,128)(2,1)S(1)}, bf16[160,1920]{1,0:T(8,128)(2,1)S(1)}, u32[]{:S(2)}, u32[]{:S(2)}) collective-permute-start(bf16[160,1920]{1,0:T(8,128)(2,1)S(1)} %collective-permute-done.24.rest_14_), channel_id=1, source_target_pairs={{0,2},{2,0},{4,6},{6,4},{8,10},{10,8},{12,14},{14,12},{16,18},{18,... | collective-permute-start | bytes 1843208 | tf_op jit(solution)/shard_map/ppermute | solution.py:257
  81.2 10.3 %collective-permute-start.18 = (bf16[640,256]{1,0:T(8,128)(2,1)S(1)}, bf16[640,256]{1,0:T(8,128)(2,1)S(1)}, u32[]{:S(2)}, u32[]{:S(2)}) collective-permute-start(bf16[640,256]{1,0:T(8,128)(2,1)S(1)} %get-tuple-element.129), channel_id=1, source_target_pairs={{0,1},{1,0},{2,3},{3,2},{4,5},{5,4},{6,7},{7,6},{8,9},{9,8},{10,11... | collective-permute-start | bytes 983048 | tf_op jit(solution)/shard_map/ppermute | solution.py:265
  82.5 2.7 %collective-permute-start.23 = (bf16[80,1920]{1,0:T(8,128)(2,1)S(1)}, bf16[80,1920]{1,0:T(8,128)(2,1)S(1)}, u32[]{:S(2)}, u32[]{:S(2)}) collective-permute-start(bf16[80,1920]{1,0:T(8,128)(2,1)S(1)} %copy-done.37), channel_id=1, source_target_pairs={{0,2},{2,0},{4,6},{6,4},{8,10},{10,8},{12,14},{14,12},{16,18},{18,... | collective-permute-start | bytes 921608 | tf_op jit(solution)/shard_map/ppermute | solution.py:257
  84.6 1.6 collective-permute-start.26
  84.6 2.0 collective-permute-start.19
  85.1 6.9 %collective-permute-start.28 = (bf16[160,1920]{1,0:T(8,128)(2,1)}, bf16[160,1920]{1,0:T(8,128)(2,1)S(1)}, u32[]{:S(2)}, u32[]{:S(2)}) collective-permute-start(bf16[160,1920]{1,0:T(8,128)(2,1)} %collective-permute-done.4.rest_13_), channel_id=1, source_target_pairs={{0,2},{2,0},{4,6},{6,4},{8,10},{10,8},{12,14},{14,12},{16,18},{18,... | collective-permute-start | bytes 1843208 | tf_op jit(solution)/shard_map/ppermute | solution.py:257
  86.2 5.8 %collective-permute-start.27 = (bf16[160,1920]{1,0:T(8,128)(2,1)S(1)}, bf16[160,1920]{1,0:T(8,128)(2,1)S(1)}, u32[]{:S(2)}, u32[]{:S(2)}) collective-permute-start(bf16[160,1920]{1,0:T(8,128)(2,1)S(1)} %copy-done.14), channel_id=1, source_target_pairs={{0,2},{2,0},{4,6},{6,4},{8,10},{10,8},{12,14},{14,12},{16,18},{18,... | collective-permute-start | bytes 1843208 | tf_op jit(solution)/shard_map/ppermute | solution.py:257
  86.7 5.4 %collective-permute-start.22 = (bf16[160,1920]{1,0:T(8,128)(2,1)S(1)}, bf16[160,1920]{1,0:T(8,128)(2,1)S(1)}, u32[]{:S(2)}, u32[]{:S(2)}) collective-permute-start(bf16[160,1920]{1,0:T(8,128)(2,1)S(1)} %collective-permute-done.12.rest_4_), channel_id=1, source_target_pairs={{0,2},{2,0},{4,6},{6,4},{8,10},{10,8},{12,14},{14,12},{16,18},{18,... | collective-permute-start | bytes 1843208 | tf_op jit(solution)/shard_map/ppermute | solution.py:257
  91.5 3.0 %collective-permute-start.21 = (bf16[160,1920]{1,0:T(8,128)(2,1)}, bf16[160,1920]{1,0:T(8,128)(2,1)S(1)}, u32[]{:S(2)}, u32[]{:S(2)}) collective-permute-start(bf16[160,1920]{1,0:T(8,128)(2,1)} %collective-permute-done.3.rest_3_), channel_id=1, source_target_pairs={{0,2},{2,0},{4,6},{6,4},{8,10},{10,8},{12,14},{14,12},{16,18},{18,... | collective-permute-start | bytes 1843208 | tf_op jit(solution)/shard_map/ppermute | solution.py:257
  91.5 3.0 %collective-permute-start.20 = (bf16[160,1920]{1,0:T(8,128)(2,1)S(1)}, bf16[160,1920]{1,0:T(8,128)(2,1)S(1)}, u32[]{:S(2)}, u32[]{:S(2)}) collective-permute-start(bf16[160,1920]{1,0:T(8,128)(2,1)S(1)} %collective-permute-done.2.rest_2_), channel_id=1, source_target_pairs={{0,2},{2,0},{4,6},{6,4},{8,10},{10,8},{12,14},{14,12},{16,18},{18,... | collective-permute-start | bytes 1843208 | tf_op jit(solution)/shard_map/ppermute | solution.py:257
  106.5 9.8 %collective-permute-start.30 = (bf16[640,256]{1,0:T(8,128)(2,1)S(1)}, bf16[640,256]{1,0:T(8,128)(2,1)S(1)}, u32[]{:S(2)}, u32[]{:S(2)}) collective-permute-start(bf16[640,256]{1,0:T(8,128)(2,1)S(1)} %get-tuple-element.165), channel_id=1, source_target_pairs={{0,1},{1,0},{2,3},{3,2},{4,5},{5,4},{6,7},{7,6},{8,9},{9,8},{10,11... | collective-permute-start | bytes 983048 | tf_op jit(solution)/shard_map/ppermute | solution.py:265
  117.0 5.5 %collective-permute-start.34 = (bf16[160,1920]{1,0:T(8,128)(2,1)}, bf16[160,1920]{1,0:T(8,128)(2,1)S(1)}, u32[]{:S(2)}, u32[]{:S(2)}) collective-permute-start(bf16[160,1920]{1,0:T(8,128)(2,1)} %get-tuple-element.181), channel_id=1, source_target_pairs={{0,2},{2,0},{4,6},{6,4},{8,10},{10,8},{12,14},{14,12},{16,18},{18,... | collective-permute-start | bytes 1843208 | tf_op jit(solution)/shard_map/ppermute | solution.py:257
  117.0 3.1 %collective-permute-start.32 = (bf16[80,1920]{1,0:T(8,128)(2,1)}, bf16[80,1920]{1,0:T(8,128)(2,1)S(1)}, u32[]{:S(2)}, u32[]{:S(2)}) collective-permute-start(bf16[80,1920]{1,0:T(8,128)(2,1)} %get-tuple-element.179), channel_id=1, source_target_pairs={{0,2},{2,0},{4,6},{6,4},{8,10},{10,8},{12,14},{14,12},{16,18},{18,... | collective-permute-start | bytes 921608 | tf_op jit(solution)/shard_map/ppermute | solution.py:257
  117.6 5.0 %collective-permute-start.31 = (bf16[80,1920]{1,0:T(8,128)(2,1)}, bf16[80,1920]{1,0:T(8,128)(2,1)}, u32[]{:S(2)}, u32[]{:S(2)}) collective-permute-start(bf16[80,1920]{1,0:T(8,128)(2,1)} %get-tuple-element.168), channel_id=1, source_target_pairs={{0,2},{2,0},{4,6},{6,4},{8,10},{10,8},{12,14},{14,12},{16,18},{18,... | collective-permute-start | bytes 921608 | tf_op jit(solution)/shard_map/ppermute | solution.py:257
  117.7 34.8 %collective-permute-start.44 = (bf16[160,1920]{1,0:T(8,128)(2,1)}, bf16[160,1920]{1,0:T(8,128)(2,1)}, u32[]{:S(2)}, u32[]{:S(2)}) collective-permute-start(bf16[160,1920]{1,0:T(8,128)(2,1)} %get-tuple-element.210), channel_id=1, source_target_pairs={{0,2},{2,0},{4,6},{6,4},{8,10},{10,8},{12,14},{14,12},{16,18},{18,... | collective-permute-start | bytes 1843208 | tf_op jit(solution)/shard_map/ppermute | solution.py:257
  118.3 21.1 %collective-permute-start.37 = (bf16[160,1920]{1,0:T(8,128)(2,1)}, bf16[160,1920]{1,0:T(8,128)(2,1)S(1)}, u32[]{:S(2)}, u32[]{:S(2)}) collective-permute-start(bf16[160,1920]{1,0:T(8,128)(2,1)} %get-tuple-element.185), channel_id=1, source_target_pairs={{0,2},{2,0},{4,6},{6,4},{8,10},{10,8},{12,14},{14,12},{16,18},{18,... | collective-permute-start | bytes 1843208 | tf_op jit(solution)/shard_map/ppermute | solution.py:257
  121.2 15.4 %collective-permute-start.33 = (bf16[80,1920]{1,0:T(8,128)(2,1)S(1)}, bf16[80,1920]{1,0:T(8,128)(2,1)S(1)}, u32[]{:S(2)}, u32[]{:S(2)}) collective-permute-start(bf16[80,1920]{1,0:T(8,128)(2,1)S(1)} %shard_map.209), channel_id=1, source_target_pairs={{0,1},{1,0},{2,3},{3,2},{4,5},{5,4},{6,7},{7,6},{8,9},{9,8},{10,11... | collective-permute-start | bytes 921608 | tf_op jit(solution)/shard_map/ppermute | solution.py:265
  122.7 21.1 %collective-permute-start.35 = (bf16[160,1920]{1,0:T(8,128)(2,1)S(1)}, bf16[160,1920]{1,0:T(8,128)(2,1)S(1)}, u32[]{:S(2)}, u32[]{:S(2)}) collective-permute-start(bf16[160,1920]{1,0:T(8,128)(2,1)S(1)} %shard_map.210), channel_id=1, source_target_pairs={{0,1},{1,0},{2,3},{3,2},{4,5},{5,4},{6,7},{7,6},{8,9},{9,8},{10,11... | collective-permute-start | bytes 1843208 | tf_op jit(solution)/shard_map/ppermute | solution.py:265
  137.8 15.9 %collective-permute-start.38 = (bf16[80,1920]{1,0:T(8,128)(2,1)S(1)}, bf16[80,1920]{1,0:T(8,128)(2,1)}, u32[]{:S(2)}, u32[]{:S(2)}) collective-permute-start(bf16[80,1920]{1,0:T(8,128)(2,1)S(1)} %shard_map.213), channel_id=1, source_target_pairs={{0,8},{8,16},{16,24},{24,28},{28,20},{20,12},{12,4},{4,0},{2,6},{1... | collective-permute-start | bytes 921608 | tf_op jit(solution)/shard_map/ppermute | solution.py:261
  151.7 4.7 %collective-permute-start.42 = (f32[2,1920]{1,0:T(2,128)S(1)}, f32[2,1920]{1,0:T(2,128)S(1)}, u32[]{:S(2)}, u32[]{:S(2)}) collective-permute-start(f32[2,1920]{1,0:T(2,128)S(1)} %fusion.10), channel_id=1, source_target_pairs={{0,2},{2,0},{4,6},{6,4},{8,10},{10,8},{12,14},{14,12},{16,18},{18,... | collective-permute-start | bytes 46088 | tf_op jit(solution)/shard_map/ppermute | solution.py:257
  151.9 9.0 %collective-permute-start.52 = (bf16[240,1920]{1,0:T(8,128)(2,1)}, bf16[240,1920]{1,0:T(8,128)(2,1)S(1)}, u32[]{:S(2)}, u32[]{:S(2)}) collective-permute-start(bf16[240,1920]{1,0:T(8,128)(2,1)} %get-tuple-element.218), channel_id=1, source_target_pairs={{0,2},{2,0},{4,6},{6,4},{8,10},{10,8},{12,14},{14,12},{16,18},{18,... | collective-permute-start | bytes 2764808 | tf_op jit(solution)/shard_map/ppermute | solution.py:257
  152.4 20.1 %collective-permute-start.49 = (bf16[160,1920]{1,0:T(8,128)(2,1)}, bf16[160,1920]{1,0:T(8,128)(2,1)S(1)}, u32[]{:S(2)}, u32[]{:S(2)}) collective-permute-start(bf16[160,1920]{1,0:T(8,128)(2,1)} %get-tuple-element.216), channel_id=1, source_target_pairs={{0,2},{2,0},{4,6},{6,4},{8,10},{10,8},{12,14},{14,12},{16,18},{18,... | collective-permute-start | bytes 1843208 | tf_op jit(solution)/shard_map/ppermute | solution.py:257
  152.5 20.1 %collective-permute-start.50 = (bf16[160,1920]{1,0:T(8,128)(2,1)S(1)}, bf16[160,1920]{1,0:T(8,128)(2,1)S(1)}, u32[]{:S(2)}, u32[]{:S(2)}) collective-permute-start(bf16[160,1920]{1,0:T(8,128)(2,1)S(1)} %shard_map.211), channel_id=1, source_target_pairs={{0,1},{1,0},{2,3},{3,2},{4,5},{5,4},{6,7},{7,6},{8,9},{9,8},{10,11... | collective-permute-start | bytes 1843208 | tf_op jit(solution)/shard_map/ppermute | solution.py:265
  155.2 12.1 %collective-permute-start.45 = (bf16[160,1920]{1,0:T(8,128)(2,1)S(1)}, bf16[160,1920]{1,0:T(8,128)(2,1)S(1)}, u32[]{:S(2)}, u32[]{:S(2)}) collective-permute-start(bf16[160,1920]{1,0:T(8,128)(2,1)S(1)} %shard_map.215), channel_id=1, source_target_pairs={{0,8},{8,16},{16,24},{24,28},{28,20},{20,12},{12,4},{4,0},{2,6},{1... | collective-permute-start | bytes 1843208 | tf_op jit(solution)/shard_map/ppermute | solution.py:261
  156.4 3.8 %collective-permute-start.41 = (bf16[80,1920]{1,0:T(8,128)(2,1)S(1)}, bf16[80,1920]{1,0:T(8,128)(2,1)S(1)}, u32[]{:S(2)}, u32[]{:S(2)}) collective-permute-start(bf16[80,1920]{1,0:T(8,128)(2,1)S(1)} %copy-done.48), channel_id=1, source_target_pairs={{0,2},{2,0},{4,6},{6,4},{8,10},{10,8},{12,14},{14,12},{16,18},{18,... | collective-permute-start | bytes 921608 | tf_op jit(solution)/shard_map/ppermute | solution.py:257
  160.3 11.0 %collective-permute-start.40 = (bf16[160,1920]{1,0:T(8,128)(2,1)S(1)}, bf16[160,1920]{1,0:T(8,128)(2,1)S(1)}, u32[]{:S(2)}, u32[]{:S(2)}) collective-permute-start(bf16[160,1920]{1,0:T(8,128)(2,1)S(1)} %copy-done.47), channel_id=1, source_target_pairs={{0,2},{2,0},{4,6},{6,4},{8,10},{10,8},{12,14},{14,12},{16,18},{18,... | collective-permute-start | bytes 1843208 | tf_op jit(solution)/shard_map/ppermute | solution.py:257
  160.8 10.4 %collective-permute-start.43 = (bf16[96,1920]{1,0:T(8,128)(2,1)S(1)}, bf16[96,1920]{1,0:T(8,128)(2,1)S(1)}, u32[]{:S(2)}, u32[]{:S(2)}) collective-permute-start(bf16[96,1920]{1,0:T(8,128)(2,1)S(1)} %shard_map.214), channel_id=1, source_target_pairs={{0,8},{8,16},{16,24},{24,28},{28,20},{20,12},{12,4},{4,0},{2,6},{1... | collective-permute-start | bytes 1105928 | tf_op jit(solution)/shard_map/ppermute | solution.py:261
  167.3 23.4 %collective-permute-start.53 = (bf16[240,1920]{1,0:T(8,128)(2,1)S(1)}, bf16[240,1920]{1,0:T(8,128)(2,1)S(1)}, u32[]{:S(2)}, u32[]{:S(2)}) collective-permute-start(bf16[240,1920]{1,0:T(8,128)(2,1)S(1)} %shard_map.219), channel_id=1, source_target_pairs={{0,1},{1,0},{2,3},{3,2},{4,5},{5,4},{6,7},{7,6},{8,9},{9,8},{10,11... | collective-permute-start | bytes 2764808 | tf_op jit(solution)/shard_map/ppermute | solution.py:265
  171.4 10.9 %collective-permute-start.46 = (bf16[176,1920]{1,0:T(8,128)(2,1)S(1)}, bf16[176,1920]{1,0:T(8,128)(2,1)S(1)}, u32[]{:S(2)}, u32[]{:S(2)}) collective-permute-start(bf16[176,1920]{1,0:T(8,128)(2,1)S(1)} %shard_map.216), channel_id=1, source_target_pairs={{0,8},{8,16},{16,24},{24,28},{28,20},{20,12},{12,4},{4,0},{2,6},{1... | collective-permute-start | bytes 2027528 | tf_op jit(solution)/shard_map/ppermute | solution.py:261
  171.5 2.7 %collective-permute-start.39 = (bf16[160,1920]{1,0:T(8,128)(2,1)S(1)}, bf16[160,1920]{1,0:T(8,128)(2,1)S(1)}, u32[]{:S(2)}, u32[]{:S(2)}) collective-permute-start(bf16[160,1920]{1,0:T(8,128)(2,1)S(1)} %copy-done.46), channel_id=1, source_target_pairs={{0,2},{2,0},{4,6},{6,4},{8,10},{10,8},{12,14},{14,12},{16,18},{18,... | collective-permute-start | bytes 1843208 | tf_op jit(solution)/shard_map/ppermute | solution.py:257
  172.6 18.2 %collective-permute-start.60 = (bf16[160,1920]{1,0:T(8,128)(2,1)S(1)}, bf16[160,1920]{1,0:T(8,128)(2,1)S(1)}, u32[]{:S(2)}, u32[]{:S(2)}) collective-permute-start(bf16[160,1920]{1,0:T(8,128)(2,1)S(1)} %copy-done.45), channel_id=1, source_target_pairs={{0,2},{2,0},{4,6},{6,4},{8,10},{10,8},{12,14},{14,12},{16,18},{18,... | collective-permute-start | bytes 1843208 | tf_op jit(solution)/shard_map/ppermute | solution.py:257
  173.0 17.7 %collective-permute-start.51 = (bf16[160,1920]{1,0:T(8,128)(2,1)S(1)}, bf16[160,1920]{1,0:T(8,128)(2,1)S(1)}, u32[]{:S(2)}, u32[]{:S(2)}) collective-permute-start(bf16[160,1920]{1,0:T(8,128)(2,1)S(1)} %shard_map.218), channel_id=1, source_target_pairs={{0,8},{8,16},{16,24},{24,28},{28,20},{20,12},{12,4},{4,0},{2,6},{1... | collective-permute-start | bytes 1843208 | tf_op jit(solution)/shard_map/ppermute | solution.py:261
  182.5 13.6 %collective-permute-start.47 = (bf16[176,1920]{1,0:T(8,128)(2,1)S(1)}, bf16[176,1920]{1,0:T(8,128)(2,1)S(1)}, u32[]{:S(2)}, u32[]{:S(2)}) collective-permute-start(bf16[176,1920]{1,0:T(8,128)(2,1)S(1)} %shard_map.217), channel_id=1, source_target_pairs={{0,8},{8,16},{16,24},{24,28},{28,20},{20,12},{12,4},{4,0},{2,6},{1... | collective-permute-start | bytes 2027528 | tf_op jit(solution)/shard_map/ppermute | solution.py:261
  182.6 21.3 %collective-permute-start.36 = (bf16[256,1280]{1,0:T(8,128)(2,1)}, bf16[256,1280]{1,0:T(8,128)(2,1)}, u32[]{:S(2)}, u32[]{:S(2)}) collective-permute-start(bf16[256,1280]{1,0:T(8,128)(2,1)} %get-tuple-element.183), channel_id=1, source_target_pairs={{0,1},{1,0},{2,3},{3,2},{4,5},{5,4},{6,7},{7,6},{8,9},{9,8},{10,11... | collective-permute-start | bytes 1966088 | tf_op jit(solution)/shard_map/ppermute | solution.py:265
  190.7 5.5 %collective-permute-start.48 = (bf16[160,1920]{1,0:T(8,128)(2,1)}, bf16[160,1920]{1,0:T(8,128)(2,1)S(1)}, u32[]{:S(2)}, u32[]{:S(2)}) collective-permute-start(bf16[160,1920]{1,0:T(8,128)(2,1)} %get-tuple-element.214), channel_id=1, source_target_pairs={{0,2},{2,0},{4,6},{6,4},{8,10},{10,8},{12,14},{14,12},{16,18},{18,... | collective-permute-start | bytes 1843208 | tf_op jit(solution)/shard_map/ppermute | solution.py:257
  191.9 10.9 %collective-permute-start.61 = (bf16[160,1920]{1,0:T(8,128)(2,1)}, bf16[160,1920]{1,0:T(8,128)(2,1)}, u32[]{:S(2)}, u32[]{:S(2)}) collective-permute-start(bf16[160,1920]{1,0:T(8,128)(2,1)} %shard_map.221), channel_id=1, source_target_pairs={{0,8},{8,16},{16,24},{24,28},{28,20},{20,12},{12,4},{4,0},{2,6},{1... | collective-permute-start | bytes 1843208 | tf_op jit(solution)/shard_map/ppermute | solution.py:261
  191.9 19.0 %collective-permute-start.59 = (bf16[80,1920]{1,0:T(8,128)(2,1)}, bf16[80,1920]{1,0:T(8,128)(2,1)S(1)}, u32[]{:S(2)}, u32[]{:S(2)}) collective-permute-start(bf16[80,1920]{1,0:T(8,128)(2,1)} %get-tuple-element.223), channel_id=1, source_target_pairs={{0,2},{2,0},{4,6},{6,4},{8,10},{10,8},{12,14},{14,12},{16,18},{18,... | collective-permute-start | bytes 921608 | tf_op jit(solution)/shard_map/ppermute | solution.py:257
  196.1 21.1 %collective-permute-start.57 = (bf16[80,1920]{1,0:T(8,128)(2,1)}, bf16[80,1920]{1,0:T(8,128)(2,1)S(1)}, u32[]{:S(2)}, u32[]{:S(2)}) collective-permute-start(bf16[80,1920]{1,0:T(8,128)(2,1)} %get-tuple-element.221), channel_id=1, source_target_pairs={{0,2},{2,0},{4,6},{6,4},{8,10},{10,8},{12,14},{14,12},{16,18},{18,... | collective-permute-start | bytes 921608 | tf_op jit(solution)/shard_map/ppermute | solution.py:257
  196.4 13.6 %collective-permute-start.54 = (bf16[176,1920]{1,0:T(8,128)(2,1)S(1)}, bf16[176,1920]{1,0:T(8,128)(2,1)S(1)}, u32[]{:S(2)}, u32[]{:S(2)}) collective-permute-start(bf16[176,1920]{1,0:T(8,128)(2,1)S(1)} %shard_map.220), channel_id=1, source_target_pairs={{0,8},{8,16},{16,24},{24,28},{28,20},{20,12},{12,4},{4,0},{2,6},{1... | collective-permute-start | bytes 2027528 | tf_op jit(solution)/shard_map/ppermute | solution.py:261
  203.8 7.1 %collective-permute-start.62 = (bf16[80,1920]{1,0:T(8,128)(2,1)S(1)}, bf16[80,1920]{1,0:T(8,128)(2,1)S(1)}, u32[]{:S(2)}, u32[]{:S(2)}) collective-permute-start(bf16[80,1920]{1,0:T(8,128)(2,1)S(1)} %slice.87), channel_id=1, source_target_pairs={{0,2},{2,0},{4,6},{6,4},{8,10},{10,8},{12,14},{14,12},{16,18},{18,... | collective-permute-start | bytes 921608 | tf_op jit(solution)/shard_map/ppermute | solution.py:257
  210.8 1.4 collective-permute-start.55
  212.3 3.8 %collective-permute-start.56 = (f32[2,1920]{1,0:T(2,128)S(1)}, f32[2,1920]{1,0:T(2,128)S(1)}, u32[]{:S(2)}, u32[]{:S(2)}) collective-permute-start(f32[2,1920]{1,0:T(2,128)S(1)} %add_add_fusion), channel_id=1, source_target_pairs={{0,1},{1,0},{2,3},{3,2},{4,5},{5,4},{6,7},{7,6},{8,9},{9,8},{10,11... | collective-permute-start | bytes 46088 | tf_op jit(solution)/shard_map/ppermute | solution.py:265
  214.1 3.1 %collective-permute-start.58 = (bf16[80,1920]{1,0:T(8,128)(2,1)S(1)}, bf16[80,1920]{1,0:T(8,128)(2,1)S(1)}, u32[]{:S(2)}, u32[]{:S(2)}) collective-permute-start(bf16[80,1920]{1,0:T(8,128)(2,1)S(1)} %slice.105), channel_id=1, source_target_pairs={{0,2},{2,0},{4,6},{6,4},{8,10},{10,8},{12,14},{14,12},{16,18},{18,... | collective-permute-start | bytes 921608 | tf_op jit(solution)/shard_map/ppermute | solution.py:257
  (50 other events, 469.5 us)

commit v3 on v2

--- a/solution.py
+++ b/solution.py
@@ -791,7 +791,7 @@
     here, there = swap_late(here, there, logsum)
     w_late = call(
         assemble_kernel,
-        [after(order, came), *here, *there],
+        [order, *here, *there],
         [SMEM] + ([ANY] * 2 + [HELD] * 8) * 2,
         [(struct(2, width, 3 * cols), HELD)],
         [dma((2,))],

time: 222 us -> 220 us (level)
  transfers between devices with their start and end apart: 63 -> 63, of which waited for: 29 -> 29; matrix products, arithmetic and copies ran while one was open for 7% -> 7% of each run, Pallas kernels for 19% -> 21%
where the time goes in v3:
time: 220 us; the launch traced here: 217 us
  waiting for transfers between devices  96.7 us (44%)
  Pallas kernels  55.9 us (25%)
  starting transfers between devices  43.3 us (20%)
  other arithmetic  10.3 us (5%)
  local copies, waits for them, and re-layouts  9.29 us (4%)
    pallas_call x19, Pallas kernels, call(): pl.pallas_call(body, out_shape=[place[id(space)](out.shape, out.dtype) fo...  55.9 us
    ppermute x14, waiting for transfers between devices, across(): return lax.ppermute(value, 'tp', ((0, 1), (1, 0)))  46.2 us
    ppermute x16, waiting for transfers between devices, around(): return lax.ppermute(value, 'fsdp', AROUND)  41.7 us
    ppermute x16, starting transfers between devices, around(): return lax.ppermute(value, 'fsdp', AROUND)  16.8 us
    ppermute x14, starting transfers between devices, across(): return lax.ppermute(value, 'tp', ((0, 1), (1, 0)))  15.3 us
    ppermute x33, starting transfers between devices, sibling(): return lax.ppermute(value, 'fsdp', CORES)  11.2 us
    ppermute x33, waiting for transfers between devices, sibling(): return lax.ppermute(value, 'fsdp', CORES)  8.72 us
  transfers between devices with their start and end apart: 63, of which 29 were waited for; matrix products, arithmetic and copies ran while one was open for 7% of the time, Pallas kernels for 21%

profile of v3, /device:TPU:0, one launch (start us, length us, event | category | flops | bytes accessed | tf_op | source)
XLA Modules:
  0.0 217.3 jit_solution(2214434637259849689)
XLA Ops:
  0.6 2.0 shard_map.203
  3.1 1.4 collective-permute-done.rest_1_
  4.9 2.6 %collective-permute-start.5 = (bf16[256,1280]{1,0:T(8,128)(2,1)}, bf16[256,1280]{1,0:T(8,128)(2,1)S(1)}, u32[]{:S(2)}, u32[]{:S(2)}) collective-permute-start(bf16[256,1280]{1,0:T(8,128)(2,1)} %tokens_in.1), channel_id=1, source_target_pairs={{0,1},{1,0},{2,3},{3,2},{4,5},{5,4},{6,7},{7,6},{8,9},{9,8},{10,11... | collective-permute-start | bytes 1966088 | tf_op jit(solution)/shard_map/ppermute | solution.py:265
  7.5 1.0 pad_maximum_fusion.1
  8.6 1.6 collective-permute-start.6
  10.3 1.6 collective-permute-start.2
  11.9 11.1 %collective-permute-done.5.other_in = bf16[256,1280]{1,0:T(8,128)(2,1)S(1)} collective-permute-done((bf16[256,1280]{1,0:T(8,128)(2,1)}, bf16[256,1280]{1,0:T(8,128)(2,1)S(1)}, u32[]{:S(2)}, u32[]{:S(2)}) %collective-permute-start.5) | collective-permute-done | bytes 655392 | tf_op jit(solution)/shard_map/ppermute | solution.py:265
  23.0 1.8 collective-permute-start.7
  25.4 1.6 collective-permute-start.3
  28.4 1.1 collective-permute-start.10
  29.5 7.6 %collective-permute-done.8.rest_10_ = bf16[80,1920]{1,0:T(8,128)(2,1)S(1)} collective-permute-done((bf16[80,1920]{1,0:T(8,128)(2,1)S(1)}, bf16[80,1920]{1,0:T(8,128)(2,1)S(1)}, u32[]{:S(2)}, u32[]{:S(2)}) %collective-permute-start.8) | collective-permute-done | bytes 307232 | tf_op jit(solution)/shard_map/ppermute | solution.py:265
  37.1 1.6 collective-permute-start.9
  38.7 1.3 collective-permute-done.3.rest_3_
  40.1 1.8 collective-permute-start.12
  41.9 1.8 fusion.2.normed
  43.7 3.9 %collective-permute-done.9.rest_4_ = bf16[160,1920]{1,0:T(8,128)(2,1)} collective-permute-done((bf16[160,1920]{1,0:T(8,128)(2,1)}, bf16[160,1920]{1,0:T(8,128)(2,1)}, u32[]{:S(2)}, u32[]{:S(2)}) %collective-permute-start.9) | collective-permute-done | bytes 614432 | tf_op jit(solution)/shard_map/ppermute | solution.py:261
  47.6 1.0 slice.92
  48.6 1.6 collective-permute-start.11
  51.2 2.8 %collective-permute-done.12.rest_4_ = bf16[160,1920]{1,0:T(8,128)(2,1)S(1)} collective-permute-done((bf16[160,1920]{1,0:T(8,128)(2,1)}, bf16[160,1920]{1,0:T(8,128)(2,1)S(1)}, u32[]{:S(2)}, u32[]{:S(2)}) %collective-permute-start.12) | collective-permute-done | bytes 614432 | tf_op jit(solution)/shard_map/ppermute | solution.py:261
  54.1 1.8 collective-permute-start.13
  55.9 1.6 collective-permute-done.11.rest_5_
  57.5 3.7 %collective-permute-done.13.rest_5_ = bf16[80,1920]{1,0:T(8,128)(2,1)S(1)} collective-permute-done((bf16[80,1920]{1,0:T(8,128)(2,1)S(1)}, bf16[80,1920]{1,0:T(8,128)(2,1)S(1)}, u32[]{:S(2)}, u32[]{:S(2)}) %collective-permute-start.13) | collective-permute-done | bytes 307232 | tf_op jit(solution)/shard_map/ppermute | solution.py:261
  61.5 3.2 %collective-permute-done.4.rest_13_ = bf16[160,1920]{1,0:T(8,128)(2,1)} collective-permute-done((bf16[160,1920]{1,0:T(8,128)(2,1)}, bf16[160,1920]{1,0:T(8,128)(2,1)}, u32[]{:S(2)}, u32[]{:S(2)}) %collective-permute-start.4) | collective-permute-done | bytes 614432 | tf_op jit(solution)/shard_map/ppermute | solution.py:265
  64.7 1.1 collective-permute-start.24
  66.8 10.9 %shard_map.204 = (bf16[640,256]{1,0:T(8,128)(2,1)S(1)}, bf16[640,256]{1,0:T(8,128)(2,1)S(1)}, f32[8,1,512]{2,1,0:T(1,128)S(1)}, bf16[1920,512]{1,0:T(8,128)(2,1)}, bf16[1280,1920]{1,0:T(8,128)(2,1)}) custom-call(s32[17]{0:T(128)S(1)} %stack.71.order, s32[1,8]{1,0:T(1,128)S(1)} %copy-done.24, f32[1,640]{1,0:T(1,128)S(1)} %broadcast_in_dim_tile.3.scaling, ...), custom_call_target="tpu_custom_call" | custom-call | flops 32000000000 | bytes 4194304 | tf_op jit(solution)/shard_map/pallas_call | solution.py:713
  77.7 3.5 %collective-permute-done.24.rest_14_ = bf16[160,1920]{1,0:T(8,128)(2,1)S(1)} collective-permute-done((bf16[160,1920]{1,0:T(8,128)(2,1)S(1)}, bf16[160,1920]{1,0:T(8,128)(2,1)S(1)}, u32[]{:S(2)}, u32[]{:S(2)}) %collective-permute-start.24) | collective-permute-done | bytes 614432 | tf_op jit(solution)/shard_map/ppermute | solution.py:265
  81.7 2.8 %collective-permute-done.25.rest_15_ = bf16[80,1920]{1,0:T(8,128)(2,1)S(1)} collective-permute-done((bf16[80,1920]{1,0:T(8,128)(2,1)S(1)}, bf16[80,1920]{1,0:T(8,128)(2,1)S(1)}, u32[]{:S(2)}, u32[]{:S(2)}) %collective-permute-start.25) | collective-permute-done | bytes 307232 | tf_op jit(solution)/shard_map/ppermute | solution.py:265
  85.1 1.0 collective-permute-done.26.rest_16_
  87.1 1.3 collective-permute-start.18
  88.3 1.9 collective-permute-done.21.rest_8_
  90.3 3.4 %shard_map.205.weights = bf16[2,1280,1920]{2,1,0:T(8,128)(2,1)S(1)} custom-call(s32[17]{0:T(128)S(1)} %stack.71.order, bf16[80,1920]{1,0:T(8,128)(2,1)} %get-tuple-element.123.rest_0_, bf16[80,1920]{1,0:T(8,128)(2,1)} %copy-done.34, bf16[160,1920]{1,0:T(8,128)(2,1)S(1)} %collective-permute-done.2.rest_2_, bf16[160,1920]{1,0:T(8,128)(2,1)} %collective-permute-done.3.rest_3_, ...), custom_call_target="tpu_custom_call" | custom-call | flops 4000000 | bytes 4194304 | tf_op jit(solution)/shard_map/pallas_call | solution.py:713
  93.7 3.1 %collective-permute-done.18.came = bf16[640,256]{1,0:T(8,128)(2,1)S(1)} collective-permute-done((bf16[640,256]{1,0:T(8,128)(2,1)S(1)}, bf16[640,256]{1,0:T(8,128)(2,1)S(1)}, u32[]{:S(2)}, u32[]{:S(2)}) %collective-permute-start.18) | collective-permute-done | bytes 327712 | tf_op jit(solution)/shard_map/ppermute | solution.py:265
  96.8 8.5 %shard_map.206 = (bf16[640,256]{1,0:T(8,128)(2,1)S(1)}, bf16[640,256]{1,0:T(8,128)(2,1)S(1)}, bf16[256,1280]{1,0:T(8,128)(2,1)S(1)}, bf16[256,1280]{1,0:T(8,128)...) custom-call(bf16[256,1280]{1,0:T(8,128)(2,1)S(1)} %copy-done, ...), custom_call_target="tpu_custom_call" | custom-call | flops 32000000000 | bytes 4194304 | tf_op jit(solution)/shard_map/pallas_call | solution.py:713
  106.0 1.3 collective-permute-start.30
  107.3 6.5 %shard_map.207 = (bf16[80,1920]{1,0:T(8,128)(2,1)}, bf16[160,1920]{1,0:T(8,128)(2,1)}, bf16[160,1920]{1,0:T(8,128)(2,1)}, bf16[160,1920]{1,0:T(8,128)(2,1)}, bf1...) custom-call(s32[17]{0:T(128)S(1)} %stack.71.order, ...), custom_call_target="tpu_custom_call" | custom-call | flops 24000000000 | bytes 4194304 | tf_op jit(solution)/shard_map/pallas_call | solution.py:713
  113.8 1.2 collective-permute-done.30.came
  116.9 1.8 collective-permute-done.32.other
  119.8 1.3 collective-permute-start.33
  122.2 12.5 %shard_map.208 = (f32[80,1]{1,0:T(8,128)S(1)}, f32[1,1280]{1,0:T(1,128)S(1)}, bf16[512,1920]{1,0:T(8,128)(2,1)}, f32[256,1280]{1,0:T(8,128)}, bf16[256,1280]{1,0:T(8,128)(2,1)}) custom-call(s32[17]{0:T(128)S(1)} %stack.71.order, s32[1,8]{1,0:T(1,128)S(1)} %copy-done.25, f32[80,1]{1,0:T(8,128)S(1)} %copy.24.scaling_col, bf16[640,256]{1,0:T(8,128)(2,1)S(1)} %copy-done.27, ...), custom_call_target="tpu_custom_call" | custom-call | flops 48000000000 | bytes 4194304 | tf_op jit(solution)/shard_map/pallas_call | solution.py:713
  135.3 1.1 shard_map.213
  136.4 1.5 collective-permute-start.38
  138.1 4.3 %collective-permute-done.35.rest_2_ = bf16[160,1920]{1,0:T(8,128)(2,1)S(1)} collective-permute-done((bf16[160,1920]{1,0:T(8,128)(2,1)S(1)}, bf16[160,1920]{1,0:T(8,128)(2,1)S(1)}, u32[]{:S(2)}, u32[]{:S(2)}) %collective-permute-start.35) | collective-permute-done | bytes 614432 | tf_op jit(solution)/shard_map/ppermute | solution.py:265
  143.3 6.9 %shard_map.212 = (bf16[80,1920]{1,0:T(8,128)(2,1)}, bf16[160,1920]{1,0:T(8,128)(2,1)}, bf16[160,1920]{1,0:T(8,128)(2,1)}, bf16[160,1920]{1,0:T(8,128)(2,1)}, bf1...) custom-call(s32[17]{0:T(128)S(1)} %stack.71.order, ...), custom_call_target="tpu_custom_call" | custom-call | flops 20000000000 | bytes 4194304 | tf_op jit(solution)/shard_map/pallas_call | solution.py:713
  151.1 1.3 collective-permute-start.50
  152.4 1.4 shard_map.215
  153.8 1.2 collective-permute-start.45
  155.1 2.6 %collective-permute-start.41 = (bf16[80,1920]{1,0:T(8,128)(2,1)S(1)}, bf16[80,1920]{1,0:T(8,128)(2,1)S(1)}, u32[]{:S(2)}, u32[]{:S(2)}) collective-permute-start(bf16[80,1920]{1,0:T(8,128)(2,1)S(1)} %copy-done.48), channel_id=1, source_target_pairs={{0,2},{2,0},{4,6},{6,4},{8,10},{10,8},{12,14},{14,12},{16,18},{18,... | collective-permute-start | bytes 921608 | tf_op jit(solution)/shard_map/ppermute | solution.py:257
  157.7 1.2 collective-permute-done.41.came
  159.8 6.1 %collective-permute-done.45.rest_3_ = bf16[160,1920]{1,0:T(8,128)(2,1)S(1)} collective-permute-done((bf16[160,1920]{1,0:T(8,128)(2,1)S(1)}, bf16[160,1920]{1,0:T(8,128)(2,1)S(1)}, u32[]{:S(2)}, u32[]{:S(2)}) %collective-permute-start.45) | collective-permute-done | bytes 614432 | tf_op jit(solution)/shard_map/ppermute | solution.py:261
  166.2 3.7 %collective-permute-done.43.rest_2_ = bf16[96,1920]{1,0:T(8,128)(2,1)S(1)} collective-permute-done((bf16[96,1920]{1,0:T(8,128)(2,1)S(1)}, bf16[96,1920]{1,0:T(8,128)(2,1)S(1)}, u32[]{:S(2)}, u32[]{:S(2)}) %collective-permute-start.43) | collective-permute-done | bytes 368672 | tf_op jit(solution)/shard_map/ppermute | solution.py:261
  170.1 1.0 collective-permute-start.39
  172.8 8.1 %collective-permute-done.46.rest_2_ = bf16[176,1920]{1,0:T(8,128)(2,1)S(1)} collective-permute-done((bf16[176,1920]{1,0:T(8,128)(2,1)S(1)}, bf16[176,1920]{1,0:T(8,128)(2,1)S(1)}, u32[]{:S(2)}, u32[]{:S(2)}) %collective-permute-start.46) | collective-permute-done | bytes 675872 | tf_op jit(solution)/shard_map/ppermute | solution.py:261
  181.6 7.7 %collective-permute-done.53 = bf16[240,1920]{1,0:T(8,128)(2,1)S(1)} collective-permute-done((bf16[240,1920]{1,0:T(8,128)(2,1)S(1)}, bf16[240,1920]{1,0:T(8,128)(2,1)S(1)}, u32[]{:S(2)}, u32[]{:S(2)}) %collective-permute-start.53) | collective-permute-done | bytes 921632 | tf_op jit(solution)/shard_map/ppermute | solution.py:265
  189.4 1.1 shard_map.221
  190.5 2.2 %collective-permute-start.59 = (bf16[80,1920]{1,0:T(8,128)(2,1)}, bf16[80,1920]{1,0:T(8,128)(2,1)S(1)}, u32[]{:S(2)}, u32[]{:S(2)}) collective-permute-start(bf16[80,1920]{1,0:T(8,128)(2,1)} %get-tuple-element.221), channel_id=1, source_target_pairs={{0,2},{2,0},{4,6},{6,4},{8,10},{10,8},{12,14},{14,12},{16,18},{18,... | collective-permute-start | bytes 921608 | tf_op jit(solution)/shard_map/ppermute | solution.py:257
  192.8 2.0 collective-permute-done.47.rest_2_
  195.1 6.4 %collective-permute-done.61 = bf16[160,1920]{1,0:T(8,128)(2,1)} collective-permute-done((bf16[160,1920]{1,0:T(8,128)(2,1)}, bf16[160,1920]{1,0:T(8,128)(2,1)}, u32[]{:S(2)}, u32[]{:S(2)}) %collective-permute-start.61) | collective-permute-done | bytes 614432 | tf_op jit(solution)/shard_map/ppermute | solution.py:261
  201.4 1.0 slice.87
  202.6 1.6 fusion.3
  204.2 2.7 %fusion.6 = f32[256,1280]{1,0:T(8,128)} fusion(f32[256,1280]{1,0:T(8,128)S(1)} %copy-done.32, bf16[256,1280]{1,0:T(8,128)(2,1)S(1)} %copy-done.1, f32[256,1280]{1,0:T(8,128)S(1)} %copy-done.30, bf16[256,1280]{1,0:T(8,128)(2,1)} %collective-permute-done.36, f32[256]{0:T(256)S(1)} %broadcast_multiply_fusion, f32[256]{0:T(256)S(1)} %get-tuple-element.238, ...), kind=kLoop, calls=%fused_computation.11 | loop fusion | flops 2949120 | bytes 5251072 | tf_op jit(solution)/shard_map/add | solution.py:934
  206.9 1.7 collective-permute-done.54
  209.6 1.3 convert_add_fusion
  210.9 1.0 collective-permute-start.56
  213.0 1.7 collective-permute-done.56
  (222 shorter events, 22.9 us)
Async XLA Ops:
  2.6 1.9 collective-permute-start
  4.5 5.7 %collective-permute-start.1 = (bf16[80,1920]{1,0:T(8,128)(2,1)}, bf16[80,1920]{1,0:T(8,128)(2,1)S(1)}, u32[]{:S(2)}, u32[]{:S(2)}) collective-permute-start(bf16[80,1920]{1,0:T(8,128)(2,1)} %get-tuple-element.123.rest_0_), channel_id=1, source_target_pairs={{0,2},{2,0},{4,6},{6,4},{8,10},{10,8},{12,14},{14,12},{16,18},{18,... | collective-permute-start | bytes 921608 | tf_op jit(solution)/shard_map/ppermute | solution.py:257
  4.9 18.1 %collective-permute-start.5 = (bf16[256,1280]{1,0:T(8,128)(2,1)}, bf16[256,1280]{1,0:T(8,128)(2,1)S(1)}, u32[]{:S(2)}, u32[]{:S(2)}) collective-permute-start(bf16[256,1280]{1,0:T(8,128)(2,1)} %tokens_in.1), channel_id=1, source_target_pairs={{0,1},{1,0},{2,3},{3,2},{4,5},{5,4},{6,7},{7,6},{8,9},{9,8},{10,11... | collective-permute-start | bytes 1966088 | tf_op jit(solution)/shard_map/ppermute | solution.py:265
  8.6 33.3 %copy-start.42 = (f32[1280]{0:T(1024)S(1)}, f32[1280]{0:T(1024)}, u32[]{:S(2)}) copy-start(f32[1280]{0:T(1024)} %param.14) | copy-start | bytes 15364
  8.6 14.4 %collective-permute-start.6 = (bf16[160,1920]{1,0:T(8,128)(2,1)S(1)}, bf16[160,1920]{1,0:T(8,128)(2,1)}, u32[]{:S(2)}, u32[]{:S(2)}) collective-permute-start(bf16[160,1920]{1,0:T(8,128)(2,1)S(1)} %pad_maximum_fusion.1), channel_id=1, source_target_pairs={{0,8},{8,16},{16,24},{24,28},{28,20},{20,12},{12,4},{4,0},{2,6},{1... | collective-permute-start | bytes 1843208 | tf_op jit(solution)/shard_map/ppermute | solution.py:261
  10.3 15.1 %collective-permute-start.2 = (bf16[160,1920]{1,0:T(8,128)(2,1)S(1)}, bf16[160,1920]{1,0:T(8,128)(2,1)S(1)}, u32[]{:S(2)}, u32[]{:S(2)}) collective-permute-start(bf16[160,1920]{1,0:T(8,128)(2,1)S(1)} %pad_maximum_fusion), channel_id=1, source_target_pairs={{0,8},{8,16},{16,24},{24,28},{28,20},{20,12},{12,4},{4,0},{2,6},{1... | collective-permute-start | bytes 1843208 | tf_op jit(solution)/shard_map/ppermute | solution.py:261
  23.0 14.1 %collective-permute-start.7 = (bf16[160,1920]{1,0:T(8,128)(2,1)}, bf16[160,1920]{1,0:T(8,128)(2,1)}, u32[]{:S(2)}, u32[]{:S(2)}) collective-permute-start(bf16[160,1920]{1,0:T(8,128)(2,1)} %collective-permute-done.6.rest_2_), channel_id=1, source_target_pairs={{0,8},{8,16},{16,24},{24,28},{28,20},{20,12},{12,4},{4,0},{2,6},{1... | collective-permute-start | bytes 1843208 | tf_op jit(solution)/shard_map/ppermute | solution.py:261
  25.4 14.7 %collective-permute-start.3 = (bf16[160,1920]{1,0:T(8,128)(2,1)S(1)}, bf16[160,1920]{1,0:T(8,128)(2,1)}, u32[]{:S(2)}, u32[]{:S(2)}) collective-permute-start(bf16[160,1920]{1,0:T(8,128)(2,1)S(1)} %collective-permute-done.2.rest_2_), channel_id=1, source_target_pairs={{0,8},{8,16},{16,24},{24,28},{28,20},{20,12},{12,4},{4,0},{2,6},{1... | collective-permute-start | bytes 1843208 | tf_op jit(solution)/shard_map/ppermute | solution.py:261
  26.9 10.2 %collective-permute-start.8 = (bf16[80,1920]{1,0:T(8,128)(2,1)S(1)}, bf16[80,1920]{1,0:T(8,128)(2,1)S(1)}, u32[]{:S(2)}, u32[]{:S(2)}) collective-permute-start(bf16[80,1920]{1,0:T(8,128)(2,1)S(1)} %copy-done.33), channel_id=1, source_target_pairs={{0,1},{1,0},{2,3},{3,2},{4,5},{5,4},{6,7},{7,6},{8,9},{9,8},{10,11... | collective-permute-start | bytes 921608 | tf_op jit(solution)/shard_map/ppermute | solution.py:265
  28.4 20.2 %collective-permute-start.10 = (bf16[160,1920]{1,0:T(8,128)(2,1)S(1)}, bf16[160,1920]{1,0:T(8,128)(2,1)S(1)}, u32[]{:S(2)}, u32[]{:S(2)}) collective-permute-start(bf16[160,1920]{1,0:T(8,128)(2,1)S(1)} %collective-permute-done.2.rest_2_), channel_id=1, source_target_pairs={{0,1},{1,0},{2,3},{3,2},{4,5},{5,4},{6,7},{7,6},{8,9},{9,8},{10,11... | collective-permute-start | bytes 1843208 | tf_op jit(solution)/shard_map/ppermute | solution.py:265
  37.1 10.5 %collective-permute-start.9 = (bf16[160,1920]{1,0:T(8,128)(2,1)}, bf16[160,1920]{1,0:T(8,128)(2,1)}, u32[]{:S(2)}, u32[]{:S(2)}) collective-permute-start(bf16[160,1920]{1,0:T(8,128)(2,1)} %collective-permute-done.7.rest_3_), channel_id=1, source_target_pairs={{0,8},{8,16},{16,24},{24,28},{28,20},{20,12},{12,4},{4,0},{2,6},{1... | collective-permute-start | bytes 1843208 | tf_op jit(solution)/shard_map/ppermute | solution.py:261
  40.1 14.0 %collective-permute-start.12 = (bf16[160,1920]{1,0:T(8,128)(2,1)}, bf16[160,1920]{1,0:T(8,128)(2,1)S(1)}, u32[]{:S(2)}, u32[]{:S(2)}) collective-permute-start(bf16[160,1920]{1,0:T(8,128)(2,1)} %collective-permute-done.3.rest_3_), channel_id=1, source_target_pairs={{0,8},{8,16},{16,24},{24,28},{28,20},{20,12},{12,4},{4,0},{2,6},{1... | collective-permute-start | bytes 1843208 | tf_op jit(solution)/shard_map/ppermute | solution.py:261
  48.6 8.9 %collective-permute-start.11 = (bf16[80,1920]{1,0:T(8,128)(2,1)S(1)}, bf16[80,1920]{1,0:T(8,128)(2,1)}, u32[]{:S(2)}, u32[]{:S(2)}) collective-permute-start(bf16[80,1920]{1,0:T(8,128)(2,1)S(1)} %slice.92), channel_id=1, source_target_pairs={{0,8},{8,16},{16,24},{24,28},{28,20},{20,12},{12,4},{4,0},{2,6},{1... | collective-permute-start | bytes 921608 | tf_op jit(solution)/shard_map/ppermute | solution.py:261
  50.3 14.4 %collective-permute-start.4 = (bf16[160,1920]{1,0:T(8,128)(2,1)}, bf16[160,1920]{1,0:T(8,128)(2,1)}, u32[]{:S(2)}, u32[]{:S(2)}) collective-permute-start(bf16[160,1920]{1,0:T(8,128)(2,1)} %collective-permute-done.3.rest_3_), channel_id=1, source_target_pairs={{0,1},{1,0},{2,3},{3,2},{4,5},{5,4},{6,7},{7,6},{8,9},{9,8},{10,11... | collective-permute-start | bytes 1843208 | tf_op jit(solution)/shard_map/ppermute | solution.py:265
  51.2 14.6 %collective-permute-start.15 = (bf16[160,1920]{1,0:T(8,128)(2,1)}, bf16[160,1920]{1,0:T(8,128)(2,1)}, u32[]{:S(2)}, u32[]{:S(2)}) collective-permute-start(bf16[160,1920]{1,0:T(8,128)(2,1)} %collective-permute-done.6.rest_2_), channel_id=1, source_target_pairs={{0,2},{2,0},{4,6},{6,4},{8,10},{10,8},{12,14},{14,12},{16,18},{18,... | collective-permute-start | bytes 1843208 | tf_op jit(solution)/shard_map/ppermute | solution.py:257
  54.1 7.1 %collective-permute-start.13 = (bf16[80,1920]{1,0:T(8,128)(2,1)S(1)}, bf16[80,1920]{1,0:T(8,128)(2,1)S(1)}, u32[]{:S(2)}, u32[]{:S(2)}) collective-permute-start(bf16[80,1920]{1,0:T(8,128)(2,1)S(1)} %slice.93), channel_id=1, source_target_pairs={{0,8},{8,16},{16,24},{24,28},{28,20},{20,12},{12,4},{4,0},{2,6},{1... | collective-permute-start | bytes 921608 | tf_op jit(solution)/shard_map/ppermute | solution.py:261
  55.9 10.8 %collective-permute-start.16 = (bf16[160,1920]{1,0:T(8,128)(2,1)}, bf16[160,1920]{1,0:T(8,128)(2,1)}, u32[]{:S(2)}, u32[]{:S(2)}) collective-permute-start(bf16[160,1920]{1,0:T(8,128)(2,1)} %collective-permute-done.7.rest_3_), channel_id=1, source_target_pairs={{0,2},{2,0},{4,6},{6,4},{8,10},{10,8},{12,14},{14,12},{16,18},{18,... | collective-permute-start | bytes 1843208 | tf_op jit(solution)/shard_map/ppermute | solution.py:257
  57.5 9.3 %collective-permute-start.17 = (bf16[160,1920]{1,0:T(8,128)(2,1)}, bf16[160,1920]{1,0:T(8,128)(2,1)}, u32[]{:S(2)}, u32[]{:S(2)}) collective-permute-start(bf16[160,1920]{1,0:T(8,128)(2,1)} %collective-permute-done.9.rest_4_), channel_id=1, source_target_pairs={{0,2},{2,0},{4,6},{6,4},{8,10},{10,8},{12,14},{14,12},{16,18},{18,... | collective-permute-start | bytes 1843208 | tf_op jit(solution)/shard_map/ppermute | solution.py:257
  61.2 5.5 %collective-permute-start.14 = (bf16[80,1920]{1,0:T(8,128)(2,1)}, bf16[80,1920]{1,0:T(8,128)(2,1)}, u32[]{:S(2)}, u32[]{:S(2)}) collective-permute-start(bf16[80,1920]{1,0:T(8,128)(2,1)} %collective-permute-done.11.rest_5_), channel_id=1, source_target_pairs={{0,2},{2,0},{4,6},{6,4},{8,10},{10,8},{12,14},{14,12},{16,18},{18,... | collective-permute-start | bytes 921608 | tf_op jit(solution)/shard_map/ppermute | solution.py:257
  64.7 16.5 %collective-permute-start.24 = (bf16[160,1920]{1,0:T(8,128)(2,1)S(1)}, bf16[160,1920]{1,0:T(8,128)(2,1)S(1)}, u32[]{:S(2)}, u32[]{:S(2)}) collective-permute-start(bf16[160,1920]{1,0:T(8,128)(2,1)S(1)} %collective-permute-done.12.rest_4_), channel_id=1, source_target_pairs={{0,1},{1,0},{2,3},{3,2},{4,5},{5,4},{6,7},{7,6},{8,9},{9,8},{10,11... | collective-permute-start | bytes 1843208 | tf_op jit(solution)/shard_map/ppermute | solution.py:265
  65.8 18.7 %collective-permute-start.25 = (bf16[80,1920]{1,0:T(8,128)(2,1)S(1)}, bf16[80,1920]{1,0:T(8,128)(2,1)S(1)}, u32[]{:S(2)}, u32[]{:S(2)}) collective-permute-start(bf16[80,1920]{1,0:T(8,128)(2,1)S(1)} %collective-permute-done.13.rest_5_), channel_id=1, source_target_pairs={{0,1},{1,0},{2,3},{3,2},{4,5},{5,4},{6,7},{7,6},{8,9},{9,8},{10,11... | collective-permute-start | bytes 921608 | tf_op jit(solution)/shard_map/ppermute | solution.py:265
  81.2 5.5 %collective-permute-start.29 = (bf16[160,1920]{1,0:T(8,128)(2,1)S(1)}, bf16[160,1920]{1,0:T(8,128)(2,1)S(1)}, u32[]{:S(2)}, u32[]{:S(2)}) collective-permute-start(bf16[160,1920]{1,0:T(8,128)(2,1)S(1)} %collective-permute-done.24.rest_14_), channel_id=1, source_target_pairs={{0,2},{2,0},{4,6},{6,4},{8,10},{10,8},{12,14},{14,12},{16,18},{18,... | collective-permute-start | bytes 1843208 | tf_op jit(solution)/shard_map/ppermute | solution.py:257
  81.2 5.8 %collective-permute-start.28 = (bf16[160,1920]{1,0:T(8,128)(2,1)}, bf16[160,1920]{1,0:T(8,128)(2,1)S(1)}, u32[]{:S(2)}, u32[]{:S(2)}) collective-permute-start(bf16[160,1920]{1,0:T(8,128)(2,1)} %collective-permute-done.4.rest_13_), channel_id=1, source_target_pairs={{0,2},{2,0},{4,6},{6,4},{8,10},{10,8},{12,14},{14,12},{16,18},{18,... | collective-permute-start | bytes 1843208 | tf_op jit(solution)/shard_map/ppermute | solution.py:257
  81.7 3.3 %collective-permute-start.23 = (bf16[80,1920]{1,0:T(8,128)(2,1)S(1)}, bf16[80,1920]{1,0:T(8,128)(2,1)S(1)}, u32[]{:S(2)}, u32[]{:S(2)}) collective-permute-start(bf16[80,1920]{1,0:T(8,128)(2,1)S(1)} %copy-done.37), channel_id=1, source_target_pairs={{0,2},{2,0},{4,6},{6,4},{8,10},{10,8},{12,14},{14,12},{16,18},{18,... | collective-permute-start | bytes 921608 | tf_op jit(solution)/shard_map/ppermute | solution.py:257
  84.5 1.6 collective-permute-start.26
  84.5 2.0 collective-permute-start.19
  85.0 3.3 %collective-permute-start.27 = (bf16[160,1920]{1,0:T(8,128)(2,1)S(1)}, bf16[160,1920]{1,0:T(8,128)(2,1)S(1)}, u32[]{:S(2)}, u32[]{:S(2)}) collective-permute-start(bf16[160,1920]{1,0:T(8,128)(2,1)S(1)} %copy-done.14), channel_id=1, source_target_pairs={{0,2},{2,0},{4,6},{6,4},{8,10},{10,8},{12,14},{14,12},{16,18},{18,... | collective-permute-start | bytes 1843208 | tf_op jit(solution)/shard_map/ppermute | solution.py:257
  86.1 2.2 %collective-permute-start.22 = (bf16[160,1920]{1,0:T(8,128)(2,1)S(1)}, bf16[160,1920]{1,0:T(8,128)(2,1)S(1)}, u32[]{:S(2)}, u32[]{:S(2)}) collective-permute-start(bf16[160,1920]{1,0:T(8,128)(2,1)S(1)} %collective-permute-done.12.rest_4_), channel_id=1, source_target_pairs={{0,2},{2,0},{4,6},{6,4},{8,10},{10,8},{12,14},{14,12},{16,18},{18,... | collective-permute-start | bytes 1843208 | tf_op jit(solution)/shard_map/ppermute | solution.py:257
  86.5 3.7 %collective-permute-start.21 = (bf16[160,1920]{1,0:T(8,128)(2,1)}, bf16[160,1920]{1,0:T(8,128)(2,1)S(1)}, u32[]{:S(2)}, u32[]{:S(2)}) collective-permute-start(bf16[160,1920]{1,0:T(8,128)(2,1)} %collective-permute-done.3.rest_3_), channel_id=1, source_target_pairs={{0,2},{2,0},{4,6},{6,4},{8,10},{10,8},{12,14},{14,12},{16,18},{18,... | collective-permute-start | bytes 1843208 | tf_op jit(solution)/shard_map/ppermute | solution.py:257
  86.7 3.6 %collective-permute-start.20 = (bf16[160,1920]{1,0:T(8,128)(2,1)S(1)}, bf16[160,1920]{1,0:T(8,128)(2,1)S(1)}, u32[]{:S(2)}, u32[]{:S(2)}) collective-permute-start(bf16[160,1920]{1,0:T(8,128)(2,1)S(1)} %collective-permute-done.2.rest_2_), channel_id=1, source_target_pairs={{0,2},{2,0},{4,6},{6,4},{8,10},{10,8},{12,14},{14,12},{16,18},{18,... | collective-permute-start | bytes 1843208 | tf_op jit(solution)/shard_map/ppermute | solution.py:257
  87.1 9.8 %collective-permute-start.18 = (bf16[640,256]{1,0:T(8,128)(2,1)S(1)}, bf16[640,256]{1,0:T(8,128)(2,1)S(1)}, u32[]{:S(2)}, u32[]{:S(2)}) collective-permute-start(bf16[640,256]{1,0:T(8,128)(2,1)S(1)} %get-tuple-element.128), channel_id=1, source_target_pairs={{0,1},{1,0},{2,3},{3,2},{4,5},{5,4},{6,7},{7,6},{8,9},{9,8},{10,11... | collective-permute-start | bytes 983048 | tf_op jit(solution)/shard_map/ppermute | solution.py:265
  106.0 8.9 %collective-permute-start.30 = (bf16[640,256]{1,0:T(8,128)(2,1)S(1)}, bf16[640,256]{1,0:T(8,128)(2,1)S(1)}, u32[]{:S(2)}, u32[]{:S(2)}) collective-permute-start(bf16[640,256]{1,0:T(8,128)(2,1)S(1)} %get-tuple-element.163), channel_id=1, source_target_pairs={{0,1},{1,0},{2,3},{3,2},{4,5},{5,4},{6,7},{7,6},{8,9},{9,8},{10,11... | collective-permute-start | bytes 983048 | tf_op jit(solution)/shard_map/ppermute | solution.py:265
  115.7 5.5 %collective-permute-start.34 = (bf16[160,1920]{1,0:T(8,128)(2,1)}, bf16[160,1920]{1,0:T(8,128)(2,1)S(1)}, u32[]{:S(2)}, u32[]{:S(2)}) collective-permute-start(bf16[160,1920]{1,0:T(8,128)(2,1)} %get-tuple-element.179), channel_id=1, source_target_pairs={{0,2},{2,0},{4,6},{6,4},{8,10},{10,8},{12,14},{14,12},{16,18},{18,... | collective-permute-start | bytes 1843208 | tf_op jit(solution)/shard_map/ppermute | solution.py:257
  115.7 3.1 %collective-permute-start.32 = (bf16[80,1920]{1,0:T(8,128)(2,1)}, bf16[80,1920]{1,0:T(8,128)(2,1)S(1)}, u32[]{:S(2)}, u32[]{:S(2)}) collective-permute-start(bf16[80,1920]{1,0:T(8,128)(2,1)} %get-tuple-element.177), channel_id=1, source_target_pairs={{0,2},{2,0},{4,6},{6,4},{8,10},{10,8},{12,14},{14,12},{16,18},{18,... | collective-permute-start | bytes 921608 | tf_op jit(solution)/shard_map/ppermute | solution.py:257
  116.2 5.0 %collective-permute-start.31 = (bf16[80,1920]{1,0:T(8,128)(2,1)}, bf16[80,1920]{1,0:T(8,128)(2,1)}, u32[]{:S(2)}, u32[]{:S(2)}) collective-permute-start(bf16[80,1920]{1,0:T(8,128)(2,1)} %get-tuple-element.166), channel_id=1, source_target_pairs={{0,2},{2,0},{4,6},{6,4},{8,10},{10,8},{12,14},{14,12},{16,18},{18,... | collective-permute-start | bytes 921608 | tf_op jit(solution)/shard_map/ppermute | solution.py:257
  116.3 34.8 %collective-permute-start.44 = (bf16[160,1920]{1,0:T(8,128)(2,1)}, bf16[160,1920]{1,0:T(8,128)(2,1)}, u32[]{:S(2)}, u32[]{:S(2)}) collective-permute-start(bf16[160,1920]{1,0:T(8,128)(2,1)} %get-tuple-element.208), channel_id=1, source_target_pairs={{0,2},{2,0},{4,6},{6,4},{8,10},{10,8},{12,14},{14,12},{16,18},{18,... | collective-permute-start | bytes 1843208 | tf_op jit(solution)/shard_map/ppermute | solution.py:257
  116.9 21.1 %collective-permute-start.37 = (bf16[160,1920]{1,0:T(8,128)(2,1)}, bf16[160,1920]{1,0:T(8,128)(2,1)S(1)}, u32[]{:S(2)}, u32[]{:S(2)}) collective-permute-start(bf16[160,1920]{1,0:T(8,128)(2,1)} %get-tuple-element.183), channel_id=1, source_target_pairs={{0,2},{2,0},{4,6},{6,4},{8,10},{10,8},{12,14},{14,12},{16,18},{18,... | collective-permute-start | bytes 1843208 | tf_op jit(solution)/shard_map/ppermute | solution.py:257
  119.8 15.4 %collective-permute-start.33 = (bf16[80,1920]{1,0:T(8,128)(2,1)S(1)}, bf16[80,1920]{1,0:T(8,128)(2,1)S(1)}, u32[]{:S(2)}, u32[]{:S(2)}) collective-permute-start(bf16[80,1920]{1,0:T(8,128)(2,1)S(1)} %shard_map.209), channel_id=1, source_target_pairs={{0,1},{1,0},{2,3},{3,2},{4,5},{5,4},{6,7},{7,6},{8,9},{9,8},{10,11... | collective-permute-start | bytes 921608 | tf_op jit(solution)/shard_map/ppermute | solution.py:265
  121.3 21.1 %collective-permute-start.35 = (bf16[160,1920]{1,0:T(8,128)(2,1)S(1)}, bf16[160,1920]{1,0:T(8,128)(2,1)S(1)}, u32[]{:S(2)}, u32[]{:S(2)}) collective-permute-start(bf16[160,1920]{1,0:T(8,128)(2,1)S(1)} %shard_map.210), channel_id=1, source_target_pairs={{0,1},{1,0},{2,3},{3,2},{4,5},{5,4},{6,7},{7,6},{8,9},{9,8},{10,11... | collective-permute-start | bytes 1843208 | tf_op jit(solution)/shard_map/ppermute | solution.py:265
  136.4 15.9 %collective-permute-start.38 = (bf16[80,1920]{1,0:T(8,128)(2,1)S(1)}, bf16[80,1920]{1,0:T(8,128)(2,1)}, u32[]{:S(2)}, u32[]{:S(2)}) collective-permute-start(bf16[80,1920]{1,0:T(8,128)(2,1)S(1)} %shard_map.213), channel_id=1, source_target_pairs={{0,8},{8,16},{16,24},{24,28},{28,20},{20,12},{12,4},{4,0},{2,6},{1... | collective-permute-start | bytes 921608 | tf_op jit(solution)/shard_map/ppermute | solution.py:261
  150.3 4.7 %collective-permute-start.42 = (f32[2,1920]{1,0:T(2,128)S(1)}, f32[2,1920]{1,0:T(2,128)S(1)}, u32[]{:S(2)}, u32[]{:S(2)}) collective-permute-start(f32[2,1920]{1,0:T(2,128)S(1)} %fusion.10), channel_id=1, source_target_pairs={{0,2},{2,0},{4,6},{6,4},{8,10},{10,8},{12,14},{14,12},{16,18},{18,... | collective-permute-start | bytes 46088 | tf_op jit(solution)/shard_map/ppermute | solution.py:257
  150.5 9.0 %collective-permute-start.52 = (bf16[240,1920]{1,0:T(8,128)(2,1)}, bf16[240,1920]{1,0:T(8,128)(2,1)S(1)}, u32[]{:S(2)}, u32[]{:S(2)}) collective-permute-start(bf16[240,1920]{1,0:T(8,128)(2,1)} %get-tuple-element.216), channel_id=1, source_target_pairs={{0,2},{2,0},{4,6},{6,4},{8,10},{10,8},{12,14},{14,12},{16,18},{18,... | collective-permute-start | bytes 2764808 | tf_op jit(solution)/shard_map/ppermute | solution.py:257
  151.0 20.1 %collective-permute-start.49 = (bf16[160,1920]{1,0:T(8,128)(2,1)}, bf16[160,1920]{1,0:T(8,128)(2,1)S(1)}, u32[]{:S(2)}, u32[]{:S(2)}) collective-permute-start(bf16[160,1920]{1,0:T(8,128)(2,1)} %get-tuple-element.214), channel_id=1, source_target_pairs={{0,2},{2,0},{4,6},{6,4},{8,10},{10,8},{12,14},{14,12},{16,18},{18,... | collective-permute-start | bytes 1843208 | tf_op jit(solution)/shard_map/ppermute | solution.py:257
  151.1 20.1 %collective-permute-start.50 = (bf16[160,1920]{1,0:T(8,128)(2,1)S(1)}, bf16[160,1920]{1,0:T(8,128)(2,1)S(1)}, u32[]{:S(2)}, u32[]{:S(2)}) collective-permute-start(bf16[160,1920]{1,0:T(8,128)(2,1)S(1)} %shard_map.211), channel_id=1, source_target_pairs={{0,1},{1,0},{2,3},{3,2},{4,5},{5,4},{6,7},{7,6},{8,9},{9,8},{10,11... | collective-permute-start | bytes 1843208 | tf_op jit(solution)/shard_map/ppermute | solution.py:265
  153.8 12.1 %collective-permute-start.45 = (bf16[160,1920]{1,0:T(8,128)(2,1)S(1)}, bf16[160,1920]{1,0:T(8,128)(2,1)S(1)}, u32[]{:S(2)}, u32[]{:S(2)}) collective-permute-start(bf16[160,1920]{1,0:T(8,128)(2,1)S(1)} %shard_map.215), channel_id=1, source_target_pairs={{0,8},{8,16},{16,24},{24,28},{28,20},{20,12},{12,4},{4,0},{2,6},{1... | collective-permute-start | bytes 1843208 | tf_op jit(solution)/shard_map/ppermute | solution.py:261
  155.1 3.8 %collective-permute-start.41 = (bf16[80,1920]{1,0:T(8,128)(2,1)S(1)}, bf16[80,1920]{1,0:T(8,128)(2,1)S(1)}, u32[]{:S(2)}, u32[]{:S(2)}) collective-permute-start(bf16[80,1920]{1,0:T(8,128)(2,1)S(1)} %copy-done.48), channel_id=1, source_target_pairs={{0,2},{2,0},{4,6},{6,4},{8,10},{10,8},{12,14},{14,12},{16,18},{18,... | collective-permute-start | bytes 921608 | tf_op jit(solution)/shard_map/ppermute | solution.py:257
  158.9 11.0 %collective-permute-start.40 = (bf16[160,1920]{1,0:T(8,128)(2,1)S(1)}, bf16[160,1920]{1,0:T(8,128)(2,1)S(1)}, u32[]{:S(2)}, u32[]{:S(2)}) collective-permute-start(bf16[160,1920]{1,0:T(8,128)(2,1)S(1)} %copy-done.47), channel_id=1, source_target_pairs={{0,2},{2,0},{4,6},{6,4},{8,10},{10,8},{12,14},{14,12},{16,18},{18,... | collective-permute-start | bytes 1843208 | tf_op jit(solution)/shard_map/ppermute | solution.py:257
  159.5 10.4 %collective-permute-start.43 = (bf16[96,1920]{1,0:T(8,128)(2,1)S(1)}, bf16[96,1920]{1,0:T(8,128)(2,1)S(1)}, u32[]{:S(2)}, u32[]{:S(2)}) collective-permute-start(bf16[96,1920]{1,0:T(8,128)(2,1)S(1)} %shard_map.214), channel_id=1, source_target_pairs={{0,8},{8,16},{16,24},{24,28},{28,20},{20,12},{12,4},{4,0},{2,6},{1... | collective-permute-start | bytes 1105928 | tf_op jit(solution)/shard_map/ppermute | solution.py:261
  165.9 23.4 %collective-permute-start.53 = (bf16[240,1920]{1,0:T(8,128)(2,1)S(1)}, bf16[240,1920]{1,0:T(8,128)(2,1)S(1)}, u32[]{:S(2)}, u32[]{:S(2)}) collective-permute-start(bf16[240,1920]{1,0:T(8,128)(2,1)S(1)} %shard_map.219), channel_id=1, source_target_pairs={{0,1},{1,0},{2,3},{3,2},{4,5},{5,4},{6,7},{7,6},{8,9},{9,8},{10,11... | collective-permute-start | bytes 2764808 | tf_op jit(solution)/shard_map/ppermute | solution.py:265
  170.1 10.9 %collective-permute-start.46 = (bf16[176,1920]{1,0:T(8,128)(2,1)S(1)}, bf16[176,1920]{1,0:T(8,128)(2,1)S(1)}, u32[]{:S(2)}, u32[]{:S(2)}) collective-permute-start(bf16[176,1920]{1,0:T(8,128)(2,1)S(1)} %shard_map.216), channel_id=1, source_target_pairs={{0,8},{8,16},{16,24},{24,28},{28,20},{20,12},{12,4},{4,0},{2,6},{1... | collective-permute-start | bytes 2027528 | tf_op jit(solution)/shard_map/ppermute | solution.py:261
  170.1 2.7 %collective-permute-start.39 = (bf16[160,1920]{1,0:T(8,128)(2,1)S(1)}, bf16[160,1920]{1,0:T(8,128)(2,1)S(1)}, u32[]{:S(2)}, u32[]{:S(2)}) collective-permute-start(bf16[160,1920]{1,0:T(8,128)(2,1)S(1)} %copy-done.46), channel_id=1, source_target_pairs={{0,2},{2,0},{4,6},{6,4},{8,10},{10,8},{12,14},{14,12},{16,18},{18,... | collective-permute-start | bytes 1843208 | tf_op jit(solution)/shard_map/ppermute | solution.py:257
  171.2 18.2 %collective-permute-start.60 = (bf16[160,1920]{1,0:T(8,128)(2,1)S(1)}, bf16[160,1920]{1,0:T(8,128)(2,1)S(1)}, u32[]{:S(2)}, u32[]{:S(2)}) collective-permute-start(bf16[160,1920]{1,0:T(8,128)(2,1)S(1)} %copy-done.45), channel_id=1, source_target_pairs={{0,2},{2,0},{4,6},{6,4},{8,10},{10,8},{12,14},{14,12},{16,18},{18,... | collective-permute-start | bytes 1843208 | tf_op jit(solution)/shard_map/ppermute | solution.py:257
  171.6 17.7 %collective-permute-start.51 = (bf16[160,1920]{1,0:T(8,128)(2,1)S(1)}, bf16[160,1920]{1,0:T(8,128)(2,1)S(1)}, u32[]{:S(2)}, u32[]{:S(2)}) collective-permute-start(bf16[160,1920]{1,0:T(8,128)(2,1)S(1)} %shard_map.218), channel_id=1, source_target_pairs={{0,8},{8,16},{16,24},{24,28},{28,20},{20,12},{12,4},{4,0},{2,6},{1... | collective-permute-start | bytes 1843208 | tf_op jit(solution)/shard_map/ppermute | solution.py:261
  181.2 13.6 %collective-permute-start.47 = (bf16[176,1920]{1,0:T(8,128)(2,1)S(1)}, bf16[176,1920]{1,0:T(8,128)(2,1)S(1)}, u32[]{:S(2)}, u32[]{:S(2)}) collective-permute-start(bf16[176,1920]{1,0:T(8,128)(2,1)S(1)} %shard_map.217), channel_id=1, source_target_pairs={{0,8},{8,16},{16,24},{24,28},{28,20},{20,12},{12,4},{4,0},{2,6},{1... | collective-permute-start | bytes 2027528 | tf_op jit(solution)/shard_map/ppermute | solution.py:261
  181.2 21.3 %collective-permute-start.36 = (bf16[256,1280]{1,0:T(8,128)(2,1)}, bf16[256,1280]{1,0:T(8,128)(2,1)}, u32[]{:S(2)}, u32[]{:S(2)}) collective-permute-start(bf16[256,1280]{1,0:T(8,128)(2,1)} %get-tuple-element.181), channel_id=1, source_target_pairs={{0,1},{1,0},{2,3},{3,2},{4,5},{5,4},{6,7},{7,6},{8,9},{9,8},{10,11... | collective-permute-start | bytes 1966088 | tf_op jit(solution)/shard_map/ppermute | solution.py:265
  189.3 5.5 %collective-permute-start.48 = (bf16[160,1920]{1,0:T(8,128)(2,1)}, bf16[160,1920]{1,0:T(8,128)(2,1)S(1)}, u32[]{:S(2)}, u32[]{:S(2)}) collective-permute-start(bf16[160,1920]{1,0:T(8,128)(2,1)} %get-tuple-element.212), channel_id=1, source_target_pairs={{0,2},{2,0},{4,6},{6,4},{8,10},{10,8},{12,14},{14,12},{16,18},{18,... | collective-permute-start | bytes 1843208 | tf_op jit(solution)/shard_map/ppermute | solution.py:257
  190.5 10.9 %collective-permute-start.61 = (bf16[160,1920]{1,0:T(8,128)(2,1)}, bf16[160,1920]{1,0:T(8,128)(2,1)}, u32[]{:S(2)}, u32[]{:S(2)}) collective-permute-start(bf16[160,1920]{1,0:T(8,128)(2,1)} %shard_map.221), channel_id=1, source_target_pairs={{0,8},{8,16},{16,24},{24,28},{28,20},{20,12},{12,4},{4,0},{2,6},{1... | collective-permute-start | bytes 1843208 | tf_op jit(solution)/shard_map/ppermute | solution.py:261
  190.5 19.0 %collective-permute-start.59 = (bf16[80,1920]{1,0:T(8,128)(2,1)}, bf16[80,1920]{1,0:T(8,128)(2,1)S(1)}, u32[]{:S(2)}, u32[]{:S(2)}) collective-permute-start(bf16[80,1920]{1,0:T(8,128)(2,1)} %get-tuple-element.221), channel_id=1, source_target_pairs={{0,2},{2,0},{4,6},{6,4},{8,10},{10,8},{12,14},{14,12},{16,18},{18,... | collective-permute-start | bytes 921608 | tf_op jit(solution)/shard_map/ppermute | solution.py:257
  194.8 21.1 %collective-permute-start.57 = (bf16[80,1920]{1,0:T(8,128)(2,1)}, bf16[80,1920]{1,0:T(8,128)(2,1)S(1)}, u32[]{:S(2)}, u32[]{:S(2)}) collective-permute-start(bf16[80,1920]{1,0:T(8,128)(2,1)} %get-tuple-element.219), channel_id=1, source_target_pairs={{0,2},{2,0},{4,6},{6,4},{8,10},{10,8},{12,14},{14,12},{16,18},{18,... | collective-permute-start | bytes 921608 | tf_op jit(solution)/shard_map/ppermute | solution.py:257
  195.0 13.6 %collective-permute-start.54 = (bf16[176,1920]{1,0:T(8,128)(2,1)S(1)}, bf16[176,1920]{1,0:T(8,128)(2,1)S(1)}, u32[]{:S(2)}, u32[]{:S(2)}) collective-permute-start(bf16[176,1920]{1,0:T(8,128)(2,1)S(1)} %shard_map.220), channel_id=1, source_target_pairs={{0,8},{8,16},{16,24},{24,28},{28,20},{20,12},{12,4},{4,0},{2,6},{1... | collective-permute-start | bytes 2027528 | tf_op jit(solution)/shard_map/ppermute | solution.py:261
  202.4 7.1 %collective-permute-start.62 = (bf16[80,1920]{1,0:T(8,128)(2,1)S(1)}, bf16[80,1920]{1,0:T(8,128)(2,1)S(1)}, u32[]{:S(2)}, u32[]{:S(2)}) collective-permute-start(bf16[80,1920]{1,0:T(8,128)(2,1)S(1)} %slice.87), channel_id=1, source_target_pairs={{0,2},{2,0},{4,6},{6,4},{8,10},{10,8},{12,14},{14,12},{16,18},{18,... | collective-permute-start | bytes 921608 | tf_op jit(solution)/shard_map/ppermute | solution.py:257
  209.5 1.4 collective-permute-start.55
  210.9 3.8 %collective-permute-start.56 = (f32[2,1920]{1,0:T(2,128)S(1)}, f32[2,1920]{1,0:T(2,128)S(1)}, u32[]{:S(2)}, u32[]{:S(2)}) collective-permute-start(f32[2,1920]{1,0:T(2,128)S(1)} %add_add_fusion), channel_id=1, source_target_pairs={{0,1},{1,0},{2,3},{3,2},{4,5},{5,4},{6,7},{7,6},{8,9},{9,8},{10,11... | collective-permute-start | bytes 46088 | tf_op jit(solution)/shard_map/ppermute | solution.py:265
  212.7 3.1 %collective-permute-start.58 = (bf16[80,1920]{1,0:T(8,128)(2,1)S(1)}, bf16[80,1920]{1,0:T(8,128)(2,1)S(1)}, u32[]{:S(2)}, u32[]{:S(2)}) collective-permute-start(bf16[80,1920]{1,0:T(8,128)(2,1)S(1)} %slice.105), channel_id=1, source_target_pairs={{0,2},{2,0},{4,6},{6,4},{8,10},{10,8},{12,14},{14,12},{16,18},{18,... | collective-permute-start | bytes 921608 | tf_op jit(solution)/shard_map/ppermute | solution.py:257
  (50 other events, 450.0 us)

commit v4 on v3

--- a/solution.py
+++ b/solution.py
@@ -243,7 +243,7 @@
 )
 VMEM = pl.BlockSpec(memory_space=pltpu.VMEM)
 HELD = pl.BlockSpec(memory_space=pltpu.VMEM)
-LIMIT = 30 * 2**20
+LIMIT = 24 * 2**20
 UNROLL = (4, 8)
 SMEM = pl.BlockSpec(memory_space=pltpu.SMEM)
 ANY = pl.BlockSpec(memory_space=pl.ANY)

time: 220 us -> 220 us (level)
  no operation moved by 1% of the time
where the time goes in v4:
time: 220 us; the launch traced here: 217 us
  waiting for transfers between devices  96.7 us (44%)
  Pallas kernels  55.9 us (25%)
  starting transfers between devices  43.3 us (20%)
  other arithmetic  10.3 us (5%)
  local copies, waits for them, and re-layouts  8.57 us (4%)
    pallas_call x19, Pallas kernels, call(): pl.pallas_call(body, out_shape=[place[id(space)](out.shape, out.dtype) fo...  55.9 us
    ppermute x14, waiting for transfers between devices, across(): return lax.ppermute(value, 'tp', ((0, 1), (1, 0)))  46.2 us
    ppermute x16, waiting for transfers between devices, around(): return lax.ppermute(value, 'fsdp', AROUND)  41.7 us
    ppermute x16, starting transfers between devices, around(): return lax.ppermute(value, 'fsdp', AROUND)  16.8 us
    ppermute x14, starting transfers between devices, across(): return lax.ppermute(value, 'tp', ((0, 1), (1, 0)))  15.4 us
    ppermute x33, starting transfers between devices, sibling(): return lax.ppermute(value, 'fsdp', CORES)  11.2 us
    ppermute x33, waiting for transfers between devices, sibling(): return lax.ppermute(value, 'fsdp', CORES)  8.72 us
  transfers between devices with their start and end apart: 63, of which 29 were waited for; matrix products, arithmetic and copies ran while one was open for 7% of the time, Pallas kernels for 21%

profile of v4, /device:TPU:0, one launch (start us, length us, event | category | flops | bytes accessed | tf_op | source)
XLA Modules:
  0.0 216.6 jit_solution(1371763398110046279)
XLA Ops:
  0.6 2.0 shard_map.203
  3.1 1.4 collective-permute-done.rest_1_
  4.9 2.6 %collective-permute-start.5 = (bf16[256,1280]{1,0:T(8,128)(2,1)}, bf16[256,1280]{1,0:T(8,128)(2,1)S(1)}, u32[]{:S(2)}, u32[]{:S(2)}) collective-permute-start(bf16[256,1280]{1,0:T(8,128)(2,1)} %tokens_in.1), channel_id=1, source_target_pairs={{0,1},{1,0},{2,3},{3,2},{4,5},{5,4},{6,7},{7,6},{8,9},{9,8},{10,11... | collective-permute-start | bytes 1966088 | tf_op jit(solution)/shard_map/ppermute | solution.py:265
  7.5 1.0 pad_maximum_fusion.1
  8.6 1.6 collective-permute-start.6
  10.3 1.6 collective-permute-start.2
  11.9 11.1 %collective-permute-done.5.other_in = bf16[256,1280]{1,0:T(8,128)(2,1)S(1)} collective-permute-done((bf16[256,1280]{1,0:T(8,128)(2,1)}, bf16[256,1280]{1,0:T(8,128)(2,1)S(1)}, u32[]{:S(2)}, u32[]{:S(2)}) %collective-permute-start.5) | collective-permute-done | bytes 655392 | tf_op jit(solution)/shard_map/ppermute | solution.py:265
  23.0 1.8 collective-permute-start.7
  25.4 1.6 collective-permute-start.3
  28.4 1.1 collective-permute-start.10
  29.5 7.6 %collective-permute-done.8.rest_10_ = bf16[80,1920]{1,0:T(8,128)(2,1)S(1)} collective-permute-done((bf16[80,1920]{1,0:T(8,128)(2,1)S(1)}, bf16[80,1920]{1,0:T(8,128)(2,1)S(1)}, u32[]{:S(2)}, u32[]{:S(2)}) %collective-permute-start.8) | collective-permute-done | bytes 307232 | tf_op jit(solution)/shard_map/ppermute | solution.py:265
  37.1 1.6 collective-permute-start.9
  38.7 1.3 collective-permute-done.3.rest_3_
  40.1 1.8 collective-permute-start.12
  41.9 1.8 fusion.2.normed
  43.7 3.9 %collective-permute-done.9.rest_4_ = bf16[160,1920]{1,0:T(8,128)(2,1)} collective-permute-done((bf16[160,1920]{1,0:T(8,128)(2,1)}, bf16[160,1920]{1,0:T(8,128)(2,1)}, u32[]{:S(2)}, u32[]{:S(2)}) %collective-permute-start.9) | collective-permute-done | bytes 614432 | tf_op jit(solution)/shard_map/ppermute | solution.py:261
  47.6 1.0 slice.92
  48.6 1.6 collective-permute-start.11
  51.2 2.8 %collective-permute-done.12.rest_4_ = bf16[160,1920]{1,0:T(8,128)(2,1)S(1)} collective-permute-done((bf16[160,1920]{1,0:T(8,128)(2,1)}, bf16[160,1920]{1,0:T(8,128)(2,1)S(1)}, u32[]{:S(2)}, u32[]{:S(2)}) %collective-permute-start.12) | collective-permute-done | bytes 614432 | tf_op jit(solution)/shard_map/ppermute | solution.py:261
  54.1 1.8 collective-permute-start.13
  55.9 1.6 collective-permute-done.11.rest_5_
  57.5 3.7 %collective-permute-done.13.rest_5_ = bf16[80,1920]{1,0:T(8,128)(2,1)S(1)} collective-permute-done((bf16[80,1920]{1,0:T(8,128)(2,1)S(1)}, bf16[80,1920]{1,0:T(8,128)(2,1)S(1)}, u32[]{:S(2)}, u32[]{:S(2)}) %collective-permute-start.13) | collective-permute-done | bytes 307232 | tf_op jit(solution)/shard_map/ppermute | solution.py:261
  61.5 3.2 %collective-permute-done.4.rest_13_ = bf16[160,1920]{1,0:T(8,128)(2,1)} collective-permute-done((bf16[160,1920]{1,0:T(8,128)(2,1)}, bf16[160,1920]{1,0:T(8,128)(2,1)}, u32[]{:S(2)}, u32[]{:S(2)}) %collective-permute-start.4) | collective-permute-done | bytes 614432 | tf_op jit(solution)/shard_map/ppermute | solution.py:265
  64.7 1.1 collective-permute-start.24
  66.8 10.9 %shard_map.204 = (bf16[640,256]{1,0:T(8,128)(2,1)S(1)}, bf16[640,256]{1,0:T(8,128)(2,1)S(1)}, f32[8,1,512]{2,1,0:T(1,128)S(1)}, bf16[1920,512]{1,0:T(8,128)(2,1)}, bf16[1280,1920]{1,0:T(8,128)(2,1)}) custom-call(s32[17]{0:T(128)S(1)} %stack.71.order, s32[1,8]{1,0:T(1,128)S(1)} %copy-done.24, f32[1,640]{1,0:T(1,128)S(1)} %broadcast_in_dim_tile.3.scaling, ...), custom_call_target="tpu_custom_call" | custom-call | flops 32000000000 | bytes 4194304 | tf_op jit(solution)/shard_map/pallas_call | solution.py:713
  77.7 3.5 %collective-permute-done.24.rest_14_ = bf16[160,1920]{1,0:T(8,128)(2,1)S(1)} collective-permute-done((bf16[160,1920]{1,0:T(8,128)(2,1)S(1)}, bf16[160,1920]{1,0:T(8,128)(2,1)S(1)}, u32[]{:S(2)}, u32[]{:S(2)}) %collective-permute-start.24) | collective-permute-done | bytes 614432 | tf_op jit(solution)/shard_map/ppermute | solution.py:265
  81.7 2.8 %collective-permute-done.25.rest_15_ = bf16[80,1920]{1,0:T(8,128)(2,1)S(1)} collective-permute-done((bf16[80,1920]{1,0:T(8,128)(2,1)S(1)}, bf16[80,1920]{1,0:T(8,128)(2,1)S(1)}, u32[]{:S(2)}, u32[]{:S(2)}) %collective-permute-start.25) | collective-permute-done | bytes 307232 | tf_op jit(solution)/shard_map/ppermute | solution.py:265
  85.1 1.0 collective-permute-done.26.rest_16_
  87.1 1.3 collective-permute-start.18
  88.3 1.9 collective-permute-done.21.rest_8_
  90.3 3.4 %shard_map.205.weights = bf16[2,1280,1920]{2,1,0:T(8,128)(2,1)S(1)} custom-call(s32[17]{0:T(128)S(1)} %stack.71.order, bf16[80,1920]{1,0:T(8,128)(2,1)} %get-tuple-element.123.rest_0_, bf16[80,1920]{1,0:T(8,128)(2,1)} %copy-done.34, bf16[160,1920]{1,0:T(8,128)(2,1)S(1)} %collective-permute-done.2.rest_2_, bf16[160,1920]{1,0:T(8,128)(2,1)} %collective-permute-done.3.rest_3_, ...), custom_call_target="tpu_custom_call" | custom-call | flops 4000000 | bytes 4194304 | tf_op jit(solution)/shard_map/pallas_call | solution.py:713
  93.7 3.1 %collective-permute-done.18.came = bf16[640,256]{1,0:T(8,128)(2,1)S(1)} collective-permute-done((bf16[640,256]{1,0:T(8,128)(2,1)S(1)}, bf16[640,256]{1,0:T(8,128)(2,1)S(1)}, u32[]{:S(2)}, u32[]{:S(2)}) %collective-permute-start.18) | collective-permute-done | bytes 327712 | tf_op jit(solution)/shard_map/ppermute | solution.py:265
  96.8 8.5 %shard_map.206 = (bf16[640,256]{1,0:T(8,128)(2,1)S(1)}, bf16[640,256]{1,0:T(8,128)(2,1)S(1)}, bf16[256,1280]{1,0:T(8,128)(2,1)S(1)}, bf16[256,1280]{1,0:T(8,128)...) custom-call(bf16[256,1280]{1,0:T(8,128)(2,1)S(1)} %copy-done, ...), custom_call_target="tpu_custom_call" | custom-call | flops 32000000000 | bytes 4194304 | tf_op jit(solution)/shard_map/pallas_call | solution.py:713
  105.3 1.3 collective-permute-start.30
  106.6 6.4 %shard_map.207 = (bf16[80,1920]{1,0:T(8,128)(2,1)}, bf16[160,1920]{1,0:T(8,128)(2,1)}, bf16[160,1920]{1,0:T(8,128)(2,1)}, bf16[160,1920]{1,0:T(8,128)(2,1)}, bf1...) custom-call(s32[17]{0:T(128)S(1)} %stack.71.order, ...), custom_call_target="tpu_custom_call" | custom-call | flops 24000000000 | bytes 4194304 | tf_op jit(solution)/shard_map/pallas_call | solution.py:713
  113.1 1.2 collective-permute-done.30.came
  116.3 1.8 collective-permute-done.32.other
  119.2 1.3 collective-permute-start.33
  121.6 12.5 %shard_map.208 = (f32[80,1]{1,0:T(8,128)S(1)}, f32[1,1280]{1,0:T(1,128)S(1)}, bf16[512,1920]{1,0:T(8,128)(2,1)}, f32[256,1280]{1,0:T(8,128)}, bf16[256,1280]{1,0:T(8,128)(2,1)}) custom-call(s32[17]{0:T(128)S(1)} %stack.71.order, s32[1,8]{1,0:T(1,128)S(1)} %copy-done.25, f32[80,1]{1,0:T(8,128)S(1)} %copy.24.scaling_col, bf16[640,256]{1,0:T(8,128)(2,1)S(1)} %copy-done.27, ...), custom_call_target="tpu_custom_call" | custom-call | flops 48000000000 | bytes 4194304 | tf_op jit(solution)/shard_map/pallas_call | solution.py:713
  134.6 1.1 shard_map.213
  135.8 1.5 collective-permute-start.38
  137.5 4.3 %collective-permute-done.35.rest_2_ = bf16[160,1920]{1,0:T(8,128)(2,1)S(1)} collective-permute-done((bf16[160,1920]{1,0:T(8,128)(2,1)S(1)}, bf16[160,1920]{1,0:T(8,128)(2,1)S(1)}, u32[]{:S(2)}, u32[]{:S(2)}) %collective-permute-start.35) | collective-permute-done | bytes 614432 | tf_op jit(solution)/shard_map/ppermute | solution.py:265
  142.6 6.9 %shard_map.212 = (bf16[80,1920]{1,0:T(8,128)(2,1)}, bf16[160,1920]{1,0:T(8,128)(2,1)}, bf16[160,1920]{1,0:T(8,128)(2,1)}, bf16[160,1920]{1,0:T(8,128)(2,1)}, bf1...) custom-call(s32[17]{0:T(128)S(1)} %stack.71.order, ...), custom_call_target="tpu_custom_call" | custom-call | flops 20000000000 | bytes 4194304 | tf_op jit(solution)/shard_map/pallas_call | solution.py:713
  150.5 1.3 collective-permute-start.50
  151.8 1.4 shard_map.215
  153.2 1.2 collective-permute-start.45
  154.4 2.6 %collective-permute-start.41 = (bf16[80,1920]{1,0:T(8,128)(2,1)S(1)}, bf16[80,1920]{1,0:T(8,128)(2,1)S(1)}, u32[]{:S(2)}, u32[]{:S(2)}) collective-permute-start(bf16[80,1920]{1,0:T(8,128)(2,1)S(1)} %copy-done.48), channel_id=1, source_target_pairs={{0,2},{2,0},{4,6},{6,4},{8,10},{10,8},{12,14},{14,12},{16,18},{18,... | collective-permute-start | bytes 921608 | tf_op jit(solution)/shard_map/ppermute | solution.py:257
  157.1 1.2 collective-permute-done.41.came
  159.2 6.1 %collective-permute-done.45.rest_3_ = bf16[160,1920]{1,0:T(8,128)(2,1)S(1)} collective-permute-done((bf16[160,1920]{1,0:T(8,128)(2,1)S(1)}, bf16[160,1920]{1,0:T(8,128)(2,1)S(1)}, u32[]{:S(2)}, u32[]{:S(2)}) %collective-permute-start.45) | collective-permute-done | bytes 614432 | tf_op jit(solution)/shard_map/ppermute | solution.py:261
  165.6 3.7 %collective-permute-done.43.rest_2_ = bf16[96,1920]{1,0:T(8,128)(2,1)S(1)} collective-permute-done((bf16[96,1920]{1,0:T(8,128)(2,1)S(1)}, bf16[96,1920]{1,0:T(8,128)(2,1)S(1)}, u32[]{:S(2)}, u32[]{:S(2)}) %collective-permute-start.43) | collective-permute-done | bytes 368672 | tf_op jit(solution)/shard_map/ppermute | solution.py:261
  169.5 1.0 collective-permute-start.39
  172.2 8.1 %collective-permute-done.46.rest_2_ = bf16[176,1920]{1,0:T(8,128)(2,1)S(1)} collective-permute-done((bf16[176,1920]{1,0:T(8,128)(2,1)S(1)}, bf16[176,1920]{1,0:T(8,128)(2,1)S(1)}, u32[]{:S(2)}, u32[]{:S(2)}) %collective-permute-start.46) | collective-permute-done | bytes 675872 | tf_op jit(solution)/shard_map/ppermute | solution.py:261
  180.9 7.7 %collective-permute-done.53 = bf16[240,1920]{1,0:T(8,128)(2,1)S(1)} collective-permute-done((bf16[240,1920]{1,0:T(8,128)(2,1)S(1)}, bf16[240,1920]{1,0:T(8,128)(2,1)S(1)}, u32[]{:S(2)}, u32[]{:S(2)}) %collective-permute-start.53) | collective-permute-done | bytes 921632 | tf_op jit(solution)/shard_map/ppermute | solution.py:265
  188.7 1.1 shard_map.221
  189.9 2.2 %collective-permute-start.59 = (bf16[80,1920]{1,0:T(8,128)(2,1)}, bf16[80,1920]{1,0:T(8,128)(2,1)S(1)}, u32[]{:S(2)}, u32[]{:S(2)}) collective-permute-start(bf16[80,1920]{1,0:T(8,128)(2,1)} %get-tuple-element.221), channel_id=1, source_target_pairs={{0,2},{2,0},{4,6},{6,4},{8,10},{10,8},{12,14},{14,12},{16,18},{18,... | collective-permute-start | bytes 921608 | tf_op jit(solution)/shard_map/ppermute | solution.py:257
  192.1 2.0 collective-permute-done.47.rest_2_
  194.4 6.4 %collective-permute-done.61 = bf16[160,1920]{1,0:T(8,128)(2,1)} collective-permute-done((bf16[160,1920]{1,0:T(8,128)(2,1)}, bf16[160,1920]{1,0:T(8,128)(2,1)}, u32[]{:S(2)}, u32[]{:S(2)}) %collective-permute-start.61) | collective-permute-done | bytes 614432 | tf_op jit(solution)/shard_map/ppermute | solution.py:261
  200.8 1.0 slice.87
  201.9 1.6 fusion.3
  203.6 2.7 %fusion.6 = f32[256,1280]{1,0:T(8,128)} fusion(f32[256,1280]{1,0:T(8,128)S(1)} %copy-done.32, bf16[256,1280]{1,0:T(8,128)(2,1)S(1)} %copy-done.1, f32[256,1280]{1,0:T(8,128)S(1)} %copy-done.30, bf16[256,1280]{1,0:T(8,128)(2,1)} %collective-permute-done.36, f32[256]{0:T(256)S(1)} %broadcast_multiply_fusion, f32[256]{0:T(256)S(1)} %get-tuple-element.238, ...), kind=kLoop, calls=%fused_computation.11 | loop fusion | flops 2949120 | bytes 5251072 | tf_op jit(solution)/shard_map/add | solution.py:934
  206.3 1.7 collective-permute-done.54
  208.9 1.3 convert_add_fusion
  210.3 1.0 collective-permute-start.56
  212.4 1.7 collective-permute-done.56
  (222 shorter events, 22.2 us)
Async XLA Ops:
  2.6 1.9 collective-permute-start
  4.5 5.7 %collective-permute-start.1 = (bf16[80,1920]{1,0:T(8,128)(2,1)}, bf16[80,1920]{1,0:T(8,128)(2,1)S(1)}, u32[]{:S(2)}, u32[]{:S(2)}) collective-permute-start(bf16[80,1920]{1,0:T(8,128)(2,1)} %get-tuple-element.123.rest_0_), channel_id=1, source_target_pairs={{0,2},{2,0},{4,6},{6,4},{8,10},{10,8},{12,14},{14,12},{16,18},{18,... | collective-permute-start | bytes 921608 | tf_op jit(solution)/shard_map/ppermute | solution.py:257
  4.9 18.1 %collective-permute-start.5 = (bf16[256,1280]{1,0:T(8,128)(2,1)}, bf16[256,1280]{1,0:T(8,128)(2,1)S(1)}, u32[]{:S(2)}, u32[]{:S(2)}) collective-permute-start(bf16[256,1280]{1,0:T(8,128)(2,1)} %tokens_in.1), channel_id=1, source_target_pairs={{0,1},{1,0},{2,3},{3,2},{4,5},{5,4},{6,7},{7,6},{8,9},{9,8},{10,11... | collective-permute-start | bytes 1966088 | tf_op jit(solution)/shard_map/ppermute | solution.py:265
  8.6 33.3 %copy-start.42 = (f32[1280]{0:T(1024)S(1)}, f32[1280]{0:T(1024)}, u32[]{:S(2)}) copy-start(f32[1280]{0:T(1024)} %param.14) | copy-start | bytes 15364
  8.6 14.4 %collective-permute-start.6 = (bf16[160,1920]{1,0:T(8,128)(2,1)S(1)}, bf16[160,1920]{1,0:T(8,128)(2,1)}, u32[]{:S(2)}, u32[]{:S(2)}) collective-permute-start(bf16[160,1920]{1,0:T(8,128)(2,1)S(1)} %pad_maximum_fusion.1), channel_id=1, source_target_pairs={{0,8},{8,16},{16,24},{24,28},{28,20},{20,12},{12,4},{4,0},{2,6},{1... | collective-permute-start | bytes 1843208 | tf_op jit(solution)/shard_map/ppermute | solution.py:261
  10.3 15.1 %collective-permute-start.2 = (bf16[160,1920]{1,0:T(8,128)(2,1)S(1)}, bf16[160,1920]{1,0:T(8,128)(2,1)S(1)}, u32[]{:S(2)}, u32[]{:S(2)}) collective-permute-start(bf16[160,1920]{1,0:T(8,128)(2,1)S(1)} %pad_maximum_fusion), channel_id=1, source_target_pairs={{0,8},{8,16},{16,24},{24,28},{28,20},{20,12},{12,4},{4,0},{2,6},{1... | collective-permute-start | bytes 1843208 | tf_op jit(solution)/shard_map/ppermute | solution.py:261
  23.0 14.1 %collective-permute-start.7 = (bf16[160,1920]{1,0:T(8,128)(2,1)}, bf16[160,1920]{1,0:T(8,128)(2,1)}, u32[]{:S(2)}, u32[]{:S(2)}) collective-permute-start(bf16[160,1920]{1,0:T(8,128)(2,1)} %collective-permute-done.6.rest_2_), channel_id=1, source_target_pairs={{0,8},{8,16},{16,24},{24,28},{28,20},{20,12},{12,4},{4,0},{2,6},{1... | collective-permute-start | bytes 1843208 | tf_op jit(solution)/shard_map/ppermute | solution.py:261
  25.4 14.7 %collective-permute-start.3 = (bf16[160,1920]{1,0:T(8,128)(2,1)S(1)}, bf16[160,1920]{1,0:T(8,128)(2,1)}, u32[]{:S(2)}, u32[]{:S(2)}) collective-permute-start(bf16[160,1920]{1,0:T(8,128)(2,1)S(1)} %collective-permute-done.2.rest_2_), channel_id=1, source_target_pairs={{0,8},{8,16},{16,24},{24,28},{28,20},{20,12},{12,4},{4,0},{2,6},{1... | collective-permute-start | bytes 1843208 | tf_op jit(solution)/shard_map/ppermute | solution.py:261
  26.9 10.2 %collective-permute-start.8 = (bf16[80,1920]{1,0:T(8,128)(2,1)S(1)}, bf16[80,1920]{1,0:T(8,128)(2,1)S(1)}, u32[]{:S(2)}, u32[]{:S(2)}) collective-permute-start(bf16[80,1920]{1,0:T(8,128)(2,1)S(1)} %copy-done.33), channel_id=1, source_target_pairs={{0,1},{1,0},{2,3},{3,2},{4,5},{5,4},{6,7},{7,6},{8,9},{9,8},{10,11... | collective-permute-start | bytes 921608 | tf_op jit(solution)/shard_map/ppermute | solution.py:265
  28.4 20.2 %collective-permute-start.10 = (bf16[160,1920]{1,0:T(8,128)(2,1)S(1)}, bf16[160,1920]{1,0:T(8,128)(2,1)S(1)}, u32[]{:S(2)}, u32[]{:S(2)}) collective-permute-start(bf16[160,1920]{1,0:T(8,128)(2,1)S(1)} %collective-permute-done.2.rest_2_), channel_id=1, source_target_pairs={{0,1},{1,0},{2,3},{3,2},{4,5},{5,4},{6,7},{7,6},{8,9},{9,8},{10,11... | collective-permute-start | bytes 1843208 | tf_op jit(solution)/shard_map/ppermute | solution.py:265
  37.1 10.5 %collective-permute-start.9 = (bf16[160,1920]{1,0:T(8,128)(2,1)}, bf16[160,1920]{1,0:T(8,128)(2,1)}, u32[]{:S(2)}, u32[]{:S(2)}) collective-permute-start(bf16[160,1920]{1,0:T(8,128)(2,1)} %collective-permute-done.7.rest_3_), channel_id=1, source_target_pairs={{0,8},{8,16},{16,24},{24,28},{28,20},{20,12},{12,4},{4,0},{2,6},{1... | collective-permute-start | bytes 1843208 | tf_op jit(solution)/shard_map/ppermute | solution.py:261
  40.1 14.0 %collective-permute-start.12 = (bf16[160,1920]{1,0:T(8,128)(2,1)}, bf16[160,1920]{1,0:T(8,128)(2,1)S(1)}, u32[]{:S(2)}, u32[]{:S(2)}) collective-permute-start(bf16[160,1920]{1,0:T(8,128)(2,1)} %collective-permute-done.3.rest_3_), channel_id=1, source_target_pairs={{0,8},{8,16},{16,24},{24,28},{28,20},{20,12},{12,4},{4,0},{2,6},{1... | collective-permute-start | bytes 1843208 | tf_op jit(solution)/shard_map/ppermute | solution.py:261
  48.6 8.9 %collective-permute-start.11 = (bf16[80,1920]{1,0:T(8,128)(2,1)S(1)}, bf16[80,1920]{1,0:T(8,128)(2,1)}, u32[]{:S(2)}, u32[]{:S(2)}) collective-permute-start(bf16[80,1920]{1,0:T(8,128)(2,1)S(1)} %slice.92), channel_id=1, source_target_pairs={{0,8},{8,16},{16,24},{24,28},{28,20},{20,12},{12,4},{4,0},{2,6},{1... | collective-permute-start | bytes 921608 | tf_op jit(solution)/shard_map/ppermute | solution.py:261
  50.3 14.4 %collective-permute-start.4 = (bf16[160,1920]{1,0:T(8,128)(2,1)}, bf16[160,1920]{1,0:T(8,128)(2,1)}, u32[]{:S(2)}, u32[]{:S(2)}) collective-permute-start(bf16[160,1920]{1,0:T(8,128)(2,1)} %collective-permute-done.3.rest_3_), channel_id=1, source_target_pairs={{0,1},{1,0},{2,3},{3,2},{4,5},{5,4},{6,7},{7,6},{8,9},{9,8},{10,11... | collective-permute-start | bytes 1843208 | tf_op jit(solution)/shard_map/ppermute | solution.py:265
  51.2 14.6 %collective-permute-start.15 = (bf16[160,1920]{1,0:T(8,128)(2,1)}, bf16[160,1920]{1,0:T(8,128)(2,1)}, u32[]{:S(2)}, u32[]{:S(2)}) collective-permute-start(bf16[160,1920]{1,0:T(8,128)(2,1)} %collective-permute-done.6.rest_2_), channel_id=1, source_target_pairs={{0,2},{2,0},{4,6},{6,4},{8,10},{10,8},{12,14},{14,12},{16,18},{18,... | collective-permute-start | bytes 1843208 | tf_op jit(solution)/shard_map/ppermute | solution.py:257
  54.1 7.1 %collective-permute-start.13 = (bf16[80,1920]{1,0:T(8,128)(2,1)S(1)}, bf16[80,1920]{1,0:T(8,128)(2,1)S(1)}, u32[]{:S(2)}, u32[]{:S(2)}) collective-permute-start(bf16[80,1920]{1,0:T(8,128)(2,1)S(1)} %slice.93), channel_id=1, source_target_pairs={{0,8},{8,16},{16,24},{24,28},{28,20},{20,12},{12,4},{4,0},{2,6},{1... | collective-permute-start | bytes 921608 | tf_op jit(solution)/shard_map/ppermute | solution.py:261
  55.9 10.8 %collective-permute-start.16 = (bf16[160,1920]{1,0:T(8,128)(2,1)}, bf16[160,1920]{1,0:T(8,128)(2,1)}, u32[]{:S(2)}, u32[]{:S(2)}) collective-permute-start(bf16[160,1920]{1,0:T(8,128)(2,1)} %collective-permute-done.7.rest_3_), channel_id=1, source_target_pairs={{0,2},{2,0},{4,6},{6,4},{8,10},{10,8},{12,14},{14,12},{16,18},{18,... | collective-permute-start | bytes 1843208 | tf_op jit(solution)/shard_map/ppermute | solution.py:257
  57.5 9.3 %collective-permute-start.17 = (bf16[160,1920]{1,0:T(8,128)(2,1)}, bf16[160,1920]{1,0:T(8,128)(2,1)}, u32[]{:S(2)}, u32[]{:S(2)}) collective-permute-start(bf16[160,1920]{1,0:T(8,128)(2,1)} %collective-permute-done.9.rest_4_), channel_id=1, source_target_pairs={{0,2},{2,0},{4,6},{6,4},{8,10},{10,8},{12,14},{14,12},{16,18},{18,... | collective-permute-start | bytes 1843208 | tf_op jit(solution)/shard_map/ppermute | solution.py:257
  61.2 5.5 %collective-permute-start.14 = (bf16[80,1920]{1,0:T(8,128)(2,1)}, bf16[80,1920]{1,0:T(8,128)(2,1)}, u32[]{:S(2)}, u32[]{:S(2)}) collective-permute-start(bf16[80,1920]{1,0:T(8,128)(2,1)} %collective-permute-done.11.rest_5_), channel_id=1, source_target_pairs={{0,2},{2,0},{4,6},{6,4},{8,10},{10,8},{12,14},{14,12},{16,18},{18,... | collective-permute-start | bytes 921608 | tf_op jit(solution)/shard_map/ppermute | solution.py:257
  64.7 16.5 %collective-permute-start.24 = (bf16[160,1920]{1,0:T(8,128)(2,1)S(1)}, bf16[160,1920]{1,0:T(8,128)(2,1)S(1)}, u32[]{:S(2)}, u32[]{:S(2)}) collective-permute-start(bf16[160,1920]{1,0:T(8,128)(2,1)S(1)} %collective-permute-done.12.rest_4_), channel_id=1, source_target_pairs={{0,1},{1,0},{2,3},{3,2},{4,5},{5,4},{6,7},{7,6},{8,9},{9,8},{10,11... | collective-permute-start | bytes 1843208 | tf_op jit(solution)/shard_map/ppermute | solution.py:265
  65.8 18.7 %collective-permute-start.25 = (bf16[80,1920]{1,0:T(8,128)(2,1)S(1)}, bf16[80,1920]{1,0:T(8,128)(2,1)S(1)}, u32[]{:S(2)}, u32[]{:S(2)}) collective-permute-start(bf16[80,1920]{1,0:T(8,128)(2,1)S(1)} %collective-permute-done.13.rest_5_), channel_id=1, source_target_pairs={{0,1},{1,0},{2,3},{3,2},{4,5},{5,4},{6,7},{7,6},{8,9},{9,8},{10,11... | collective-permute-start | bytes 921608 | tf_op jit(solution)/shard_map/ppermute | solution.py:265
  81.2 5.5 %collective-permute-start.29 = (bf16[160,1920]{1,0:T(8,128)(2,1)S(1)}, bf16[160,1920]{1,0:T(8,128)(2,1)S(1)}, u32[]{:S(2)}, u32[]{:S(2)}) collective-permute-start(bf16[160,1920]{1,0:T(8,128)(2,1)S(1)} %collective-permute-done.24.rest_14_), channel_id=1, source_target_pairs={{0,2},{2,0},{4,6},{6,4},{8,10},{10,8},{12,14},{14,12},{16,18},{18,... | collective-permute-start | bytes 1843208 | tf_op jit(solution)/shard_map/ppermute | solution.py:257
  81.2 5.8 %collective-permute-start.28 = (bf16[160,1920]{1,0:T(8,128)(2,1)}, bf16[160,1920]{1,0:T(8,128)(2,1)S(1)}, u32[]{:S(2)}, u32[]{:S(2)}) collective-permute-start(bf16[160,1920]{1,0:T(8,128)(2,1)} %collective-permute-done.4.rest_13_), channel_id=1, source_target_pairs={{0,2},{2,0},{4,6},{6,4},{8,10},{10,8},{12,14},{14,12},{16,18},{18,... | collective-permute-start | bytes 1843208 | tf_op jit(solution)/shard_map/ppermute | solution.py:257
  81.7 3.3 %collective-permute-start.23 = (bf16[80,1920]{1,0:T(8,128)(2,1)S(1)}, bf16[80,1920]{1,0:T(8,128)(2,1)S(1)}, u32[]{:S(2)}, u32[]{:S(2)}) collective-permute-start(bf16[80,1920]{1,0:T(8,128)(2,1)S(1)} %copy-done.37), channel_id=1, source_target_pairs={{0,2},{2,0},{4,6},{6,4},{8,10},{10,8},{12,14},{14,12},{16,18},{18,... | collective-permute-start | bytes 921608 | tf_op jit(solution)/shard_map/ppermute | solution.py:257
  84.5 1.6 collective-permute-start.26
  84.5 2.0 collective-permute-start.19
  85.0 3.3 %collective-permute-start.27 = (bf16[160,1920]{1,0:T(8,128)(2,1)S(1)}, bf16[160,1920]{1,0:T(8,128)(2,1)S(1)}, u32[]{:S(2)}, u32[]{:S(2)}) collective-permute-start(bf16[160,1920]{1,0:T(8,128)(2,1)S(1)} %copy-done.14), channel_id=1, source_target_pairs={{0,2},{2,0},{4,6},{6,4},{8,10},{10,8},{12,14},{14,12},{16,18},{18,... | collective-permute-start | bytes 1843208 | tf_op jit(solution)/shard_map/ppermute | solution.py:257
  86.1 2.2 %collective-permute-start.22 = (bf16[160,1920]{1,0:T(8,128)(2,1)S(1)}, bf16[160,1920]{1,0:T(8,128)(2,1)S(1)}, u32[]{:S(2)}, u32[]{:S(2)}) collective-permute-start(bf16[160,1920]{1,0:T(8,128)(2,1)S(1)} %collective-permute-done.12.rest_4_), channel_id=1, source_target_pairs={{0,2},{2,0},{4,6},{6,4},{8,10},{10,8},{12,14},{14,12},{16,18},{18,... | collective-permute-start | bytes 1843208 | tf_op jit(solution)/shard_map/ppermute | solution.py:257
  86.5 3.7 %collective-permute-start.21 = (bf16[160,1920]{1,0:T(8,128)(2,1)}, bf16[160,1920]{1,0:T(8,128)(2,1)S(1)}, u32[]{:S(2)}, u32[]{:S(2)}) collective-permute-start(bf16[160,1920]{1,0:T(8,128)(2,1)} %collective-permute-done.3.rest_3_), channel_id=1, source_target_pairs={{0,2},{2,0},{4,6},{6,4},{8,10},{10,8},{12,14},{14,12},{16,18},{18,... | collective-permute-start | bytes 1843208 | tf_op jit(solution)/shard_map/ppermute | solution.py:257
  86.7 3.6 %collective-permute-start.20 = (bf16[160,1920]{1,0:T(8,128)(2,1)S(1)}, bf16[160,1920]{1,0:T(8,128)(2,1)S(1)}, u32[]{:S(2)}, u32[]{:S(2)}) collective-permute-start(bf16[160,1920]{1,0:T(8,128)(2,1)S(1)} %collective-permute-done.2.rest_2_), channel_id=1, source_target_pairs={{0,2},{2,0},{4,6},{6,4},{8,10},{10,8},{12,14},{14,12},{16,18},{18,... | collective-permute-start | bytes 1843208 | tf_op jit(solution)/shard_map/ppermute | solution.py:257
  87.1 9.8 %collective-permute-start.18 = (bf16[640,256]{1,0:T(8,128)(2,1)S(1)}, bf16[640,256]{1,0:T(8,128)(2,1)S(1)}, u32[]{:S(2)}, u32[]{:S(2)}) collective-permute-start(bf16[640,256]{1,0:T(8,128)(2,1)S(1)} %get-tuple-element.128), channel_id=1, source_target_pairs={{0,1},{1,0},{2,3},{3,2},{4,5},{5,4},{6,7},{7,6},{8,9},{9,8},{10,11... | collective-permute-start | bytes 983048 | tf_op jit(solution)/shard_map/ppermute | solution.py:265
  105.3 9.0 %collective-permute-start.30 = (bf16[640,256]{1,0:T(8,128)(2,1)S(1)}, bf16[640,256]{1,0:T(8,128)(2,1)S(1)}, u32[]{:S(2)}, u32[]{:S(2)}) collective-permute-start(bf16[640,256]{1,0:T(8,128)(2,1)S(1)} %get-tuple-element.163), channel_id=1, source_target_pairs={{0,1},{1,0},{2,3},{3,2},{4,5},{5,4},{6,7},{7,6},{8,9},{9,8},{10,11... | collective-permute-start | bytes 983048 | tf_op jit(solution)/shard_map/ppermute | solution.py:265
  115.0 5.5 %collective-permute-start.34 = (bf16[160,1920]{1,0:T(8,128)(2,1)}, bf16[160,1920]{1,0:T(8,128)(2,1)S(1)}, u32[]{:S(2)}, u32[]{:S(2)}) collective-permute-start(bf16[160,1920]{1,0:T(8,128)(2,1)} %get-tuple-element.179), channel_id=1, source_target_pairs={{0,2},{2,0},{4,6},{6,4},{8,10},{10,8},{12,14},{14,12},{16,18},{18,... | collective-permute-start | bytes 1843208 | tf_op jit(solution)/shard_map/ppermute | solution.py:257
  115.0 3.1 %collective-permute-start.32 = (bf16[80,1920]{1,0:T(8,128)(2,1)}, bf16[80,1920]{1,0:T(8,128)(2,1)S(1)}, u32[]{:S(2)}, u32[]{:S(2)}) collective-permute-start(bf16[80,1920]{1,0:T(8,128)(2,1)} %get-tuple-element.177), channel_id=1, source_target_pairs={{0,2},{2,0},{4,6},{6,4},{8,10},{10,8},{12,14},{14,12},{16,18},{18,... | collective-permute-start | bytes 921608 | tf_op jit(solution)/shard_map/ppermute | solution.py:257
  115.5 5.0 %collective-permute-start.31 = (bf16[80,1920]{1,0:T(8,128)(2,1)}, bf16[80,1920]{1,0:T(8,128)(2,1)}, u32[]{:S(2)}, u32[]{:S(2)}) collective-permute-start(bf16[80,1920]{1,0:T(8,128)(2,1)} %get-tuple-element.166), channel_id=1, source_target_pairs={{0,2},{2,0},{4,6},{6,4},{8,10},{10,8},{12,14},{14,12},{16,18},{18,... | collective-permute-start | bytes 921608 | tf_op jit(solution)/shard_map/ppermute | solution.py:257
  115.7 34.8 %collective-permute-start.44 = (bf16[160,1920]{1,0:T(8,128)(2,1)}, bf16[160,1920]{1,0:T(8,128)(2,1)}, u32[]{:S(2)}, u32[]{:S(2)}) collective-permute-start(bf16[160,1920]{1,0:T(8,128)(2,1)} %get-tuple-element.208), channel_id=1, source_target_pairs={{0,2},{2,0},{4,6},{6,4},{8,10},{10,8},{12,14},{14,12},{16,18},{18,... | collective-permute-start | bytes 1843208 | tf_op jit(solution)/shard_map/ppermute | solution.py:257
  116.2 21.1 %collective-permute-start.37 = (bf16[160,1920]{1,0:T(8,128)(2,1)}, bf16[160,1920]{1,0:T(8,128)(2,1)S(1)}, u32[]{:S(2)}, u32[]{:S(2)}) collective-permute-start(bf16[160,1920]{1,0:T(8,128)(2,1)} %get-tuple-element.183), channel_id=1, source_target_pairs={{0,2},{2,0},{4,6},{6,4},{8,10},{10,8},{12,14},{14,12},{16,18},{18,... | collective-permute-start | bytes 1843208 | tf_op jit(solution)/shard_map/ppermute | solution.py:257
  119.2 15.4 %collective-permute-start.33 = (bf16[80,1920]{1,0:T(8,128)(2,1)S(1)}, bf16[80,1920]{1,0:T(8,128)(2,1)S(1)}, u32[]{:S(2)}, u32[]{:S(2)}) collective-permute-start(bf16[80,1920]{1,0:T(8,128)(2,1)S(1)} %shard_map.209), channel_id=1, source_target_pairs={{0,1},{1,0},{2,3},{3,2},{4,5},{5,4},{6,7},{7,6},{8,9},{9,8},{10,11... | collective-permute-start | bytes 921608 | tf_op jit(solution)/shard_map/ppermute | solution.py:265
  120.7 21.1 %collective-permute-start.35 = (bf16[160,1920]{1,0:T(8,128)(2,1)S(1)}, bf16[160,1920]{1,0:T(8,128)(2,1)S(1)}, u32[]{:S(2)}, u32[]{:S(2)}) collective-permute-start(bf16[160,1920]{1,0:T(8,128)(2,1)S(1)} %shard_map.210), channel_id=1, source_target_pairs={{0,1},{1,0},{2,3},{3,2},{4,5},{5,4},{6,7},{7,6},{8,9},{9,8},{10,11... | collective-permute-start | bytes 1843208 | tf_op jit(solution)/shard_map/ppermute | solution.py:265
  135.8 15.9 %collective-permute-start.38 = (bf16[80,1920]{1,0:T(8,128)(2,1)S(1)}, bf16[80,1920]{1,0:T(8,128)(2,1)}, u32[]{:S(2)}, u32[]{:S(2)}) collective-permute-start(bf16[80,1920]{1,0:T(8,128)(2,1)S(1)} %shard_map.213), channel_id=1, source_target_pairs={{0,8},{8,16},{16,24},{24,28},{28,20},{20,12},{12,4},{4,0},{2,6},{1... | collective-permute-start | bytes 921608 | tf_op jit(solution)/shard_map/ppermute | solution.py:261
  149.7 4.8 %collective-permute-start.42 = (f32[2,1920]{1,0:T(2,128)S(1)}, f32[2,1920]{1,0:T(2,128)S(1)}, u32[]{:S(2)}, u32[]{:S(2)}) collective-permute-start(f32[2,1920]{1,0:T(2,128)S(1)} %fusion.10), channel_id=1, source_target_pairs={{0,2},{2,0},{4,6},{6,4},{8,10},{10,8},{12,14},{14,12},{16,18},{18,... | collective-permute-start | bytes 46088 | tf_op jit(solution)/shard_map/ppermute | solution.py:257
  149.9 9.0 %collective-permute-start.52 = (bf16[240,1920]{1,0:T(8,128)(2,1)}, bf16[240,1920]{1,0:T(8,128)(2,1)S(1)}, u32[]{:S(2)}, u32[]{:S(2)}) collective-permute-start(bf16[240,1920]{1,0:T(8,128)(2,1)} %get-tuple-element.216), channel_id=1, source_target_pairs={{0,2},{2,0},{4,6},{6,4},{8,10},{10,8},{12,14},{14,12},{16,18},{18,... | collective-permute-start | bytes 2764808 | tf_op jit(solution)/shard_map/ppermute | solution.py:257
  150.4 20.1 %collective-permute-start.49 = (bf16[160,1920]{1,0:T(8,128)(2,1)}, bf16[160,1920]{1,0:T(8,128)(2,1)S(1)}, u32[]{:S(2)}, u32[]{:S(2)}) collective-permute-start(bf16[160,1920]{1,0:T(8,128)(2,1)} %get-tuple-element.214), channel_id=1, source_target_pairs={{0,2},{2,0},{4,6},{6,4},{8,10},{10,8},{12,14},{14,12},{16,18},{18,... | collective-permute-start | bytes 1843208 | tf_op jit(solution)/shard_map/ppermute | solution.py:257
  150.5 20.1 %collective-permute-start.50 = (bf16[160,1920]{1,0:T(8,128)(2,1)S(1)}, bf16[160,1920]{1,0:T(8,128)(2,1)S(1)}, u32[]{:S(2)}, u32[]{:S(2)}) collective-permute-start(bf16[160,1920]{1,0:T(8,128)(2,1)S(1)} %shard_map.211), channel_id=1, source_target_pairs={{0,1},{1,0},{2,3},{3,2},{4,5},{5,4},{6,7},{7,6},{8,9},{9,8},{10,11... | collective-permute-start | bytes 1843208 | tf_op jit(solution)/shard_map/ppermute | solution.py:265
  153.2 12.1 %collective-permute-start.45 = (bf16[160,1920]{1,0:T(8,128)(2,1)S(1)}, bf16[160,1920]{1,0:T(8,128)(2,1)S(1)}, u32[]{:S(2)}, u32[]{:S(2)}) collective-permute-start(bf16[160,1920]{1,0:T(8,128)(2,1)S(1)} %shard_map.215), channel_id=1, source_target_pairs={{0,8},{8,16},{16,24},{24,28},{28,20},{20,12},{12,4},{4,0},{2,6},{1... | collective-permute-start | bytes 1843208 | tf_op jit(solution)/shard_map/ppermute | solution.py:261
  154.4 3.8 %collective-permute-start.41 = (bf16[80,1920]{1,0:T(8,128)(2,1)S(1)}, bf16[80,1920]{1,0:T(8,128)(2,1)S(1)}, u32[]{:S(2)}, u32[]{:S(2)}) collective-permute-start(bf16[80,1920]{1,0:T(8,128)(2,1)S(1)} %copy-done.48), channel_id=1, source_target_pairs={{0,2},{2,0},{4,6},{6,4},{8,10},{10,8},{12,14},{14,12},{16,18},{18,... | collective-permute-start | bytes 921608 | tf_op jit(solution)/shard_map/ppermute | solution.py:257
  158.3 11.0 %collective-permute-start.40 = (bf16[160,1920]{1,0:T(8,128)(2,1)S(1)}, bf16[160,1920]{1,0:T(8,128)(2,1)S(1)}, u32[]{:S(2)}, u32[]{:S(2)}) collective-permute-start(bf16[160,1920]{1,0:T(8,128)(2,1)S(1)} %copy-done.47), channel_id=1, source_target_pairs={{0,2},{2,0},{4,6},{6,4},{8,10},{10,8},{12,14},{14,12},{16,18},{18,... | collective-permute-start | bytes 1843208 | tf_op jit(solution)/shard_map/ppermute | solution.py:257
  158.8 10.4 %collective-permute-start.43 = (bf16[96,1920]{1,0:T(8,128)(2,1)S(1)}, bf16[96,1920]{1,0:T(8,128)(2,1)S(1)}, u32[]{:S(2)}, u32[]{:S(2)}) collective-permute-start(bf16[96,1920]{1,0:T(8,128)(2,1)S(1)} %shard_map.214), channel_id=1, source_target_pairs={{0,8},{8,16},{16,24},{24,28},{28,20},{20,12},{12,4},{4,0},{2,6},{1... | collective-permute-start | bytes 1105928 | tf_op jit(solution)/shard_map/ppermute | solution.py:261
  165.3 23.4 %collective-permute-start.53 = (bf16[240,1920]{1,0:T(8,128)(2,1)S(1)}, bf16[240,1920]{1,0:T(8,128)(2,1)S(1)}, u32[]{:S(2)}, u32[]{:S(2)}) collective-permute-start(bf16[240,1920]{1,0:T(8,128)(2,1)S(1)} %shard_map.219), channel_id=1, source_target_pairs={{0,1},{1,0},{2,3},{3,2},{4,5},{5,4},{6,7},{7,6},{8,9},{9,8},{10,11... | collective-permute-start | bytes 2764808 | tf_op jit(solution)/shard_map/ppermute | solution.py:265
  169.4 10.9 %collective-permute-start.46 = (bf16[176,1920]{1,0:T(8,128)(2,1)S(1)}, bf16[176,1920]{1,0:T(8,128)(2,1)S(1)}, u32[]{:S(2)}, u32[]{:S(2)}) collective-permute-start(bf16[176,1920]{1,0:T(8,128)(2,1)S(1)} %shard_map.216), channel_id=1, source_target_pairs={{0,8},{8,16},{16,24},{24,28},{28,20},{20,12},{12,4},{4,0},{2,6},{1... | collective-permute-start | bytes 2027528 | tf_op jit(solution)/shard_map/ppermute | solution.py:261
  169.5 2.7 %collective-permute-start.39 = (bf16[160,1920]{1,0:T(8,128)(2,1)S(1)}, bf16[160,1920]{1,0:T(8,128)(2,1)S(1)}, u32[]{:S(2)}, u32[]{:S(2)}) collective-permute-start(bf16[160,1920]{1,0:T(8,128)(2,1)S(1)} %copy-done.46), channel_id=1, source_target_pairs={{0,2},{2,0},{4,6},{6,4},{8,10},{10,8},{12,14},{14,12},{16,18},{18,... | collective-permute-start | bytes 1843208 | tf_op jit(solution)/shard_map/ppermute | solution.py:257
  170.5 18.2 %collective-permute-start.60 = (bf16[160,1920]{1,0:T(8,128)(2,1)S(1)}, bf16[160,1920]{1,0:T(8,128)(2,1)S(1)}, u32[]{:S(2)}, u32[]{:S(2)}) collective-permute-start(bf16[160,1920]{1,0:T(8,128)(2,1)S(1)} %copy-done.45), channel_id=1, source_target_pairs={{0,2},{2,0},{4,6},{6,4},{8,10},{10,8},{12,14},{14,12},{16,18},{18,... | collective-permute-start | bytes 1843208 | tf_op jit(solution)/shard_map/ppermute | solution.py:257
  171.0 17.7 %collective-permute-start.51 = (bf16[160,1920]{1,0:T(8,128)(2,1)S(1)}, bf16[160,1920]{1,0:T(8,128)(2,1)S(1)}, u32[]{:S(2)}, u32[]{:S(2)}) collective-permute-start(bf16[160,1920]{1,0:T(8,128)(2,1)S(1)} %shard_map.218), channel_id=1, source_target_pairs={{0,8},{8,16},{16,24},{24,28},{28,20},{20,12},{12,4},{4,0},{2,6},{1... | collective-permute-start | bytes 1843208 | tf_op jit(solution)/shard_map/ppermute | solution.py:261
  180.5 13.6 %collective-permute-start.47 = (bf16[176,1920]{1,0:T(8,128)(2,1)S(1)}, bf16[176,1920]{1,0:T(8,128)(2,1)S(1)}, u32[]{:S(2)}, u32[]{:S(2)}) collective-permute-start(bf16[176,1920]{1,0:T(8,128)(2,1)S(1)} %shard_map.217), channel_id=1, source_target_pairs={{0,8},{8,16},{16,24},{24,28},{28,20},{20,12},{12,4},{4,0},{2,6},{1... | collective-permute-start | bytes 2027528 | tf_op jit(solution)/shard_map/ppermute | solution.py:261
  180.6 21.3 %collective-permute-start.36 = (bf16[256,1280]{1,0:T(8,128)(2,1)}, bf16[256,1280]{1,0:T(8,128)(2,1)}, u32[]{:S(2)}, u32[]{:S(2)}) collective-permute-start(bf16[256,1280]{1,0:T(8,128)(2,1)} %get-tuple-element.181), channel_id=1, source_target_pairs={{0,1},{1,0},{2,3},{3,2},{4,5},{5,4},{6,7},{7,6},{8,9},{9,8},{10,11... | collective-permute-start | bytes 1966088 | tf_op jit(solution)/shard_map/ppermute | solution.py:265
  188.7 5.5 %collective-permute-start.48 = (bf16[160,1920]{1,0:T(8,128)(2,1)}, bf16[160,1920]{1,0:T(8,128)(2,1)S(1)}, u32[]{:S(2)}, u32[]{:S(2)}) collective-permute-start(bf16[160,1920]{1,0:T(8,128)(2,1)} %get-tuple-element.212), channel_id=1, source_target_pairs={{0,2},{2,0},{4,6},{6,4},{8,10},{10,8},{12,14},{14,12},{16,18},{18,... | collective-permute-start | bytes 1843208 | tf_op jit(solution)/shard_map/ppermute | solution.py:257
  189.9 10.9 %collective-permute-start.61 = (bf16[160,1920]{1,0:T(8,128)(2,1)}, bf16[160,1920]{1,0:T(8,128)(2,1)}, u32[]{:S(2)}, u32[]{:S(2)}) collective-permute-start(bf16[160,1920]{1,0:T(8,128)(2,1)} %shard_map.221), channel_id=1, source_target_pairs={{0,8},{8,16},{16,24},{24,28},{28,20},{20,12},{12,4},{4,0},{2,6},{1... | collective-permute-start | bytes 1843208 | tf_op jit(solution)/shard_map/ppermute | solution.py:261
  189.9 19.0 %collective-permute-start.59 = (bf16[80,1920]{1,0:T(8,128)(2,1)}, bf16[80,1920]{1,0:T(8,128)(2,1)S(1)}, u32[]{:S(2)}, u32[]{:S(2)}) collective-permute-start(bf16[80,1920]{1,0:T(8,128)(2,1)} %get-tuple-element.221), channel_id=1, source_target_pairs={{0,2},{2,0},{4,6},{6,4},{8,10},{10,8},{12,14},{14,12},{16,18},{18,... | collective-permute-start | bytes 921608 | tf_op jit(solution)/shard_map/ppermute | solution.py:257
  194.1 21.1 %collective-permute-start.57 = (bf16[80,1920]{1,0:T(8,128)(2,1)}, bf16[80,1920]{1,0:T(8,128)(2,1)S(1)}, u32[]{:S(2)}, u32[]{:S(2)}) collective-permute-start(bf16[80,1920]{1,0:T(8,128)(2,1)} %get-tuple-element.219), channel_id=1, source_target_pairs={{0,2},{2,0},{4,6},{6,4},{8,10},{10,8},{12,14},{14,12},{16,18},{18,... | collective-permute-start | bytes 921608 | tf_op jit(solution)/shard_map/ppermute | solution.py:257
  194.4 13.6 %collective-permute-start.54 = (bf16[176,1920]{1,0:T(8,128)(2,1)S(1)}, bf16[176,1920]{1,0:T(8,128)(2,1)S(1)}, u32[]{:S(2)}, u32[]{:S(2)}) collective-permute-start(bf16[176,1920]{1,0:T(8,128)(2,1)S(1)} %shard_map.220), channel_id=1, source_target_pairs={{0,8},{8,16},{16,24},{24,28},{28,20},{20,12},{12,4},{4,0},{2,6},{1... | collective-permute-start | bytes 2027528 | tf_op jit(solution)/shard_map/ppermute | solution.py:261
  201.8 7.1 %collective-permute-start.62 = (bf16[80,1920]{1,0:T(8,128)(2,1)S(1)}, bf16[80,1920]{1,0:T(8,128)(2,1)S(1)}, u32[]{:S(2)}, u32[]{:S(2)}) collective-permute-start(bf16[80,1920]{1,0:T(8,128)(2,1)S(1)} %slice.87), channel_id=1, source_target_pairs={{0,2},{2,0},{4,6},{6,4},{8,10},{10,8},{12,14},{14,12},{16,18},{18,... | collective-permute-start | bytes 921608 | tf_op jit(solution)/shard_map/ppermute | solution.py:257
  208.8 1.4 collective-permute-start.55
  210.3 3.8 %collective-permute-start.56 = (f32[2,1920]{1,0:T(2,128)S(1)}, f32[2,1920]{1,0:T(2,128)S(1)}, u32[]{:S(2)}, u32[]{:S(2)}) collective-permute-start(f32[2,1920]{1,0:T(2,128)S(1)} %add_add_fusion), channel_id=1, source_target_pairs={{0,1},{1,0},{2,3},{3,2},{4,5},{5,4},{6,7},{7,6},{8,9},{9,8},{10,11... | collective-permute-start | bytes 46088 | tf_op jit(solution)/shard_map/ppermute | solution.py:265
  212.1 3.1 %collective-permute-start.58 = (bf16[80,1920]{1,0:T(8,128)(2,1)S(1)}, bf16[80,1920]{1,0:T(8,128)(2,1)S(1)}, u32[]{:S(2)}, u32[]{:S(2)}) collective-permute-start(bf16[80,1920]{1,0:T(8,128)(2,1)S(1)} %slice.105), channel_id=1, source_target_pairs={{0,2},{2,0},{4,6},{6,4},{8,10},{10,8},{12,14},{14,12},{16,18},{18,... | collective-permute-start | bytes 921608 | tf_op jit(solution)/shard_map/ppermute | solution.py:257
  (50 other events, 457.0 us)
